TPU v7x, 32 devices: a whole 2x2x4 slice. The times are simulated.
32 devices in a mesh: dp: 16 (over z, y, core), cp: 2 (over x).
Axes of the slice: x: 2, y: 2, z: 4, core: 2. Of those that a mesh axis runs over, the one named last changes fastest.
Arguments:
- tokens: bfloat16 [8192, 960], P(('dp', 'cp')), may hold values from -6 to 6
- out_grad: bfloat16 [8192, 960], P(('dp', 'cp')), may hold values from -6 to 6
- lengths: int32 [16, 3], P('dp'), may hold values from 1 to 256, 512 in all within a row
- slot_positions: int32 [16, 512], P('dp'), may hold values from 0 to 511, as said below
- params: float32 [9830400], P('cp'), as said below
- first_moment: float32 [9830400], P('cp'), as said below
- second_moment: float32 [9830400], P('cp'), as said below
- norm_gains: float32 [2, 960], P(None, 'cp'), may hold values from 0.5 to 1.5
- gain_first: float32 [2, 960], P(None, 'cp'), as said below
- gain_second: float32 [2, 960], P(None, 'cp'), as said below
Outputs:
- block_out: float32 [8192, 960], P(('dp', 'cp'))
- input_grad: float32 [8192, 960], P(('dp', 'cp'))
- param_grad: float32 [9830400], P('cp')
- new_first: float32 [9830400], P('cp')
- new_second: float32 [9830400], P('cp')
- new_params: float32 [9830400], P('cp')
- gain_grad: float32 [2, 960], P(None, 'cp')
- new_gain_first: float32 [2, 960], P(None, 'cp')
- new_gain_second: float32 [2, 960], P(None, 'cp')
- new_gains: float32 [2, 960], P(None, 'cp')
Inputs may be any that keep to these rules, and one draw needn't show every extreme that they name: Each row holds the lengths of the 3 sequences of one window in the order in which they are packed; they add up to 512, and the largest is exactly 256. `slot_positions`: in each row, for every j below 256, the 2 entries c * 256 + j, for c below 2, hold the window positions j * 2 to j * 2 + 1 in some order; so each row is a permutation of the window's positions. `params`: owner blocks of the seven matrices, laid out as the steps say. `first_moment`: laid out as params. `second_moment`: laid out as params; every entry is positive. `gain_first`: one row for each norm. `gain_second`: one row for each norm; every entry is positive.
All inputs are finite; a program needn't handle non-finite values.
Results may differ from a plain program's by a relative error of at most 0.02.
Values may be sent and summed in bfloat16 or wider, within the bound.
A program may use at most 448 MiB of HBM per device.

v0:
```python
import jax
import jax.numpy as jnp
from jax import lax
from jax.sharding import PartitionSpec as P

D = 960
H = 15
KVH = 5
HD = 64
FF = 2560
STEP = 10
QD = 960
KD = 320


eps_norm = 1e-05
beta_one = 0.9
beta_two = 0.95
adam_eps = 1e-08
decay_coef = 0.1
rope_base = 10000.0
gain_rate = 1.0
masked_score = -1e30


def matrix_shapes():
    return [(D, QD), (D, KD), (D, KD), (QD, D), (D, FF), (D, FF), (FF, D)]


def matrix_rates(longest):
    plain_rate = 3.0 * D ** (-0.5)
    out_rate = 3.0 * (longest / (6.0 * QD)) ** 0.5
    return [
        plain_rate,
        plain_rate,
        plain_rate,
        out_rate,
        plain_rate,
        plain_rate,
        3.0 * FF ** (-0.5),
    ]


def owner_rates(shard_count, longest):
    pieces = []
    for shape_pair, rate_value in zip(matrix_shapes(), matrix_rates(longest)):
        pieces.append(
            jnp.full((shape_pair[0] // shard_count * shape_pair[1],), rate_value, jnp.float32)
        )
    return jnp.concatenate(pieces)


def split_owned(flat, shard_count):
    pieces = []
    offset = 0
    for row_count, col_count in matrix_shapes():
        seg_size = row_count // shard_count * col_count
        pieces.append(flat[offset : offset + seg_size].reshape(row_count // shard_count, col_count))
        offset += seg_size
    return pieces


def rms_norm(values, gain_row):
    return (
        values * lax.rsqrt(jnp.mean(values * values, axis=-1, keepdims=True) + eps_norm) * gain_row
    )


def swiglu(gate_act, up_act):
    return jax.nn.silu(gate_act) * up_act


def window_layout(seq_lengths, slot_pos):
    seq_ends = jnp.cumsum(seq_lengths)
    seq_starts = seq_ends - seq_lengths
    segment = jnp.sum((slot_pos[:, None] >= seq_ends[None, :]).astype(jnp.int32), axis=1)
    chosen = segment[:, None] == jnp.arange(seq_lengths.shape[0], dtype=jnp.int32)[None, :]
    position = slot_pos - jnp.sum(jnp.where(chosen, seq_starts[None, :], 0), axis=1)
    return (segment, position)


def rope_tables(position):
    half_dim = HD // 2
    inv_freq = rope_base ** (-(jnp.arange(half_dim, dtype=jnp.float32) * 2.0 / HD))
    angles = position.astype(jnp.float32)[:, None] * inv_freq[None, :]
    return (jnp.cos(angles), jnp.sin(angles))


def rotate(values, cosine, sine_vals, direction):
    half_dim = HD // 2
    first_half = values[..., :half_dim]
    second_half = values[..., half_dim:]
    cos_wide = cosine[:, None, :]
    sin_wide = direction * sine_vals[:, None, :]
    return jnp.concatenate(
        [
            first_half * cos_wide - second_half * sin_wide,
            second_half * cos_wide + first_half * sin_wide,
        ],
        axis=-1,
    )


def group_forward(group_args, allowed, score_scale):
    query_grp, key_grp, value_grp = group_args
    raw_scores = jnp.einsum("qhd,kd->hqk", query_grp, key_grp, preferred_element_type=jnp.float32)
    scores = jnp.where(allowed[None], raw_scores * score_scale, masked_score)
    row_max = jnp.max(scores, axis=-1, keepdims=True)
    exp_scores = jnp.exp(scores - row_max)
    row_total = jnp.sum(exp_scores, axis=-1, keepdims=True)
    probs_low = (exp_scores / row_total).astype(jnp.bfloat16)
    output = jnp.einsum("hqk,kd->qhd", probs_low, value_grp, preferred_element_type=jnp.float32)
    return (output, row_max + jnp.log(row_total))


def group_backward(group_args, allowed, score_scale):
    query_grp, key_grp, value_grp, grad_grp, log_sums = group_args
    raw_scores = jnp.einsum("qhd,kd->hqk", query_grp, key_grp, preferred_element_type=jnp.float32)
    scores = jnp.where(allowed[None], raw_scores * score_scale, masked_score)
    probs = jnp.exp(scores - log_sums)
    probs_low = probs.astype(jnp.bfloat16)
    grad_probs = jnp.einsum("qhd,kd->hqk", grad_grp, value_grp, preferred_element_type=jnp.float32)
    row_dot = jnp.sum(probs * grad_probs, axis=-1, keepdims=True)
    grad_scores = (probs * (grad_probs - row_dot)).astype(jnp.bfloat16)
    grad_query = (
        jnp.einsum("hqk,kd->qhd", grad_scores, key_grp, preferred_element_type=jnp.float32)
        * score_scale
    )
    grad_key = (
        jnp.einsum("hqk,qhd->kd", grad_scores, query_grp, preferred_element_type=jnp.float32)
        * score_scale
    )
    grad_value = jnp.einsum("hqk,qhd->kd", probs_low, grad_grp, preferred_element_type=jnp.float32)
    return (grad_query, grad_key, grad_value)


def adamw_step(weight, gradient, first_old, second_old, step_rates, decay_value):
    first_new = beta_one * first_old + (1.0 - beta_one) * gradient
    second_new = beta_two * second_old + (1.0 - beta_two) * gradient * gradient
    first_hat = first_new / (1.0 - beta_one**STEP)
    second_hat = second_new / (1.0 - beta_two**STEP)
    updated = weight - step_rates * (
        first_hat / (jnp.sqrt(second_hat) + adam_eps) + decay_value * weight
    )
    return (first_new, second_new, updated)


def body(
    tokens,
    out_grad,
    lengths,
    slot_positions,
    params,
    first_moment,
    second_moment,
    norm_gains,
    gain_first,
    gain_second,
):
    low_type = jnp.bfloat16
    shard_count = lax.axis_size("cp")
    local_rows = tokens.shape[0]
    window_rows = local_rows * shard_count
    longest = window_rows // 2
    group_size = H // KVH
    score_scale = HD ** (-0.5)
    my_shard = lax.axis_index("cp")
    shard_query, shard_key, shard_value, shard_out, shard_gate, shard_up, shard_down = split_owned(
        params, shard_count
    )
    w_query, w_key, w_value, w_out, w_gate, w_up, w_down, gain_pair = (
        lax.all_gather(shard_query.astype(low_type), "cp", axis=0, tiled=True),
        lax.all_gather(shard_key.astype(low_type), "cp", axis=0, tiled=True),
        lax.all_gather(shard_value.astype(low_type), "cp", axis=0, tiled=True),
        lax.all_gather(shard_out.astype(low_type), "cp", axis=0, tiled=True),
        lax.all_gather(shard_gate.astype(low_type), "cp", axis=0, tiled=True),
        lax.all_gather(shard_up.astype(low_type), "cp", axis=0, tiled=True),
        lax.all_gather(shard_down.astype(low_type), "cp", axis=0, tiled=True),
        lax.all_gather(norm_gains.astype(low_type), "cp", axis=1, tiled=True),
    )
    segment_all, position_all = window_layout(lengths[0], slot_positions[0])
    segment_mine = lax.dynamic_slice_in_dim(segment_all, my_shard * local_rows, local_rows)
    position_mine = lax.dynamic_slice_in_dim(position_all, my_shard * local_rows, local_rows)
    allowed = (segment_mine[:, None] == segment_all[None, :]) & (
        position_all[None, :] <= position_mine[:, None]
    )
    cosine, sine_vals = rope_tables(position_mine)
    inputs = tokens.astype(jnp.float32)
    normed_one, pull_one = jax.vjp(rms_norm, inputs, gain_pair[0].astype(jnp.float32))
    xn_one = normed_one.astype(low_type)
    query_pre = jnp.dot(xn_one, w_query, preferred_element_type=jnp.float32)
    key_pre = jnp.dot(xn_one, w_key, preferred_element_type=jnp.float32)
    value_low = jnp.dot(xn_one, w_value, preferred_element_type=jnp.float32).astype(low_type)
    query_rot = rotate(query_pre.reshape(local_rows, H, HD), cosine, sine_vals, 1.0).astype(
        low_type
    )
    key_rot = rotate(key_pre.reshape(local_rows, KVH, HD), cosine, sine_vals, 1.0).astype(low_type)
    keys_all, values_all = (
        lax.all_gather(key_rot, "cp", axis=0, tiled=True),
        lax.all_gather(value_low.reshape(local_rows, KVH, HD), "cp", axis=0, tiled=True),
    )
    key_groups = keys_all.transpose(1, 0, 2)
    value_groups = values_all.transpose(1, 0, 2)
    query_groups = query_rot.reshape(local_rows, KVH, group_size, HD).transpose(1, 0, 2, 3)
    attended, log_sums = lax.map(
        lambda group_args: group_forward(group_args, allowed, score_scale),
        (query_groups, key_groups, value_groups),
    )
    attn_low = attended.transpose(1, 0, 2, 3).reshape(local_rows, QD).astype(low_type)
    resid_one = inputs + jnp.dot(attn_low, w_out, preferred_element_type=jnp.float32)
    normed_two, pull_two = jax.vjp(rms_norm, resid_one, gain_pair[1].astype(jnp.float32))
    xn_two = normed_two.astype(low_type)
    gate_act = jnp.dot(xn_two, w_gate, preferred_element_type=jnp.float32)
    up_act = jnp.dot(xn_two, w_up, preferred_element_type=jnp.float32)
    hidden_act, pull_act = jax.vjp(swiglu, gate_act, up_act)
    hidden_low = hidden_act.astype(low_type)
    block_out = resid_one + jnp.dot(hidden_low, w_down, preferred_element_type=jnp.float32)
    grad_hidden = jnp.dot(out_grad, w_down.T, preferred_element_type=jnp.float32)
    grad_down = jnp.dot(hidden_low.T, out_grad, preferred_element_type=jnp.float32)
    grad_gate_act, grad_up_act = pull_act(grad_hidden)
    gate_back = grad_gate_act.astype(low_type)
    up_back = grad_up_act.astype(low_type)
    grad_gate = jnp.dot(xn_two.T, gate_back, preferred_element_type=jnp.float32)
    grad_up = jnp.dot(xn_two.T, up_back, preferred_element_type=jnp.float32)
    grad_xn_two = jnp.dot(gate_back, w_gate.T, preferred_element_type=jnp.float32) + jnp.dot(
        up_back, w_up.T, preferred_element_type=jnp.float32
    )
    back_two, gain_grad_two = pull_two(grad_xn_two)
    grad_resid = out_grad.astype(jnp.float32) + back_two
    resid_low = grad_resid.astype(low_type)
    grad_out = jnp.dot(attn_low.T, resid_low, preferred_element_type=jnp.float32)
    grad_attn = jnp.dot(resid_low, w_out.T, preferred_element_type=jnp.float32).astype(low_type)
    grad_groups = grad_attn.reshape(local_rows, KVH, group_size, HD).transpose(1, 0, 2, 3)
    grad_q, grad_k_part, grad_v_part = lax.map(
        lambda group_args: group_backward(group_args, allowed, score_scale),
        (query_groups, key_groups, value_groups, grad_groups, log_sums),
    )
    key_terms = grad_k_part.transpose(1, 0, 2).reshape(window_rows, KD)
    value_terms = grad_v_part.transpose(1, 0, 2).reshape(window_rows, KD)
    key_mine, value_mine = (
        lax.psum_scatter(
            key_terms.astype(jnp.bfloat16), "cp", scatter_dimension=0, tiled=True
        ).astype(jnp.float32),
        lax.psum_scatter(
            value_terms.astype(jnp.bfloat16), "cp", scatter_dimension=0, tiled=True
        ).astype(jnp.float32),
    )
    query_back = rotate(
        grad_q.transpose(1, 0, 2, 3).reshape(local_rows, H, HD), cosine, sine_vals, -1.0
    )
    query_back = query_back.reshape(local_rows, QD).astype(low_type)
    key_back = rotate(key_mine.reshape(local_rows, KVH, HD), cosine, sine_vals, -1.0)
    key_back = key_back.reshape(local_rows, KD).astype(low_type)
    value_back = value_mine.astype(low_type)
    grad_query = jnp.dot(xn_one.T, query_back, preferred_element_type=jnp.float32)
    grad_key = jnp.dot(xn_one.T, key_back, preferred_element_type=jnp.float32)
    grad_value = jnp.dot(xn_one.T, value_back, preferred_element_type=jnp.float32)
    grad_xn_one = (
        jnp.dot(query_back, w_query.T, preferred_element_type=jnp.float32)
        + jnp.dot(key_back, w_key.T, preferred_element_type=jnp.float32)
        + jnp.dot(value_back, w_value.T, preferred_element_type=jnp.float32)
    )
    back_one, gain_grad_one = pull_one(grad_xn_one)
    input_grad = grad_resid + back_one
    gain_local = jnp.stack([gain_grad_one, gain_grad_two])
    grad_owner = jnp.concatenate(
        [
            piece.reshape(shard_count, -1)
            for piece in (grad_query, grad_key, grad_value, grad_out, grad_gate, grad_up, grad_down)
        ],
        axis=1,
    )
    replica_count = lax.axis_size("dp")
    owned_part, gain_part = (
        lax.psum_scatter(
            grad_owner.astype(jnp.bfloat16), "cp", scatter_dimension=0, tiled=True
        ).astype(jnp.float32),
        lax.psum_scatter(
            gain_local.astype(jnp.bfloat16), "cp", scatter_dimension=1, tiled=True
        ).astype(jnp.float32),
    )
    replica_rows = owned_part.reshape(replica_count, -1)
    replica_piece = lax.psum_scatter(replica_rows, "dp", scatter_dimension=0, tiled=True)
    owned_grad = (
        lax.all_gather(replica_piece.astype(jnp.bfloat16), "dp", axis=0, tiled=True)
        .astype(replica_piece.dtype)
        .reshape(-1)
    )
    gain_owned = lax.psum(gain_part, "dp")
    step_rates = owner_rates(shard_count, longest)
    new_first, new_second, new_params = adamw_step(
        params, owned_grad, first_moment, second_moment, step_rates, decay_coef
    )
    new_gain_first, new_gain_second, new_gains = adamw_step(
        norm_gains, gain_owned, gain_first, gain_second, gain_rate, 0.0
    )
    return (
        block_out,
        input_grad,
        owned_grad,
        new_first,
        new_second,
        new_params,
        gain_owned,
        new_gain_first,
        new_gain_second,
        new_gains,
    )


def solution(mesh):
    return jax.shard_map(
        body,
        mesh=mesh,
        in_specs=(
            P(("dp", "cp"), None),
            P(("dp", "cp"), None),
            P("dp", None),
            P("dp", None),
            P("cp"),
            P("cp"),
            P("cp"),
            P(None, "cp"),
            P(None, "cp"),
            P(None, "cp"),
        ),
        out_specs=(
            P(("dp", "cp"), None),
            P(("dp", "cp"), None),
            P("cp"),
            P("cp"),
            P("cp"),
            P("cp"),
            P(None, "cp"),
            P(None, "cp"),
            P(None, "cp"),
            P(None, "cp"),
        ),
        check_vma=False,
    )
```

profile of v0, /device:TPU:0, one launch (start us, length us, event | category | flops | bytes accessed | tf_op | source)
XLA Modules:
  0.0 1741.3 jit_solution(17808782581536771020)
XLA Ops:
  7.2 7.4 convert.76
  27.1 5.9 convert_element_type.145
  45.3 16.5 all-gather.1
  68.3 9.5 all_gather.35
  78.3 16.3 all-gather.2
  97.8 7.5 all_gather.37
  108.2 7.1 while.30
  119.2 52.3 %all-gather.15.cloned.1.call-done = bf16[960,2560]{1,0:T(8,128)(2,1)} async-done(((bf16[480,2560]{1,0:T(8,128)(2,1)}), bf16[960,2560]{1,0:T(8,128)(2,1)}) %all-gather.15.cloned.1.call-update) | async-done | bytes 4915216 | tf_op jit(solution)/shard_map/all_gather | solution.py:176
  177.0 60.9 %all-gather.17.cloned.1.call-done = bf16[960,2560]{1,0:T(8,128)(2,1)} async-done(((bf16[480,2560]{1,0:T(8,128)(2,1)}), bf16[960,2560]{1,0:T(8,128)(2,1)}) %all-gather.17.cloned.1.call-update) | async-done | bytes 4915216 | tf_op jit(solution)/shard_map/all_gather | solution.py:177
  243.3 65.1 %all-gather.19.cloned.1.call-done = bf16[2560,960]{1,0:T(8,128)(2,1)} async-done(((bf16[1280,960]{1,0:T(8,128)(2,1)}), bf16[2560,960]{1,0:T(8,128)(2,1)}) %all-gather.19.cloned.1.call-update) | async-done | bytes 4915216 | tf_op jit(solution)/shard_map/all_gather | solution.py:178
  308.4 7.8 multiply_convert_fusion
  329.3 35.2 %while.31 = (s32[]{:T(128)}, f32[5,256,3,64]{1,3,2,0:T(8,128)}, bf16[5,512,64]{1,2,0:T(8,128)(2,1)}, bf16[5,512,64]{1,2,0:T(8,128)(2,1)}, bf16[5,512,64]{1,2,0:T...) while((s32[]{:T(128)}, f32[5,256,3,64]{1,3,2,0:T(8,128)}, ...), condition=%wide.region_12.13_spmd.clone.clone, body=%wide.region_10.12_spmd.clone.sunk.clone | while | flops 255671552 | bytes 13134985 | solution.py:234
  388.2 8.1 reshape.336
  401.4 8.2 reshape.337
  414.5 7.8 copy.65
  422.4 10.7 reshape.390
  466.8 6.9 constant_dynamic-update-slice_fusion.2
  489.2 433.5 %all-reduce.6.cloned.1.call-done = bf16[2,4915200]{1,0:T(2,128)(2,1)} async-done(((bf16[2,4915200]{1,0:T(2,128)(2,1)}), bf16[2,4915200]{1,0:T(2,128)(2,1)}) %all-reduce.6.cloned.1.call-update) | async-done | bytes 19660816
  922.7 193.1 %fusion.47 = f32[4915200]{0:T(1024)} fusion(bf16[2,4915200]{1,0:T(2,128)(2,1)} %all-reduce.6.cloned.1.call-done, u32[]{:T(128)} %bitcast.68), kind=kLoop, calls=%fused_computation.61 | loop fusion | flops 4915200 | bytes 29491204 | tf_op jit(solution)/shard_map/reshape | solution.py:282
  1115.8 18.8 %reshape.350 = f32[16,307200]{1,0:T(8,128)} reshape(f32[4915200]{0:T(1024)} %fusion.47) | data formatting | bytes 39321600 | tf_op jit(solution)/shard_map/reshape | solution.py:282
  1134.6 411.4 %all-reduce.7 = (bf16[16,307200]{1,0:T(8,128)(2,1)}, f32[2,480]{1,0:T(2,128)S(1)}) all-reduce(f32[16,307200]{1,0:T(8,128)} %reshape.350, bf16[2,480]{1,0:T(2,128)(2,1)S(1)} %copy.71), channel_id=5, replica_groups=mesh['dp'=16,'cp'=2] {'dp'}, use_global_device_ids=true, to_apply=%region_17.18.clone | all-reduce | flops 4916160 | bytes 29496960
  1565.9 92.6 %all-gather.21.cloned.1.call-done = bf16[16,1,307200]{2,1,0:T(2,128)(2,1)} async-done(((bf16[1,1,307200]{2,1,0:T(2,128)(2,1)}), bf16[16,1,307200]{2,1,0:T(2,128)(2,1)}) %all-gather.21.cloned.1.call-update) | async-done | bytes 9830416 | tf_op jit(solution)/shard_map/all_gather | solution.py:285
  1658.5 23.6 %reshape.361 = f32[16,1,307200]{2,1,0:T(1,128)} convert(bf16[16,1,307200]{2,1,0:T(2,128)(2,1)} %all-gather.21.cloned.1.call-done) | non-fusion elementwise | flops 4915200 | bytes 29491200 | tf_op jit(solution)/shard_map/reshape | solution.py:287
  1682.1 52.1 %multiply_subtract_fusion = (f32[4915200]{0:T(1024)}, f32[4915200]{0:T(1024)}, f32[4915200]{0:T(1024)}) fusion(f32[4915200]{0:T(1024)} %param.18, f32[4915200]{0:T(1024)} %broadcast_dynamic-update-slice_fusion.1, f32[4915200]{0:T(1024)} %bitcast.247, f32[4915200]{0:T(1024)} %param.20, f32[4915200]{0:T(1024)} %param.19), kind=kLoop, calls=%fused_computation.62 | loop fusion | flops 73728000 | bytes 157286400 | tf_op jit(solution)/shard_map/sub | solution.py:142
  (270 shorter events, 209.3 us)
Async XLA Ops:
  7.2 98.2 %all-gather.11.cloned.1.call-start = ((), (), s32[]{:S(2)}) async-start(), calls=%async_computation.3 | async-start | bytes 2949120 | tf_op jit(solution)/shard_map/all_gather | solution.py:172
  20.4 94.9 %all-gather.13.cloned.1.call-start = ((), (), s32[]{:S(2)}) async-start(), calls=%async_computation.4 | async-start | bytes 2949120 | tf_op jit(solution)/shard_map/all_gather | solution.py:175
  22.2 149.3 %all-gather.15.cloned.1.call-start = ((), (), s32[]{:S(2)}) async-start(), calls=%async_computation.5 | async-start | bytes 7372800 | tf_op jit(solution)/shard_map/all_gather | solution.py:176
  33.0 204.8 %all-gather.17.cloned.1.call-start = ((), (), s32[]{:S(2)}) async-start(), calls=%async_computation.6 | async-start | bytes 7372800 | tf_op jit(solution)/shard_map/all_gather | solution.py:177
  38.9 269.5 %all-gather.19.cloned.1.call-start = ((), (), s32[]{:S(2)}) async-start(), calls=%async_computation.7 | async-start | bytes 7864320 | tf_op jit(solution)/shard_map/all_gather | solution.py:178
  42.2 20.8 %copy-start.21 = (f32[2,480]{1,0:T(2,128)S(1)}, f32[2,480]{1,0:T(2,128)}, u32[]{:S(2)}) copy-start(f32[2,480]{1,0:T(2,128)} %param.21) | copy-start | bytes 11524
  42.2 25.4 %copy-start.1 = (bf16[256,960]{0,1:T(8,128)(2,1)S(1)}, bf16[256,960]{0,1:T(8,128)(2,1)}, u32[]{:S(2)}) copy-start(bf16[256,960]{0,1:T(8,128)(2,1)} %param.14) | copy-start | bytes 1474564
  42.3 400.0 %reduce-scatter.6.cloned.1.call-start = ((), (), s32[]{:S(2)}) async-start(), calls=%async_computation.8 | async-start | bytes 491520 | tf_op jit(solution)/shard_map/reduce_scatter | solution.py:241
  45.2 32.5 %copy-start.17 = (bf16[153600]{0:T(1024)(128)(2,1)S(1)}, bf16[153600]{0:T(1024)(128)(2,1)}, u32[]{:S(2)}) copy-start(bf16[153600]{0:T(1024)(128)(2,1)} %get-tuple-element.234) | copy-start | bytes 921604
  63.0 34.8 %copy-start.8 = (bf16[960,320]{0,1:T(8,128)(2,1)}, bf16[960,320]{0,1:T(8,128)(2,1)S(1)}, u32[]{:S(2)}) copy-start(bf16[960,320]{0,1:T(8,128)(2,1)S(1)} %reshape.356) | copy-start | bytes 1843204
  63.0 33.3 %copy-start.29 = (s32[1,3]{1,0:T(1,128)S(1)}, s32[1,3]{1,0:T(1,128)}, u32[]{:S(2)}) copy-start(s32[1,3]{1,0:T(1,128)} %param.16) | copy-start | bytes 40
  63.0 33.5 %copy-start.18 = (s32[1,512]{1,0:T(1,128)S(1)}, s32[1,512]{1,0:T(1,128)}, u32[]{:S(2)}) copy-start(s32[1,512]{1,0:T(1,128)} %param.17) | copy-start | bytes 6148
  67.8 29.1 %copy-start.23 = (f32[256]{0:T(256)}, f32[256]{0:T(256)S(1)}, u32[]{:S(2)}) copy-start(f32[256]{0:T(256)S(1)} %fusion.59) | copy-start | bytes 3076
  67.8 29.1 %copy-start.19 = (f32[256]{0:T(256)}, f32[256]{0:T(256)S(1)}, u32[]{:S(2)}) copy-start(f32[256]{0:T(256)S(1)} %fusion.64) | copy-start | bytes 3076
  95.9 12.2 copy-start.9
  119.0 207.3 %copy-start.2 = (f32[256,960]{0,1:T(8,128)}, f32[256,960]{0,1:T(8,128)S(1)}, u32[]{:S(2)}) copy-start(f32[256,960]{0,1:T(8,128)S(1)} %get-tuple-element.253) | copy-start | bytes 2949124
  177.0 131.4 %copy-start.5 = (bf16[256,960]{0,1:T(8,128)(2,1)S(1)}, bf16[256,960]{0,1:T(8,128)(2,1)}, u32[]{:S(2)}) copy-start(bf16[256,960]{0,1:T(8,128)(2,1)} %param.15) | copy-start | bytes 1474564
  329.3 36.7 %copy-start.20 = (f32[256]{0:T(256)S(1)}, f32[256]{0:T(256)}, u32[]{:S(2)}) copy-start(f32[256]{0:T(256)} %copy-done.19) | copy-start | bytes 3076
  364.5 87.0 %reduce-scatter.8.cloned.1.call-start = ((), (), s32[]{:S(2)}) async-start(), calls=%async_computation.9 | async-start | bytes 491520 | tf_op jit(solution)/shard_map/reduce_scatter | solution.py:244
  439.0 49.1 %reduce-scatter.10.cloned.1.call-start = ((), (), s32[]{:S(2)}) async-start(), calls=%async_computation.11 | async-start | bytes 368640
  458.1 464.6 %all-reduce.6.cloned.1.call-start = ((), (), s32[]{:S(2)}) async-start(), calls=%async_computation.12 | async-start | bytes 39321600
  462.4 11.3 slice-start
  482.5 1176.0 %all-gather.21.cloned.1.call-start = ((), (), s32[]{:S(2)}) async-start(), calls=%async_computation.10 | async-start | bytes 20889600 | tf_op jit(solution)/shard_map/all_gather | solution.py:285
  1545.9 19.4 %copy-start.27 = (f32[2,480]{1,0:T(2,128)}, f32[2,480]{1,0:T(2,128)S(1)}, u32[]{:S(2)}) copy-start(f32[2,480]{1,0:T(2,128)S(1)} %get-tuple-element.216) | copy-start | bytes 11524
  (24 other events, 115.1 us)
Sparse Core Ops, SparseCore 0:
  20.6 39.2 all-gather.10
  62.0 42.5 all-gather.12
  106.7 64.7 all-gather.14
  172.9 64.8 all-gather.16
  239.8 68.5 all-gather.18
  364.7 12.3 reduce-scatter.5
  439.1 12.3 reduce-scatter.7
  458.2 11.4 reduce-scatter.9
  482.6 440.0 all-reduce.5
  1551.5 106.9 all-gather.20
where the time goes:
time: 1750 us; the launch traced here: 1740 us
  waiting for transfers between devices  706 us (40%)
  blocking collectives  466 us (27%)
  other arithmetic  288 us (16%)
  local copies, waits for them, and re-layouts  163 us (9%)
  matrix products  103 us (6%)
    unnamed x12, waiting for transfers between devices  434 us
    unnamed x1, blocking collectives  411 us
    reshape x1, other arithmetic, body(): replica_rows = owned_part.reshape(replica_count, -1)  193 us
    all_gather x1, waiting for transfers between devices, body(): lax.all_gather(replica_piece.astype(jnp.bfloat16), 'dp', axis=0, tiled=True)  92.6 us
    unnamed x101, local copies, waits for them, and re-layouts  69.1 us
    all_gather x1, waiting for transfers between devices, body(): lax.all_gather(shard_down.astype(low_type), 'cp', axis=0, tiled=True)  65.1 us
    all_gather x1, waiting for transfers between devices, body(): lax.all_gather(shard_up.astype(low_type), 'cp', axis=0, tiled=True)  60.9 us
    sub x2, other arithmetic, adamw_step(): weight - step_rates * (first_hat / (jnp.sqrt(second_hat) + adam_eps) + de...  52.8 us
  transfers between devices with their start and end apart: 10, of which 6 were waited for; matrix products, arithmetic and copies ran while one was open for 11% of the time, Pallas kernels for 0%

commit v1 on v0

--- a/solution.py
+++ b/solution.py
@@ -143,6 +143,60 @@
         first_hat / (jnp.sqrt(second_hat) + adam_eps) + decay_value * weight
     )
     return (first_new, second_new, updated)
+
+
+def swap_shards(values):
+    return lax.ppermute(values, "cp", [(0, 1), (1, 0)])
+
+
+def swap_replicas(values, distance):
+    return lax.ppermute(
+        values, "dp", [(index, index ^ distance) for index in range(lax.axis_size("dp"))]
+    )
+
+
+def in_order(mine, theirs, my_shard, axis):
+    return jnp.where(
+        my_shard == 0,
+        jnp.concatenate([mine, theirs], axis=axis),
+        jnp.concatenate([theirs, mine], axis=axis),
+    )
+
+
+def split_columns(values, my_shard):
+    half = values.shape[1] // 2
+    lower, upper = values[:, :half], values[:, half:]
+    return (jnp.where(my_shard == 0, lower, upper), jnp.where(my_shard == 0, upper, lower))
+
+
+def gather_rows(half):
+    my_shard = lax.axis_index("cp")
+    quarter = lax.axis_index("dp") % 4
+    mine = half.reshape(4, half.shape[0] // 4, half.shape[1])
+    other = (1 - my_shard) * 4
+    fetched = swap_shards(lax.dynamic_index_in_dim(mine, quarter, 0))
+    across = swap_replicas(fetched, 2)
+    whole = jnp.zeros((8,) + mine.shape[1:], half.dtype)
+    whole = lax.dynamic_update_slice_in_dim(whole, mine, my_shard * 4, 0)
+    for piece, place in (
+        (fetched, quarter),
+        (across, quarter ^ 2),
+        (swap_replicas(fetched, 1), quarter ^ 1),
+        (swap_replicas(across, 1), quarter ^ 3),
+    ):
+        whole = lax.dynamic_update_slice_in_dim(whole, piece, other + place, 0)
+    return whole.reshape(-1, half.shape[1])
+
+
+def owned_product(left_mine, left_peer, right_mine, right_peer):
+    left = jnp.concatenate([left_mine, left_peer], axis=0)
+    right = jnp.concatenate([right_mine, right_peer], axis=0)
+    return jnp.dot(left.T, right, preferred_element_type=jnp.float32).astype(jnp.bfloat16)
+
+
+def scatter_replicas(matrices):
+    flat = jnp.concatenate([piece.reshape(-1, 128) for piece in matrices], axis=0)
+    return lax.psum_scatter(flat, "dp", scatter_dimension=0, tiled=True)
 
 
 def body(
@@ -159,134 +213,131 @@
 ):
     low_type = jnp.bfloat16
     shard_count = lax.axis_size("cp")
+    replica_count = lax.axis_size("dp")
     local_rows = tokens.shape[0]
-    window_rows = local_rows * shard_count
-    longest = window_rows // 2
+    longest = local_rows * shard_count // 2
     group_size = H // KVH
     score_scale = HD ** (-0.5)
     my_shard = lax.axis_index("cp")
-    shard_query, shard_key, shard_value, shard_out, shard_gate, shard_up, shard_down = split_owned(
-        params, shard_count
-    )
-    w_query, w_key, w_value, w_out, w_gate, w_up, w_down, gain_pair = (
-        lax.all_gather(shard_query.astype(low_type), "cp", axis=0, tiled=True),
-        lax.all_gather(shard_key.astype(low_type), "cp", axis=0, tiled=True),
-        lax.all_gather(shard_value.astype(low_type), "cp", axis=0, tiled=True),
-        lax.all_gather(shard_out.astype(low_type), "cp", axis=0, tiled=True),
-        lax.all_gather(shard_gate.astype(low_type), "cp", axis=0, tiled=True),
-        lax.all_gather(shard_up.astype(low_type), "cp", axis=0, tiled=True),
-        lax.all_gather(shard_down.astype(low_type), "cp", axis=0, tiled=True),
-        lax.all_gather(norm_gains.astype(low_type), "cp", axis=1, tiled=True),
-    )
+    low_params = params.astype(low_type)
+    half_query, half_key, half_value, half_out, half_gate, half_up, half_down = split_owned(
+        low_params, shard_count
+    )
+    gains_low = norm_gains.astype(low_type)
+    gain_pair = in_order(gains_low, swap_shards(gains_low), my_shard, 1)
+    w_qkv = gather_rows(jnp.concatenate([half_query, half_key, half_value], axis=1))
+    w_out = gather_rows(half_out)
+    w_pair = gather_rows(jnp.concatenate([half_gate, half_up], axis=1))
+    w_down = gather_rows(half_down)
+
+    out_peer = swap_shards(out_grad)
     segment_all, position_all = window_layout(lengths[0], slot_positions[0])
-    segment_mine = lax.dynamic_slice_in_dim(segment_all, my_shard * local_rows, local_rows)
-    position_mine = lax.dynamic_slice_in_dim(position_all, my_shard * local_rows, local_rows)
-    allowed = (segment_mine[:, None] == segment_all[None, :]) & (
-        position_all[None, :] <= position_mine[:, None]
+
+    def shard_rows(values, shard):
+        return lax.dynamic_slice_in_dim(values, shard * local_rows, local_rows)
+
+    segment_mine = shard_rows(segment_all, my_shard)
+    position_mine = shard_rows(position_all, my_shard)
+    segment_keys = jnp.concatenate([segment_mine, shard_rows(segment_all, 1 - my_shard)])
+    position_keys = jnp.concatenate([position_mine, shard_rows(position_all, 1 - my_shard)])
+    allowed = (segment_mine[:, None] == segment_keys[None, :]) & (
+        position_keys[None, :] <= position_mine[:, None]
     )
     cosine, sine_vals = rope_tables(position_mine)
     inputs = tokens.astype(jnp.float32)
     normed_one, pull_one = jax.vjp(rms_norm, inputs, gain_pair[0].astype(jnp.float32))
     xn_one = normed_one.astype(low_type)
-    query_pre = jnp.dot(xn_one, w_query, preferred_element_type=jnp.float32)
-    key_pre = jnp.dot(xn_one, w_key, preferred_element_type=jnp.float32)
-    value_low = jnp.dot(xn_one, w_value, preferred_element_type=jnp.float32).astype(low_type)
+    one_mine, one_theirs = split_columns(xn_one, my_shard)
+    one_peer = swap_shards(one_theirs)
+    qkv_pre = jnp.dot(xn_one, w_qkv, preferred_element_type=jnp.float32)
+    query_pre = qkv_pre[:, :QD]
+    key_pre = qkv_pre[:, QD : QD + KD]
+    value_low = qkv_pre[:, QD + KD :].astype(low_type)
     query_rot = rotate(query_pre.reshape(local_rows, H, HD), cosine, sine_vals, 1.0).astype(
         low_type
     )
     key_rot = rotate(key_pre.reshape(local_rows, KVH, HD), cosine, sine_vals, 1.0).astype(low_type)
-    keys_all, values_all = (
-        lax.all_gather(key_rot, "cp", axis=0, tiled=True),
-        lax.all_gather(value_low.reshape(local_rows, KVH, HD), "cp", axis=0, tiled=True),
-    )
-    key_groups = keys_all.transpose(1, 0, 2)
-    value_groups = values_all.transpose(1, 0, 2)
+    key_value = jnp.concatenate([key_rot.reshape(local_rows, KD), value_low], axis=1)
+    key_value = jnp.concatenate([key_value, swap_shards(key_value)], axis=0)
+    key_groups = key_value[:, :KD].reshape(-1, KVH, HD).transpose(1, 0, 2)
+    value_groups = key_value[:, KD:].reshape(-1, KVH, HD).transpose(1, 0, 2)
     query_groups = query_rot.reshape(local_rows, KVH, group_size, HD).transpose(1, 0, 2, 3)
     attended, log_sums = lax.map(
         lambda group_args: group_forward(group_args, allowed, score_scale),
         (query_groups, key_groups, value_groups),
     )
     attn_low = attended.transpose(1, 0, 2, 3).reshape(local_rows, QD).astype(low_type)
+    attn_mine, attn_theirs = split_columns(attn_low, my_shard)
+    attn_peer = swap_shards(attn_theirs)
     resid_one = inputs + jnp.dot(attn_low, w_out, preferred_element_type=jnp.float32)
     normed_two, pull_two = jax.vjp(rms_norm, resid_one, gain_pair[1].astype(jnp.float32))
     xn_two = normed_two.astype(low_type)
-    gate_act = jnp.dot(xn_two, w_gate, preferred_element_type=jnp.float32)
-    up_act = jnp.dot(xn_two, w_up, preferred_element_type=jnp.float32)
+    two_mine, two_theirs = split_columns(xn_two, my_shard)
+    two_peer = swap_shards(two_theirs)
+    pair_act = jnp.dot(xn_two, w_pair, preferred_element_type=jnp.float32)
+    gate_act = pair_act[:, :FF]
+    up_act = pair_act[:, FF:]
     hidden_act, pull_act = jax.vjp(swiglu, gate_act, up_act)
     hidden_low = hidden_act.astype(low_type)
+    hidden_mine, hidden_theirs = split_columns(hidden_low, my_shard)
+    hidden_peer = swap_shards(hidden_theirs)
     block_out = resid_one + jnp.dot(hidden_low, w_down, preferred_element_type=jnp.float32)
     grad_hidden = jnp.dot(out_grad, w_down.T, preferred_element_type=jnp.float32)
-    grad_down = jnp.dot(hidden_low.T, out_grad, preferred_element_type=jnp.float32)
     grad_gate_act, grad_up_act = pull_act(grad_hidden)
-    gate_back = grad_gate_act.astype(low_type)
-    up_back = grad_up_act.astype(low_type)
-    grad_gate = jnp.dot(xn_two.T, gate_back, preferred_element_type=jnp.float32)
-    grad_up = jnp.dot(xn_two.T, up_back, preferred_element_type=jnp.float32)
-    grad_xn_two = jnp.dot(gate_back, w_gate.T, preferred_element_type=jnp.float32) + jnp.dot(
-        up_back, w_up.T, preferred_element_type=jnp.float32
-    )
+    pair_back = jnp.concatenate(
+        [grad_gate_act.astype(low_type), grad_up_act.astype(low_type)], axis=1
+    )
+    pair_peer = swap_shards(pair_back)
+    grad_down = owned_product(hidden_mine, hidden_peer, out_grad, out_peer)
+    down_piece = scatter_replicas([grad_down])
+    grad_xn_two = jnp.dot(pair_back, w_pair.T, preferred_element_type=jnp.float32)
     back_two, gain_grad_two = pull_two(grad_xn_two)
     grad_resid = out_grad.astype(jnp.float32) + back_two
     resid_low = grad_resid.astype(low_type)
-    grad_out = jnp.dot(attn_low.T, resid_low, preferred_element_type=jnp.float32)
+    resid_peer = swap_shards(resid_low)
+    grad_pair = owned_product(two_mine, two_peer, pair_back, pair_peer)
+    pair_piece = scatter_replicas([grad_pair[:, :FF], grad_pair[:, FF:]])
     grad_attn = jnp.dot(resid_low, w_out.T, preferred_element_type=jnp.float32).astype(low_type)
     grad_groups = grad_attn.reshape(local_rows, KVH, group_size, HD).transpose(1, 0, 2, 3)
     grad_q, grad_k_part, grad_v_part = lax.map(
         lambda group_args: group_backward(group_args, allowed, score_scale),
         (query_groups, key_groups, value_groups, grad_groups, log_sums),
     )
-    key_terms = grad_k_part.transpose(1, 0, 2).reshape(window_rows, KD)
-    value_terms = grad_v_part.transpose(1, 0, 2).reshape(window_rows, KD)
-    key_mine, value_mine = (
-        lax.psum_scatter(
-            key_terms.astype(jnp.bfloat16), "cp", scatter_dimension=0, tiled=True
-        ).astype(jnp.float32),
-        lax.psum_scatter(
-            value_terms.astype(jnp.bfloat16), "cp", scatter_dimension=0, tiled=True
-        ).astype(jnp.float32),
+    key_terms = grad_k_part.transpose(1, 0, 2).reshape(-1, KD)
+    value_terms = grad_v_part.transpose(1, 0, 2).reshape(-1, KD)
+    terms = jnp.concatenate([key_terms, value_terms], axis=1)
+    terms_mine = terms[:local_rows] + swap_shards(terms[local_rows:].astype(low_type)).astype(
+        jnp.float32
     )
     query_back = rotate(
         grad_q.transpose(1, 0, 2, 3).reshape(local_rows, H, HD), cosine, sine_vals, -1.0
     )
-    query_back = query_back.reshape(local_rows, QD).astype(low_type)
-    key_back = rotate(key_mine.reshape(local_rows, KVH, HD), cosine, sine_vals, -1.0)
-    key_back = key_back.reshape(local_rows, KD).astype(low_type)
-    value_back = value_mine.astype(low_type)
-    grad_query = jnp.dot(xn_one.T, query_back, preferred_element_type=jnp.float32)
-    grad_key = jnp.dot(xn_one.T, key_back, preferred_element_type=jnp.float32)
-    grad_value = jnp.dot(xn_one.T, value_back, preferred_element_type=jnp.float32)
-    grad_xn_one = (
-        jnp.dot(query_back, w_query.T, preferred_element_type=jnp.float32)
-        + jnp.dot(key_back, w_key.T, preferred_element_type=jnp.float32)
-        + jnp.dot(value_back, w_value.T, preferred_element_type=jnp.float32)
-    )
+    key_back = rotate(terms_mine[:, :KD].reshape(local_rows, KVH, HD), cosine, sine_vals, -1.0)
+    qkv_back = jnp.concatenate(
+        [
+            query_back.reshape(local_rows, QD).astype(low_type),
+            key_back.reshape(local_rows, KD).astype(low_type),
+            terms_mine[:, KD:].astype(low_type),
+        ],
+        axis=1,
+    )
+    qkv_peer = swap_shards(qkv_back)
+    grad_xn_one = jnp.dot(qkv_back, w_qkv.T, preferred_element_type=jnp.float32)
     back_one, gain_grad_one = pull_one(grad_xn_one)
     input_grad = grad_resid + back_one
-    gain_local = jnp.stack([gain_grad_one, gain_grad_two])
-    grad_owner = jnp.concatenate(
+    grad_out = owned_product(attn_mine, attn_peer, resid_low, resid_peer)
+    grad_qkv = owned_product(one_mine, one_peer, qkv_back, qkv_peer)
+    attn_piece = scatter_replicas(
+        [grad_qkv[:, :QD], grad_qkv[:, QD : QD + KD], grad_qkv[:, QD + KD :], grad_out]
+    )
+    gain_all = lax.psum(jnp.stack([gain_grad_one, gain_grad_two]), ("dp", "cp"))
+    gain_owned = split_columns(gain_all, my_shard)[0]
+    owned_grad = jnp.concatenate(
         [
-            piece.reshape(shard_count, -1)
-            for piece in (grad_query, grad_key, grad_value, grad_out, grad_gate, grad_up, grad_down)
-        ],
-        axis=1,
-    )
-    replica_count = lax.axis_size("dp")
-    owned_part, gain_part = (
-        lax.psum_scatter(
-            grad_owner.astype(jnp.bfloat16), "cp", scatter_dimension=0, tiled=True
-        ).astype(jnp.float32),
-        lax.psum_scatter(
-            gain_local.astype(jnp.bfloat16), "cp", scatter_dimension=1, tiled=True
-        ).astype(jnp.float32),
-    )
-    replica_rows = owned_part.reshape(replica_count, -1)
-    replica_piece = lax.psum_scatter(replica_rows, "dp", scatter_dimension=0, tiled=True)
-    owned_grad = (
-        lax.all_gather(replica_piece.astype(jnp.bfloat16), "dp", axis=0, tiled=True)
-        .astype(replica_piece.dtype)
-        .reshape(-1)
-    )
-    gain_owned = lax.psum(gain_part, "dp")
+            lax.all_gather(piece, "dp", axis=0, tiled=True).reshape(-1)
+            for piece in (attn_piece, pair_piece, down_piece)
+        ]
+    ).astype(jnp.float32)
     step_rates = owner_rates(shard_count, longest)
     new_first, new_second, new_params = adamw_step(
         params, owned_grad, first_moment, second_moment, step_rates, decay_coef

time: 1750 us -> 694 us (0.40)
  blocking collectives: 466 us -> 40.2 us
  waiting for transfers between devices: 706 us -> 304 us
  other arithmetic: 288 us -> 107 us
  local copies, waits for them, and re-layouts: 163 us -> 111 us
  starting transfers between devices: 0.42 us -> 24.6 us
  matrix products: 103 us -> 83.7 us
    unnamed x1 -> x0, blocking collectives: 411 us -> none
    unnamed x12 -> x8, waiting for transfers between devices: 434 us -> 36.6 us
    reshape x3 -> x0, other arithmetic: 218 us -> none  [the longest x1 193 us: body(): replica_rows = owned_part.reshape(replica_count, -1)]
    all_gather x6 -> x3, waiting for transfers between devices: 271 us -> 89.1 us  [body(): lax.all_gather(piece, 'dp', axis=0, tiled=True).reshape(-1)]
    ppermute x0 -> x27, waiting for transfers between devices: none -> 102 us  [the longest x15 84.3 us: swap_shards(): return lax.ppermute(values, 'cp', [(0, 1), (1, 0)])]
    reduce_scatter x2 -> x1, waiting for transfers between devices: 1.18 us -> 76.8 us  [scatter_replicas(): return lax.psum_scatter(flat, 'dp', scatter_dimension=0, tiled=True)]
    all_gather x5 -> x0, blocking collectives: 54.2 us -> none  [the longest x1 16.5 us: body(): lax.all_gather(shard_value.astype(low_type), 'cp', axis=0, tiled=True)]
    unnamed x101 -> x102, local copies, waits for them, and re-layouts: 69.1 us -> 18.8 us
  transfers between devices with their start and end apart: 10 -> 33, of which waited for: 6 -> 11; matrix products, arithmetic and copies ran while one was open for 11% -> 34% of each run, Pallas kernels for 0% -> 0%
where the time goes in v1:
time: 694 us; the launch traced here: 687 us
  waiting for transfers between devices  304 us (44%)
  local copies, waits for them, and re-layouts  111 us (16%)
  other arithmetic  107 us (15%)
  matrix products  83.7 us (12%)
  blocking collectives  40.2 us (6%)
  starting transfers between devices  24.6 us (4%)
  between operations  15.5 us (2%)
    all_gather x3, waiting for transfers between devices, body(): lax.all_gather(piece, 'dp', axis=0, tiled=True).reshape(-1)  89.1 us
    ppermute x15, waiting for transfers between devices, swap_shards(): return lax.ppermute(values, 'cp', [(0, 1), (1, 0)])  84.3 us
    reduce_scatter x1, waiting for transfers between devices, scatter_replicas(): return lax.psum_scatter(flat, 'dp', scatter_dimension=0, tiled=True)  76.8 us
    sub x2, other arithmetic, adamw_step(): weight - step_rates * (first_hat / (jnp.sqrt(second_hat) + adam_eps) + de...  60.1 us
    psum x1, blocking collectives, body(): gain_all = lax.psum(jnp.stack([gain_grad_one, gain_grad_two]), ('dp', 'cp'))  40.2 us
    unnamed x8, waiting for transfers between devices  36.6 us
    slice x9, local copies, waits for them, and re-layouts, split_owned(): flat[offset:offset + seg_size].reshape(row_count // shard_count, col_count)  22.4 us
    dynamic_update_slice x16, local copies, waits for them, and re-layouts, gather_rows(): whole = lax.dynamic_update_slice_in_dim(whole, piece, other + place, 0)  22 us
  transfers between devices with their start and end apart: 33, of which 11 were waited for; matrix products, arithmetic and copies ran while one was open for 34% of the time, Pallas kernels for 0%

profile of v1, /device:TPU:0, one launch (start us, length us, event | category | flops | bytes accessed | tf_op | source)
XLA Modules:
  0.0 686.9 jit_solution(9563055866254204413)
XLA Ops:
  10.9 7.4 %convert_element_type.102 = bf16[4915200]{0:T(1024)(128)(2,1)S(1)} convert(f32[4915200]{0:T(1024)} %param.18) | non-fusion elementwise | flops 4915200 | bytes 29491200 | tf_op jit(solution)/shard_map/convert_element_type | solution.py:222
  37.0 5.8 slice.213
  68.7 5.1 broadcast_in_dim.113
  91.6 5.6 collective-permute-done.14
  111.1 5.8 collective-permute-done.15
  120.4 9.7 %while.30 = (s32[]{:T(128)}, bf16[5,256,3,64]{1,3,2,0:T(8,128)(2,1)}, f32[5,3,256,1]{2,1,3,0:T(4,128)S(1)}, bf16[5,512,64]{1,2,0:T(8,128)(2,1)S(1)}, bf16[5,512,...) while((s32[]{:T(128)}, ...), condition=%wide.region_7.8_spmd.clone.clone, body=%wide.region_4.7_spmd.clone.sunk.clone | while | flops 104201472 | bytes 5444721 | solution.py:265
  133.0 9.9 %collective-permute-done.11 = bf16[1,120,5120]{2,1,0:T(8,128)(2,1)} collective-permute-done((bf16[1,120,5120]{2,1,0:T(8,128)(2,1)}, bf16[1,120,5120]{2,1,0:T(8,128)(2,1)}, u32[]{:S(2)}, u32[]{:S(2)}) %collective-permute-start.11) | collective-permute-done | bytes 1228832 | tf_op jit(solution)/shard_map/ppermute | solution.py:153
  150.8 5.7 fusion.115
  156.5 6.2 fusion.54
  162.8 8.2 %multiply_reduce_fusion = (f32[960]{0:T(1024)}, f32[256]{0:T(256)S(1)}, f32[256,960]{0,1:T(8,128)S(1)}) fusion(f32[256,960]{0,1:T(8,128)S(1)} %get-tuple-element.270, f32[256]{0:T(256)S(1)} %fusion.94, f32[960]{0:T(1024)S(1)} %bitcast.259, bf16[960,5120]{1,0:T(8,128)(2,1)} %bitcast.23, bf16[256,2560]{1,0:T(8,128)(2,1)S(1)} %get-tuple-element.237, ...), kind=kOutput, calls=%fused_computation.122 | convolution fusion | flops 2523298560 | bytes 14427648 | tf_op jit(solution)/shard_map/dot_general | solution.py:293
  175.4 28.4 %while.31 = (s32[]{:T(128)}, f32[5,256,3,64]{1,3,2,0:T(8,128)}, f32[5,512,64]{1,2,0:T(8,128)S(1)}, f32[5,512,64]{1,2,0:T(8,128)}, bf16[5,512,64]{1,2,0:T(8,128)(...) while((s32[]{:T(128)}, f32[5,256,3,64]{1,3,2,0:T(8,128)}, ...), condition=%wide.region_12.13_spmd.clone.clone, body=%wide.region_10.12_spmd.clone.sunk.clone | while | flops 255671552 | bytes 13134985 | solution.py:302
  212.0 11.2 %collective-permute-done.25 = bf16[256,1280]{1,0:T(8,128)(2,1)S(1)} collective-permute-done((bf16[256,1280]{1,0:T(8,128)(2,1)S(1)}, bf16[256,1280]{1,0:T(8,128)(2,1)S(1)}, u32[]{:S(2)}, u32[]{:S(2)}) %collective-permute-start.25) | collective-permute-done | bytes 655392 | tf_op jit(solution)/shard_map/ppermute | solution.py:149
  242.1 67.0 %collective-permute-done.21 = bf16[256,480]{0,1:T(8,128)(2,1)S(1)} collective-permute-done((bf16[256,480]{0,1:T(8,128)(2,1)S(1)}, bf16[256,480]{0,1:T(8,128)(2,1)S(1)}, u32[]{:S(2)}, u32[]{:S(2)}) %collective-permute-start.21) | collective-permute-done | bytes 245792 | tf_op jit(solution)/shard_map/ppermute | solution.py:149
  320.5 10.9 %pad_maximum_fusion.3 = bf16[9600,128]{1,0:T(8,128)(2,1)} fusion(bf16[3600,128]{1,0:T(8,128)(2,1)S(1)} %reshape.340, bf16[1200,128]{1,0:T(8,128)(2,1)} %reshape.339, bf16[1200,128]{1,0:T(8,128)(2,1)} %reshape.338, bf16[3600,128]{1,0:T(8,128)(2,1)S(1)} %reshape.337), kind=kLoop, calls=%fused_computation.84 | loop fusion | flops 9830400 | bytes 4915200 | tf_op jit(solution)/shard_map/concatenate | solution.py:198
  331.7 5.4 convolution_convert_fusion
  338.9 6.0 reshape.343
  348.8 6.8 pad_maximum_fusion.1
  359.6 36.5 %reduce-scatter.10.cloned.1.call-done = bf16[600,128]{1,0:T(8,128)(2,1)} async-done(((bf16[9600,128]{1,0:T(8,128)(2,1)}), bf16[600,128]{1,0:T(8,128)(2,1)}) %reduce-scatter.10.cloned.1.call-update) | async-done | bytes 153616
  400.2 76.8 %reduce-scatter.8.cloned.1.call-done = bf16[1200,128]{1,0:T(8,128)(2,1)} async-done(((bf16[19200,128]{1,0:T(8,128)(2,1)}), bf16[1200,128]{1,0:T(8,128)(2,1)}) %reduce-scatter.8.cloned.1.call-update) | async-done | bytes 307216 | tf_op jit(solution)/shard_map/reduce_scatter | solution.py:199
  479.5 5.7 convolution_add_fusion
  487.4 40.2 %psum.7 = f32[2,960]{1,0:T(2,128)S(1)} all-reduce(f32[2,960]{1,0:T(2,128)S(1)} %pad_maximum_fusion.11), channel_id=1, replica_groups=mesh['dp'=16,'cp'=2] {'dp','cp'}, use_global_device_ids=true, to_apply=%region_19.20 | all-reduce | flops 1920 | bytes 15360 | tf_op jit(solution)/shard_map/psum | solution.py:333
  531.1 33.5 %all-gather.4.cloned.1.call-done = bf16[9600,128]{1,0:T(8,128)(2,1)} async-done(((bf16[600,128]{1,0:T(8,128)(2,1)}), bf16[9600,128]{1,0:T(8,128)(2,1)}) %all-gather.4.cloned.1.call-update) | async-done | bytes 2457616 | tf_op jit(solution)/shard_map/all_gather | solution.py:337
  564.6 55.6 %all-gather.6.cloned.1.call-done = bf16[19200,128]{1,0:T(8,128)(2,1)} async-done(((bf16[1200,128]{1,0:T(8,128)(2,1)}), bf16[19200,128]{1,0:T(8,128)(2,1)}) %all-gather.6.cloned.1.call-update) | async-done | bytes 4915216 | tf_op jit(solution)/shard_map/all_gather | solution.py:337
  620.2 59.4 %multiply_subtract_fusion = (f32[4915200]{0:T(1024)}, f32[4915200]{0:T(1024)}, f32[4915200]{0:T(1024)}, f32[4915200]{0:T(1024)}) fusion(f32[4915200]{0:T(1024)} %param.18, f32[4915200]{0:T(1024)} %broadcast_dynamic-update-slice_fusion.1, f32[4915200]{0:T(1024)} %param.20, f32[4915200]{0:T(1024)} %param.19, bf16[1228800]{0:T(1024)(128)(2,1)} %bitcast.239, ...), kind=kLoop, calls=%fused_computation.60 | loop fusion | flops 103219200 | bytes 167116800 | tf_op jit(solution)/shard_map/sub | solution.py:142
  (340 shorter events, 196.6 us)
Async XLA Ops:
  7.2 351.0 %reduce-scatter.12.cloned.1.call-start = ((), (), s32[]{:S(2)}) async-start(), calls=%async_computation.8 | async-start | bytes 2611200
  7.9 73.5 %collective-permute-start = (bf16[2,480]{1,0:T(2,128)(2,1)S(1)}, bf16[2,480]{1,0:T(2,128)(2,1)S(1)}, u32[]{:S(2)}, u32[]{:S(2)}) collective-permute-start(bf16[2,480]{1,0:T(2,128)(2,1)S(1)} %convert_element_type.100), channel_id=1, source_target_pairs={{0,1},{1,0},{2,3},{3,2},{4,5},{5,4},{6,7},{7,6},{8,9},{9,8},{10,11... | collective-permute-start | bytes 5768 | tf_op jit(solution)/shard_map/ppermute | solution.py:149
  28.4 56.3 %collective-permute-start.1 = (bf16[1,120,1600]{2,1,0:T(8,128)(2,1)}, bf16[1,120,1600]{2,1,0:T(8,128)(2,1)}, u32[]{:S(2)}, u32[]{:S(2)}) collective-permute-start(bf16[1,120,1600]{2,1,0:T(8,128)(2,1)} %constant_dynamic-slice_fusion.3), channel_id=1, source_target_pairs={{0,1},{1,0},{2,3},{3,2},{4,5},{5,4},{6,7},{7,6},{8,9},{9,8},{10,11... | collective-permute-start | bytes 1152008 | tf_op jit(solution)/shard_map/ppermute | solution.py:149
  30.2 51.6 %collective-permute-start.6 = (bf16[1,120,960]{2,1,0:T(8,128)(2,1)}, bf16[1,120,960]{2,1,0:T(8,128)(2,1)S(1)}, u32[]{:S(2)}, u32[]{:S(2)}) collective-permute-start(bf16[1,120,960]{2,1,0:T(8,128)(2,1)} %constant_dynamic-slice_fusion.2), channel_id=1, source_target_pairs={{0,1},{1,0},{2,3},{3,2},{4,5},{5,4},{6,7},{7,6},{8,9},{9,8},{10,11... | collective-permute-start | bytes 691208 | tf_op jit(solution)/shard_map/ppermute | solution.py:149
  52.8 55.8 %collective-permute-start.10 = (bf16[1,120,5120]{2,1,0:T(8,128)(2,1)}, bf16[1,120,5120]{2,1,0:T(8,128)(2,1)}, u32[]{:S(2)}, u32[]{:S(2)}) collective-permute-start(bf16[1,120,5120]{2,1,0:T(8,128)(2,1)} %constant_dynamic-slice_fusion.1), channel_id=1, source_target_pairs={{0,1},{1,0},{2,3},{3,2},{4,5},{5,4},{6,7},{7,6},{8,9},{9,8},{10,11... | collective-permute-start | bytes 3686408 | tf_op jit(solution)/shard_map/ppermute | solution.py:149
  58.7 38.4 %collective-permute-start.14 = (bf16[1,320,960]{2,1,0:T(8,128)(2,1)}, bf16[1,320,960]{2,1,0:T(8,128)(2,1)}, u32[]{:S(2)}, u32[]{:S(2)}) collective-permute-start(bf16[1,320,960]{2,1,0:T(8,128)(2,1)} %constant_dynamic-slice_fusion), channel_id=1, source_target_pairs={{0,1},{1,0},{2,3},{3,2},{4,5},{5,4},{6,7},{7,6},{8,9},{9,8},{10,11... | collective-permute-start | bytes 1843208 | tf_op jit(solution)/shard_map/ppermute | solution.py:149
  81.4 130.5 %collective-permute-start.26 = (bf16[256,960]{0,1:T(8,128)(2,1)}, bf16[256,960]{0,1:T(8,128)(2,1)}, u32[]{:S(2)}, u32[]{:S(2)}) collective-permute-start(bf16[256,960]{0,1:T(8,128)(2,1)} %param.15), channel_id=1, source_target_pairs={{0,1},{1,0},{2,3},{3,2},{4,5},{5,4},{6,7},{7,6},{8,9},{9,8},{10,11... | collective-permute-start | bytes 1474568 | tf_op jit(solution)/shard_map/ppermute | solution.py:149
  99.1 17.8 %collective-permute-start.15 = (bf16[1,320,960]{2,1,0:T(8,128)(2,1)}, bf16[1,320,960]{2,1,0:T(8,128)(2,1)}, u32[]{:S(2)}, u32[]{:S(2)}) collective-permute-start(bf16[1,320,960]{2,1,0:T(8,128)(2,1)} %collective-permute-done.14), channel_id=1, source_target_pairs={{0,4},{2,6},{4,0},{6,2},{8,12},{10,14},{12,8},{14,10},{16,20},{18,... | collective-permute-start | bytes 1843208 | tf_op jit(solution)/shard_map/ppermute | solution.py:153
  108.6 34.3 %collective-permute-start.11 = (bf16[1,120,5120]{2,1,0:T(8,128)(2,1)}, bf16[1,120,5120]{2,1,0:T(8,128)(2,1)}, u32[]{:S(2)}, u32[]{:S(2)}) collective-permute-start(bf16[1,120,5120]{2,1,0:T(8,128)(2,1)} %collective-permute-done.10), channel_id=1, source_target_pairs={{0,4},{2,6},{4,0},{6,2},{8,12},{10,14},{12,8},{14,10},{16,20},{18,... | collective-permute-start | bytes 3686408 | tf_op jit(solution)/shard_map/ppermute | solution.py:153
  116.9 30.3 %collective-permute-start.12 = (bf16[1,120,5120]{2,1,0:T(8,128)(2,1)}, bf16[1,120,5120]{2,1,0:T(8,128)(2,1)}, u32[]{:S(2)}, u32[]{:S(2)}) collective-permute-start(bf16[1,120,5120]{2,1,0:T(8,128)(2,1)} %collective-permute-done.10), channel_id=1, source_target_pairs={{0,2},{2,0},{4,6},{6,4},{8,10},{10,8},{12,14},{14,12},{16,18},{18,... | collective-permute-start | bytes 3686408 | tf_op jit(solution)/shard_map/ppermute | solution.py:153
  118.9 24.0 %collective-permute-start.17 = (bf16[1,320,960]{2,1,0:T(8,128)(2,1)}, bf16[1,320,960]{2,1,0:T(8,128)(2,1)}, u32[]{:S(2)}, u32[]{:S(2)}) collective-permute-start(bf16[1,320,960]{2,1,0:T(8,128)(2,1)} %collective-permute-done.15), channel_id=1, source_target_pairs={{0,2},{2,0},{4,6},{6,4},{8,10},{10,8},{12,14},{14,12},{16,18},{18,... | collective-permute-start | bytes 1843208 | tf_op jit(solution)/shard_map/ppermute | solution.py:153
  175.1 135.8 %collective-permute-start.22 = (bf16[256,960]{0,1:T(8,128)(2,1)}, bf16[256,960]{0,1:T(8,128)(2,1)}, u32[]{:S(2)}, u32[]{:S(2)}) collective-permute-start(bf16[256,960]{0,1:T(8,128)(2,1)} %fusion.100), channel_id=1, source_target_pairs={{0,1},{1,0},{2,3},{3,2},{4,5},{5,4},{6,7},{7,6},{8,9},{9,8},{10,11... | collective-permute-start | bytes 1474568 | tf_op jit(solution)/shard_map/ppermute | solution.py:149
  205.5 17.6 %collective-permute-start.25 = (bf16[256,1280]{1,0:T(8,128)(2,1)S(1)}, bf16[256,1280]{1,0:T(8,128)(2,1)S(1)}, u32[]{:S(2)}, u32[]{:S(2)}) collective-permute-start(bf16[256,1280]{1,0:T(8,128)(2,1)S(1)} %get-tuple-element.244), channel_id=1, source_target_pairs={{0,1},{1,0},{2,3},{3,2},{4,5},{5,4},{6,7},{7,6},{8,9},{9,8},{10,11... | collective-permute-start | bytes 1966088 | tf_op jit(solution)/shard_map/ppermute | solution.py:149
  208.1 27.1 %collective-permute-start.18 = (bf16[256,640]{0,1:T(8,128)(2,1)}, bf16[256,640]{0,1:T(8,128)(2,1)S(1)}, u32[]{:S(2)}, u32[]{:S(2)}) collective-permute-start(bf16[256,640]{0,1:T(8,128)(2,1)} %fusion.82), channel_id=1, source_target_pairs={{0,1},{1,0},{2,3},{3,2},{4,5},{5,4},{6,7},{7,6},{8,9},{9,8},{10,11... | collective-permute-start | bytes 983048 | tf_op jit(solution)/shard_map/ppermute | solution.py:149
  210.3 121.5 %collective-permute-start.24 = (bf16[256,5120]{1,0:T(8,128)(2,1)}, bf16[256,5120]{1,0:T(8,128)(2,1)}, u32[]{:S(2)}, u32[]{:S(2)}) collective-permute-start(bf16[256,5120]{1,0:T(8,128)(2,1)} %pad_maximum_fusion.2), channel_id=1, source_target_pairs={{0,1},{1,0},{2,3},{3,2},{4,5},{5,4},{6,7},{7,6},{8,9},{9,8},{10,11... | collective-permute-start | bytes 7864328 | tf_op jit(solution)/shard_map/ppermute | solution.py:149
  233.9 162.2 %reduce-scatter.10.cloned.1.call-start = ((), (), s32[]{:S(2)}) async-start(), calls=%async_computation.7 | async-start | bytes 2611200
  236.6 77.8 %collective-permute-start.20 = (bf16[256,1600]{0,1:T(8,128)(2,1)}, bf16[256,1600]{0,1:T(8,128)(2,1)}, u32[]{:S(2)}, u32[]{:S(2)}) collective-permute-start(bf16[256,1600]{0,1:T(8,128)(2,1)} %pad_maximum_fusion.4), channel_id=1, source_target_pairs={{0,1},{1,0},{2,3},{3,2},{4,5},{5,4},{6,7},{7,6},{8,9},{9,8},{10,11... | collective-permute-start | bytes 2457608 | tf_op jit(solution)/shard_map/ppermute | solution.py:149
  238.4 70.8 %collective-permute-start.21 = (bf16[256,480]{0,1:T(8,128)(2,1)S(1)}, bf16[256,480]{0,1:T(8,128)(2,1)S(1)}, u32[]{:S(2)}, u32[]{:S(2)}) collective-permute-start(bf16[256,480]{0,1:T(8,128)(2,1)S(1)} %get-tuple-element.254), channel_id=1, source_target_pairs={{0,1},{1,0},{2,3},{3,2},{4,5},{5,4},{6,7},{7,6},{8,9},{9,8},{10,11... | collective-permute-start | bytes 737288 | tf_op jit(solution)/shard_map/ppermute | solution.py:149
  239.6 74.8 %collective-permute-start.19 = (bf16[256,480]{0,1:T(8,128)(2,1)}, bf16[256,480]{0,1:T(8,128)(2,1)S(1)}, u32[]{:S(2)}, u32[]{:S(2)}) collective-permute-start(bf16[256,480]{0,1:T(8,128)(2,1)} %get-tuple-element.252), channel_id=1, source_target_pairs={{0,1},{1,0},{2,3},{3,2},{4,5},{5,4},{6,7},{7,6},{8,9},{9,8},{10,11... | collective-permute-start | bytes 737288 | tf_op jit(solution)/shard_map/ppermute | solution.py:149
  309.2 22.5 %collective-permute-start.23 = (bf16[256,480]{0,1:T(8,128)(2,1)}, bf16[256,480]{0,1:T(8,128)(2,1)}, u32[]{:S(2)}, u32[]{:S(2)}) collective-permute-start(bf16[256,480]{0,1:T(8,128)(2,1)} %get-tuple-element.256), channel_id=1, source_target_pairs={{0,1},{1,0},{2,3},{3,2},{4,5},{5,4},{6,7},{7,6},{8,9},{9,8},{10,11... | collective-permute-start | bytes 737288 | tf_op jit(solution)/shard_map/ppermute | solution.py:149
  331.4 145.6 %reduce-scatter.8.cloned.1.call-start = ((), (), s32[]{:S(2)}) async-start(), calls=%async_computation.4 | async-start | bytes 5222400 | tf_op jit(solution)/shard_map/reduce_scatter | solution.py:199
  355.6 175.5 %all-gather.8.cloned.1.call-start = ((), (), s32[]{:S(2)}) async-start(), calls=%async_computation.6 | async-start | bytes 2611200 | tf_op jit(solution)/shard_map/all_gather | solution.py:337
  358.2 206.4 %all-gather.4.cloned.1.call-start = ((), (), s32[]{:S(2)}) async-start(), calls=%async_computation.3 | async-start | bytes 2611200 | tf_op jit(solution)/shard_map/all_gather | solution.py:337
  396.1 224.1 %all-gather.6.cloned.1.call-start = ((), (), s32[]{:S(2)}) async-start(), calls=%async_computation.5 | async-start | bytes 5222400 | tf_op jit(solution)/shard_map/all_gather | solution.py:337
  (58 other events, 825.2 us)
Sparse Core Ops, SparseCore 0:
  234.0 64.4 reduce-scatter.11
  331.5 64.4 reduce-scatter.9
  400.6 76.3 reduce-scatter.7
  479.3 41.6 all-gather.7
  523.3 41.3 all-gather.3
  566.9 53.2 all-gather.5

commit v2 on v1

--- a/solution.py
+++ b/solution.py
@@ -1,6 +1,8 @@
 import jax
 import jax.numpy as jnp
 from jax import lax
+from jax.experimental import pallas as pl
+from jax.experimental.pallas import tpu as pltpu
 from jax.sharding import PartitionSpec as P
 
 D = 960
@@ -41,25 +43,6 @@
     ]
 
 
-def owner_rates(shard_count, longest):
-    pieces = []
-    for shape_pair, rate_value in zip(matrix_shapes(), matrix_rates(longest)):
-        pieces.append(
-            jnp.full((shape_pair[0] // shard_count * shape_pair[1],), rate_value, jnp.float32)
-        )
-    return jnp.concatenate(pieces)
-
-
-def split_owned(flat, shard_count):
-    pieces = []
-    offset = 0
-    for row_count, col_count in matrix_shapes():
-        seg_size = row_count // shard_count * col_count
-        pieces.append(flat[offset : offset + seg_size].reshape(row_count // shard_count, col_count))
-        offset += seg_size
-    return pieces
-
-
 def rms_norm(values, gain_row):
     return (
         values * lax.rsqrt(jnp.mean(values * values, axis=-1, keepdims=True) + eps_norm) * gain_row
@@ -169,15 +152,34 @@
     return (jnp.where(my_shard == 0, lower, upper), jnp.where(my_shard == 0, upper, lower))
 
 
-def gather_rows(half):
+def gather_rows(params, columns):
     my_shard = lax.axis_index("cp")
     quarter = lax.axis_index("dp") % 4
-    mine = half.reshape(4, half.shape[0] // 4, half.shape[1])
+    low_type = jnp.bfloat16
+
+    def piece_of(start, size):
+        return lax.dynamic_slice_in_dim(params, start, size).astype(low_type)
+
+    fetched = jnp.concatenate(
+        [
+            piece_of(offset + quarter * (rows // 4 * width), rows // 4 * width).reshape(
+                1, rows // 4, width
+            )
+            for offset, rows, width in columns
+        ],
+        axis=2,
+    )
+    fetched = swap_shards(fetched)
+    mine = jnp.concatenate(
+        [
+            params[offset : offset + rows * width].astype(low_type).reshape(4, rows // 4, width)
+            for offset, rows, width in columns
+        ],
+        axis=2,
+    )
+    across = swap_replicas(fetched, 2)
+    whole = jnp.concatenate([mine, mine], axis=0)
     other = (1 - my_shard) * 4
-    fetched = swap_shards(lax.dynamic_index_in_dim(mine, quarter, 0))
-    across = swap_replicas(fetched, 2)
-    whole = jnp.zeros((8,) + mine.shape[1:], half.dtype)
-    whole = lax.dynamic_update_slice_in_dim(whole, mine, my_shard * 4, 0)
     for piece, place in (
         (fetched, quarter),
         (across, quarter ^ 2),
@@ -185,7 +187,7 @@
         (swap_replicas(across, 1), quarter ^ 3),
     ):
         whole = lax.dynamic_update_slice_in_dim(whole, piece, other + place, 0)
-    return whole.reshape(-1, half.shape[1])
+    return whole.reshape(-1, whole.shape[2])
 
 
 def owned_product(left_mine, left_peer, right_mine, right_peer):
@@ -194,9 +196,68 @@
     return jnp.dot(left.T, right, preferred_element_type=jnp.float32).astype(jnp.bfloat16)
 
 
-def scatter_replicas(matrices):
-    flat = jnp.concatenate([piece.reshape(-1, 128) for piece in matrices], axis=0)
-    return lax.psum_scatter(flat, "dp", scatter_dimension=0, tiled=True)
+def scatter_replicas(flat, distance):
+    bit = (lax.axis_index("dp") // distance) % 2
+    halves = flat.reshape(2, flat.shape[0] // 2, flat.shape[1])
+    mine = lax.dynamic_index_in_dim(halves, bit, 0, keepdims=False)
+    theirs = lax.dynamic_index_in_dim(halves, 1 - bit, 0, keepdims=False)
+    received = swap_replicas(theirs, distance)
+    return (mine.astype(jnp.float32) + received.astype(jnp.float32)).astype(jnp.bfloat16)
+
+
+def scatter_steps(flat, distance, limit):
+    while distance < limit:
+        flat = scatter_replicas(flat, distance)
+        distance *= 2
+    return flat
+
+
+def gather_steps(piece):
+    distance = lax.axis_size("dp") // 2
+    while distance >= 1:
+        bit = (lax.axis_index("dp") // distance) % 2
+        piece = in_order(piece, swap_replicas(piece, distance), bit, 0)
+        distance //= 2
+    return piece
+
+
+BLOCK = 1200
+CHUNK_BLOCKS = 8
+
+
+def update_kernel(first_rate, last_rate, split, *refs):
+    params_ref, first_ref, second_ref, grad_ref = refs[:4]
+    grad_out, first_out, second_out, params_out = refs[-4:]
+    gradient = grad_ref[...].astype(jnp.float32)
+    rate = jnp.where(pl.program_id(0) < split, first_rate, last_rate)
+    grad_out[...] = gradient
+    first_out[...], second_out[...], params_out[...] = adamw_step(
+        params_ref[...], gradient, first_ref[...], second_ref[...], rate, decay_coef
+    )
+
+
+def update_chunk(state, gradient, chunk, rates, split, earlier):
+    rows = state[0].shape[0]
+
+    def state_block(i):
+        return (chunk * CHUNK_BLOCKS + i, 0)
+
+    spec = pl.BlockSpec((BLOCK, 128), state_block)
+    grad_spec = pl.BlockSpec((BLOCK, 128), lambda i: (i, 0))
+    return pl.pallas_call(
+        lambda *refs: update_kernel(rates[0], rates[1], split, *refs),
+        grid=(CHUNK_BLOCKS,),
+        in_specs=[spec] * 3 + [grad_spec] + [pl.BlockSpec(memory_space=pl.ANY)] * len(earlier),
+        out_specs=[spec] * 4,
+        out_shape=[jax.ShapeDtypeStruct((rows, 128), jnp.float32)] * 4,
+        input_output_aliases={4 + index: index for index in range(len(earlier))},
+        compiler_params=pltpu.CompilerParams(vmem_limit_bytes=40 * 1024 * 1024),
+        cost_estimate=pl.CostEstimate(
+            flops=20 * BLOCK * CHUNK_BLOCKS * 128,
+            bytes_accessed=30 * BLOCK * CHUNK_BLOCKS * 128,
+            transcendentals=0,
+        ),
+    )(*state, gradient, *earlier)
 
 
 def body(
@@ -219,16 +280,17 @@
     group_size = H // KVH
     score_scale = HD ** (-0.5)
     my_shard = lax.axis_index("cp")
-    low_params = params.astype(low_type)
-    half_query, half_key, half_value, half_out, half_gate, half_up, half_down = split_owned(
-        low_params, shard_count
-    )
+    blocks = []
+    offset = 0
+    for row_count, col_count in matrix_shapes():
+        blocks.append((offset, row_count // shard_count, col_count))
+        offset += row_count // shard_count * col_count
     gains_low = norm_gains.astype(low_type)
     gain_pair = in_order(gains_low, swap_shards(gains_low), my_shard, 1)
-    w_qkv = gather_rows(jnp.concatenate([half_query, half_key, half_value], axis=1))
-    w_out = gather_rows(half_out)
-    w_pair = gather_rows(jnp.concatenate([half_gate, half_up], axis=1))
-    w_down = gather_rows(half_down)
+    w_qkv = gather_rows(params, blocks[:3])
+    w_out = gather_rows(params, blocks[3:4])
+    w_pair = gather_rows(params, blocks[4:6])
+    w_down = gather_rows(params, blocks[6:])
 
     out_peer = swap_shards(out_grad)
     segment_all, position_all = window_layout(lengths[0], slot_positions[0])
@@ -262,11 +324,17 @@
     key_groups = key_value[:, :KD].reshape(-1, KVH, HD).transpose(1, 0, 2)
     value_groups = key_value[:, KD:].reshape(-1, KVH, HD).transpose(1, 0, 2)
     query_groups = query_rot.reshape(local_rows, KVH, group_size, HD).transpose(1, 0, 2, 3)
-    attended, log_sums = lax.map(
-        lambda group_args: group_forward(group_args, allowed, score_scale),
-        (query_groups, key_groups, value_groups),
-    )
-    attn_low = attended.transpose(1, 0, 2, 3).reshape(local_rows, QD).astype(low_type)
+    forward_groups = [
+        group_forward(
+            (query_groups[group], key_groups[group], value_groups[group]), allowed, score_scale
+        )
+        for group in range(KVH)
+    ]
+    attn_low = jnp.concatenate(
+        [attended.reshape(local_rows, -1).astype(low_type) for attended, _ in forward_groups],
+        axis=1,
+    )
+    attn_low, one_peer, out_peer = lax.optimization_barrier((attn_low, one_peer, out_peer))
     attn_mine, attn_theirs = split_columns(attn_low, my_shard)
     attn_peer = swap_shards(attn_theirs)
     resid_one = inputs + jnp.dot(attn_low, w_out, preferred_element_type=jnp.float32)
@@ -284,33 +352,53 @@
     block_out = resid_one + jnp.dot(hidden_low, w_down, preferred_element_type=jnp.float32)
     grad_hidden = jnp.dot(out_grad, w_down.T, preferred_element_type=jnp.float32)
     grad_gate_act, grad_up_act = pull_act(grad_hidden)
-    pair_back = jnp.concatenate(
-        [grad_gate_act.astype(low_type), grad_up_act.astype(low_type)], axis=1
-    )
-    pair_peer = swap_shards(pair_back)
-    grad_down = owned_product(hidden_mine, hidden_peer, out_grad, out_peer)
-    down_piece = scatter_replicas([grad_down])
+    gate_back = grad_gate_act.astype(low_type)
+    up_back = grad_up_act.astype(low_type)
+    gate_peer = swap_shards(gate_back)
+    up_peer = swap_shards(up_back)
+    pair_back = jnp.concatenate([gate_back, up_back], axis=1)
+    pair_back, attn_peer, two_peer = lax.optimization_barrier((pair_back, attn_peer, two_peer))
     grad_xn_two = jnp.dot(pair_back, w_pair.T, preferred_element_type=jnp.float32)
     back_two, gain_grad_two = pull_two(grad_xn_two)
     grad_resid = out_grad.astype(jnp.float32) + back_two
     resid_low = grad_resid.astype(low_type)
+    resid_low, hidden_peer = lax.optimization_barrier((resid_low, hidden_peer))
     resid_peer = swap_shards(resid_low)
-    grad_pair = owned_product(two_mine, two_peer, pair_back, pair_peer)
-    pair_piece = scatter_replicas([grad_pair[:, :FF], grad_pair[:, FF:]])
+    grad_down = owned_product(hidden_mine, hidden_peer, out_grad, out_peer).reshape(-1, 128)
+    down_part = scatter_replicas(grad_down, 1)
     grad_attn = jnp.dot(resid_low, w_out.T, preferred_element_type=jnp.float32).astype(low_type)
     grad_groups = grad_attn.reshape(local_rows, KVH, group_size, HD).transpose(1, 0, 2, 3)
-    grad_q, grad_k_part, grad_v_part = lax.map(
-        lambda group_args: group_backward(group_args, allowed, score_scale),
-        (query_groups, key_groups, value_groups, grad_groups, log_sums),
-    )
-    key_terms = grad_k_part.transpose(1, 0, 2).reshape(-1, KD)
-    value_terms = grad_v_part.transpose(1, 0, 2).reshape(-1, KD)
+    backward_groups = []
+    for group in range(KVH):
+        grad_group = grad_groups[group]
+        if group == 3:
+            grad_group, down_part = lax.optimization_barrier((grad_group, down_part))
+            down_part = scatter_replicas(down_part, 2)
+        backward_groups.append(
+            group_backward(
+                (
+                    query_groups[group],
+                    key_groups[group],
+                    value_groups[group],
+                    grad_group,
+                    forward_groups[group][1],
+                ),
+                allowed,
+                score_scale,
+            )
+        )
+    grad_q = jnp.stack([terms[0] for terms in backward_groups], axis=1)
+    key_terms = jnp.concatenate([terms[1] for terms in backward_groups], axis=1)
+    value_terms = jnp.concatenate([terms[2] for terms in backward_groups], axis=1)
     terms = jnp.concatenate([key_terms, value_terms], axis=1)
+    terms, gate_peer, down_part = lax.optimization_barrier((terms, gate_peer, down_part))
+    grad_gate = owned_product(two_mine, two_peer, gate_back, gate_peer).reshape(-1, 128)
+    gate_part = scatter_replicas(grad_gate, 1)
     terms_mine = terms[:local_rows] + swap_shards(terms[local_rows:].astype(low_type)).astype(
         jnp.float32
     )
     query_back = rotate(
-        grad_q.transpose(1, 0, 2, 3).reshape(local_rows, H, HD), cosine, sine_vals, -1.0
+        grad_q.reshape(local_rows, H, HD), cosine, sine_vals, -1.0
     )
     key_back = rotate(terms_mine[:, :KD].reshape(local_rows, KVH, HD), cosine, sine_vals, -1.0)
     qkv_back = jnp.concatenate(
@@ -321,27 +409,41 @@
         ],
         axis=1,
     )
+    qkv_back, up_peer, gate_part = lax.optimization_barrier((qkv_back, up_peer, gate_part))
+    grad_up = owned_product(two_mine, two_peer, up_back, up_peer).reshape(-1, 128)
     qkv_peer = swap_shards(qkv_back)
     grad_xn_one = jnp.dot(qkv_back, w_qkv.T, preferred_element_type=jnp.float32)
     back_one, gain_grad_one = pull_one(grad_xn_one)
     input_grad = grad_resid + back_one
     grad_out = owned_product(attn_mine, attn_peer, resid_low, resid_peer)
     grad_qkv = owned_product(one_mine, one_peer, qkv_back, qkv_peer)
-    attn_piece = scatter_replicas(
-        [grad_qkv[:, :QD], grad_qkv[:, QD : QD + KD], grad_qkv[:, QD + KD :], grad_out]
-    )
-    gain_all = lax.psum(jnp.stack([gain_grad_one, gain_grad_two]), ("dp", "cp"))
-    gain_owned = split_columns(gain_all, my_shard)[0]
-    owned_grad = jnp.concatenate(
+    gain_local = jnp.stack([gain_grad_one, gain_grad_two])
+    gain_mine, gain_theirs = split_columns(gain_local, my_shard)
+    gain_rows = (gain_mine + swap_shards(gain_theirs)).astype(low_type).reshape(-1)
+    gain_rows = jnp.pad(gain_rows, (0, 128 * 128 - gain_rows.shape[0])).reshape(128, 128)
+    grad_attn_owned = jnp.concatenate(
         [
-            lax.all_gather(piece, "dp", axis=0, tiled=True).reshape(-1)
-            for piece in (attn_piece, pair_piece, down_piece)
-        ]
-    ).astype(jnp.float32)
-    step_rates = owner_rates(shard_count, longest)
-    new_first, new_second, new_params = adamw_step(
-        params, owned_grad, first_moment, second_moment, step_rates, decay_coef
-    )
+            grad_qkv[:, :QD].reshape(-1, 128),
+            grad_qkv[:, QD : QD + KD].reshape(-1, 128),
+            grad_qkv[:, QD + KD :].reshape(-1, 128),
+            grad_out.reshape(-1, 128),
+            gain_rows,
+        ],
+        axis=0,
+    )
+    down_sum = gather_steps(scatter_steps(down_part, 4, replica_count))
+    gate_sum = gather_steps(scatter_steps(gate_part, 2, replica_count))
+    up_sum = gather_steps(scatter_steps(grad_up, 1, replica_count))
+    attn_sum = gather_steps(scatter_steps(grad_attn_owned, 1, replica_count))
+    gain_owned = attn_sum[9600:9608].reshape(-1)[: 2 * (D // shard_count)]
+    gain_owned = gain_owned.reshape(2, -1).astype(jnp.float32)
+    rates = matrix_rates(longest)
+    state = [values.reshape(-1, 128) for values in (params, first_moment, second_moment)]
+    updated = update_chunk(state, down_sum, 3, (rates[6], rates[6]), 0, ())
+    updated = update_chunk(state, gate_sum, 1, (rates[4], rates[4]), 0, updated)
+    updated = update_chunk(state, up_sum, 2, (rates[5], rates[5]), 0, updated)
+    updated = update_chunk(state, attn_sum, 0, (rates[0], rates[3]), 5, updated)
+    owned_grad, new_first, new_second, new_params = [values.reshape(-1) for values in updated]
     new_gain_first, new_gain_second, new_gains = adamw_step(
         norm_gains, gain_owned, gain_first, gain_second, gain_rate, 0.0
     )

time: 694 us -> 586 us (0.84)
  waiting for transfers between devices: 304 us -> 193 us
  Pallas kernels: 0 us -> 56 us
  blocking collectives: 40.2 us -> 0 us
  starting transfers between devices: 24.6 us -> 43.5 us
  matrix products: 83.7 us -> 70.4 us
  between operations: 15.5 us -> 2.57 us
  other arithmetic: 107 us -> 97.8 us
    ppermute x12 -> x44, waiting for transfers between devices: 17.5 us -> 130 us  [swap_replicas(): lax.ppermute(values, 'dp', [(index, index ^ distance) for index in range(...]
    all_gather x3 -> x0, waiting for transfers between devices: 89.1 us -> none  [body(): lax.all_gather(piece, 'dp', axis=0, tiled=True).reshape(-1)]
    reduce_scatter x1 -> x0, waiting for transfers between devices: 76.8 us -> none  [scatter_replicas(): return lax.psum_scatter(flat, 'dp', scatter_dimension=0, tiled=True)]
    sub x2 -> x1, other arithmetic: 60.1 us -> 0.62 us  [adamw_step(): weight - step_rates * (first_hat / (jnp.sqrt(second_hat) + adam_eps) + de...]
    pallas_call x0 -> x4, Pallas kernels: none -> 56 us  [update_chunk(): pl.pallas_call(lambda *refs: update_kernel(rates[0], rates[1], split, *re...]
    psum x1 -> x0, blocking collectives: 40.2 us -> none  [body(): gain_all = lax.psum(jnp.stack([gain_grad_one, gain_grad_two]), ('dp', 'cp'))]
    select_n x1 -> x17, other arithmetic: 0.08 us -> 40 us  [in_order(): jnp.where(my_shard == 0, jnp.concatenate([mine, theirs], axis=axis), jnp....]
    unnamed x8 -> x0, waiting for transfers between devices: 36.6 us -> none
  transfers between devices with their start and end apart: 33 -> 61, of which waited for: 11 -> 24; matrix products, arithmetic and copies ran while one was open for 34% -> 46% of each run, Pallas kernels for 0% -> 7%
where the time goes in v2:
time: 586 us; the launch traced here: 575 us
  waiting for transfers between devices  193 us (33%)
  local copies, waits for them, and re-layouts  112 us (19%)
  other arithmetic  97.8 us (17%)
  matrix products  70.4 us (12%)
  Pallas kernels  56 us (10%)
  starting transfers between devices  43.5 us (7%)
    ppermute x44, waiting for transfers between devices, swap_replicas(): lax.ppermute(values, 'dp', [(index, index ^ distance) for index in range(...  130 us
    ppermute x17, waiting for transfers between devices, swap_shards(): return lax.ppermute(values, 'cp', [(0, 1), (1, 0)])  62.9 us
    pallas_call x4, Pallas kernels, update_chunk(): pl.pallas_call(lambda *refs: update_kernel(rates[0], rates[1], split, *re...  56 us
    select_n x17, other arithmetic, in_order(): jnp.where(my_shard == 0, jnp.concatenate([mine, theirs], axis=axis), jnp....  40 us
    ppermute x44, starting transfers between devices, swap_replicas(): lax.ppermute(values, 'dp', [(index, index ^ distance) for index in range(...  24.5 us
    convert_element_type x7, local copies, waits for them, and re-layouts, gather_rows(): params[offset:offset + rows * width].astype(low_type)  22.6 us
    concatenate x4, other arithmetic, gather_rows(): whole = jnp.concatenate([mine, mine], axis=0)  19.8 us
    ppermute x17, starting transfers between devices, swap_shards(): return lax.ppermute(values, 'cp', [(0, 1), (1, 0)])  19 us
  transfers between devices with their start and end apart: 61, of which 24 were waited for; matrix products, arithmetic and copies ran while one was open for 46% of the time, Pallas kernels for 7%

profile of v2, /device:TPU:0, one launch (start us, length us, event | category | flops | bytes accessed | tf_op | source)
XLA Modules:
  0.0 575.3 jit_solution(13536019201014344499)
XLA Ops:
  18.8 7.4 %convert.63 = bf16[4915200]{0:T(1024)(128)(2,1)S(1)} convert(f32[4915200]{0:T(1024)} %param.14) | non-fusion elementwise | flops 4915200 | bytes 29491200 | tf_op jit(solution)/shard_map/convert.38
  73.9 10.0 %maximum_maximum_fusion = bf16[8,120,5120]{2,1,0:T(8,128)(2,1)} fusion(bf16[4,120,2560]{2,1,0:T(8,128)(2,1)} %convert_element_type.461, bf16[4,120,2560]{2,1,0:T(8,128)(2,1)} %convert_element_type.460), kind=kLoop, calls=%fused_computation | loop fusion | flops 39321600 | bytes 14745600 | tf_op jit(solution)/shard_map/concatenate | solution.py:181
  113.1 7.9 %collective-permute-done.17 = bf16[1,320,960]{2,1,0:T(8,128)(2,1)S(1)} collective-permute-done((bf16[1,320,960]{2,1,0:T(8,128)(2,1)S(1)}, bf16[1,320,960]{2,1,0:T(8,128)(2,1)S(1)}, u32[]{:S(2)}, u32[]{:S(2)}) %collective-permute-start.17) | collective-permute-done | bytes 614432 | tf_op jit(solution)/shard_map/ppermute | solution.py:136
  135.9 13.9 %collective-permute-done.13 = bf16[1,120,5120]{2,1,0:T(8,128)(2,1)S(1)} collective-permute-done((bf16[1,120,5120]{2,1,0:T(8,128)(2,1)}, bf16[1,120,5120]{2,1,0:T(8,128)(2,1)S(1)}, u32[]{:S(2)}, u32[]{:S(2)}) %collective-permute-start.13) | collective-permute-done | bytes 1228832 | tf_op jit(solution)/shard_map/ppermute | solution.py:136
  156.0 7.3 %fusion.2 = (bf16[256,2560]{1,0:T(8,128)(2,1)}, bf16[256,2560]{1,0:T(8,128)(2,1)}, bf16[256,2560]{1,0:T(8,128)(2,1)}) fusion(f32[256,5120]{1,0:T(8,128)S(1)} %fusion.145, bf16[2560,960]{1,0:T(8,128)(2,1)} %bitcast.465, bf16[256,960]{0,1:T(8,128)(2,1)} %param.11), kind=kOutput, calls=%fused_computation.11 | convolution fusion | flops 1268776960 | bytes 14581760 | tf_op jit(solution)/shard_map/dot_general | solution.py:353
  177.9 58.5 %collective-permute-done.22 = bf16[256,1280]{1,0:T(8,128)(2,1)S(1)} collective-permute-done((bf16[256,1280]{1,0:T(8,128)(2,1)S(1)}, bf16[256,1280]{1,0:T(8,128)(2,1)S(1)}, u32[]{:S(2)}, u32[]{:S(2)}) %collective-permute-start.22) | collective-permute-done | bytes 655392 | tf_op jit(solution)/shard_map/ppermute | solution.py:132
  294.5 13.3 %collective-permute-done.25 = bf16[2400,128]{1,0:T(8,128)(2,1)S(1)} collective-permute-done((bf16[2400,128]{1,0:T(8,128)(2,1)S(1)}, bf16[2400,128]{1,0:T(8,128)(2,1)S(1)}, u32[]{:S(2)}, u32[]{:S(2)}) %collective-permute-start.25) | collective-permute-done | bytes 614432 | tf_op jit(solution)/shard_map/ppermute | solution.py:136
  319.8 6.9 %collective-permute-done.55 = bf16[1200,128]{1,0:T(8,128)(2,1)S(1)} collective-permute-done((bf16[1200,128]{1,0:T(8,128)(2,1)S(1)}, bf16[1200,128]{1,0:T(8,128)(2,1)S(1)}, u32[]{:S(2)}, u32[]{:S(2)}) %collective-permute-start.55) | collective-permute-done | bytes 307232 | tf_op jit(solution)/shard_map/ppermute | solution.py:136
  335.8 8.8 %collective-permute-done.57 = bf16[600,128]{1,0:T(8,128)(2,1)S(1)} collective-permute-done((bf16[600,128]{1,0:T(8,128)(2,1)S(1)}, bf16[600,128]{1,0:T(8,128)(2,1)S(1)}, u32[]{:S(2)}, u32[]{:S(2)}) %collective-permute-start.57) | collective-permute-done | bytes 153632 | tf_op jit(solution)/shard_map/ppermute | solution.py:136
  345.8 7.1 %collective-permute-done.58 = bf16[1200,128]{1,0:T(8,128)(2,1)S(1)} collective-permute-done((bf16[1200,128]{1,0:T(8,128)(2,1)S(1)}, bf16[1200,128]{1,0:T(8,128)(2,1)S(1)}, u32[]{:S(2)}, u32[]{:S(2)}) %collective-permute-start.58) | collective-permute-done | bytes 307232 | tf_op jit(solution)/shard_map/ppermute | solution.py:136
  378.3 8.3 %collective-permute-done.48 = bf16[2400,128]{1,0:T(8,128)(2,1)} collective-permute-done((bf16[2400,128]{1,0:T(8,128)(2,1)}, bf16[2400,128]{1,0:T(8,128)(2,1)}, u32[]{:S(2)}, u32[]{:S(2)}) %collective-permute-start.48) | collective-permute-done | bytes 614432 | tf_op jit(solution)/shard_map/ppermute | solution.py:136
  420.7 9.2 %collective-permute-done.41 = bf16[2400,128]{1,0:T(8,128)(2,1)S(1)} collective-permute-done((bf16[2400,128]{1,0:T(8,128)(2,1)S(1)}, bf16[2400,128]{1,0:T(8,128)(2,1)S(1)}, u32[]{:S(2)}, u32[]{:S(2)}) %collective-permute-start.41) | collective-permute-done | bytes 614432 | tf_op jit(solution)/shard_map/ppermute | solution.py:136
  433.6 6.8 %collective-permute-done.42 = bf16[1200,128]{1,0:T(8,128)(2,1)S(1)} collective-permute-done((bf16[1200,128]{1,0:T(8,128)(2,1)S(1)}, bf16[1200,128]{1,0:T(8,128)(2,1)S(1)}, u32[]{:S(2)}, u32[]{:S(2)}) %collective-permute-start.42) | collective-permute-done | bytes 307232 | tf_op jit(solution)/shard_map/ppermute | solution.py:136
  450.7 7.9 %collective-permute-done.34 = bf16[1216,128]{1,0:T(8,128)(2,1)S(1)} collective-permute-done((bf16[1216,128]{1,0:T(8,128)(2,1)S(1)}, bf16[1216,128]{1,0:T(8,128)(2,1)S(1)}, u32[]{:S(2)}, u32[]{:S(2)}) %collective-permute-start.34) | collective-permute-done | bytes 311328 | tf_op jit(solution)/shard_map/ppermute | solution.py:136
  467.1 7.3 %collective-permute-done.36 = bf16[608,128]{1,0:T(8,128)(2,1)S(1)} collective-permute-done((bf16[608,128]{1,0:T(8,128)(2,1)S(1)}, bf16[608,128]{1,0:T(8,128)(2,1)S(1)}, u32[]{:S(2)}, u32[]{:S(2)}) %collective-permute-start.36) | collective-permute-done | bytes 155680 | tf_op jit(solution)/shard_map/ppermute | solution.py:136
  475.1 6.4 %collective-permute-done.37 = bf16[1216,128]{1,0:T(8,128)(2,1)S(1)} collective-permute-done((bf16[1216,128]{1,0:T(8,128)(2,1)S(1)}, bf16[1216,128]{1,0:T(8,128)(2,1)S(1)}, u32[]{:S(2)}, u32[]{:S(2)}) %collective-permute-start.37) | collective-permute-done | bytes 311328 | tf_op jit(solution)/shard_map/ppermute | solution.py:136
  482.0 9.0 %maximum_select_fusion.3.refs_3_ = bf16[9600,128]{1,0:T(8,128)(2,1)S(1)} fusion(bf16[4800,128]{1,0:T(8,128)(2,1)S(1)} %collective-permute-done.60, bf16[4800,128]{1,0:T(8,128)(2,1)S(1)} %maximum_select_fusion.7, pred[]{:T(512)S(6)} %eq.111), kind=kLoop, calls=%fused_computation.28 | loop fusion | flops 11059200 | bytes 4915201 | tf_op jit(solution)/shard_map/jit(_where)/select_n | solution.py:142
  490.9 14.0 %shard_map.177 = (f32[38400,128]{1,0:T(8,128)}, f32[38400,128]{1,0:T(8,128)}, f32[38400,128]{1,0:T(8,128)}, f32[38400,128]{1,0:T(8,128)}) custom-call(f32[38400,128]{1,0:T(8,128)} %bitcast.447, f32[38400,128]{1,0:T(8,128)} %bitcast.451, f32[38400,128]{1,0:T(8,128)} %bitcast.455, bf16[9600,128]{1,0:T(8,128)(2,1)S(1)} %maximum_select_fusion.3.refs_3_), custom_call_target="tpu_custom_call" | custom-call | flops 24576000 | bytes 36864000 | tf_op jit(solution)/shard_map/pallas_call | solution.py:247
  506.3 8.6 %maximum_select_fusion.2.refs_3_ = bf16[9600,128]{1,0:T(8,128)(2,1)S(1)} fusion(bf16[4800,128]{1,0:T(8,128)(2,1)S(1)} %collective-permute-done.54, bf16[4800,128]{1,0:T(8,128)(2,1)S(1)} %maximum_select_fusion.6, pred[]{:T(512)S(6)} %eq.111), kind=kLoop, calls=%fused_computation.27 | loop fusion | flops 11059200 | bytes 4915201 | tf_op jit(solution)/shard_map/jit(_where)/select_n | solution.py:142
  514.8 14.0 %shard_map.178 = (f32[38400,128]{1,0:T(8,128)}, f32[38400,128]{1,0:T(8,128)}, f32[38400,128]{1,0:T(8,128)}, f32[38400,128]{1,0:T(8,128)}) custom-call(f32[38400,128]{1,0:T(8,128)} %bitcast.448, f32[38400,128]{1,0:T(8,128)} %bitcast.452, f32[38400,128]{1,0:T(8,128)} %bitcast.456, ...), custom_call_target="tpu_custom_call", output_to_operand_aliasing={{0}: (4, {}), {1}: (5, {}), {2}: (6, {}), {3}: (7, {})} | custom-call | flops 24576000 | bytes 36864000 | tf_op jit(solution)/shard_map/pallas_call | solution.py:247
  528.9 8.8 %maximum_select_fusion.1.refs_3_ = bf16[9600,128]{1,0:T(8,128)(2,1)S(1)} fusion(bf16[4800,128]{1,0:T(8,128)(2,1)S(1)} %collective-permute-done.47, bf16[4800,128]{1,0:T(8,128)(2,1)S(1)} %maximum_select_fusion.5, pred[]{:T(512)S(6)} %eq.111), kind=kLoop, calls=%fused_computation.26 | loop fusion | flops 11059200 | bytes 4915201 | tf_op jit(solution)/shard_map/jit(_where)/select_n | solution.py:142
  537.6 14.0 %shard_map.179 = (f32[38400,128]{1,0:T(8,128)}, f32[38400,128]{1,0:T(8,128)}, f32[38400,128]{1,0:T(8,128)}, f32[38400,128]{1,0:T(8,128)}) custom-call(f32[38400,128]{1,0:T(8,128)} %bitcast.449, f32[38400,128]{1,0:T(8,128)} %bitcast.453, f32[38400,128]{1,0:T(8,128)} %bitcast.457, ...), custom_call_target="tpu_custom_call", output_to_operand_aliasing={{0}: (4, {}), {1}: (5, {}), {2}: (6, {}), {3}: (7, {})} | custom-call | flops 24576000 | bytes 36864000 | tf_op jit(solution)/shard_map/pallas_call | solution.py:247
  551.7 8.7 %maximum_select_fusion.refs_3_ = bf16[9728,128]{1,0:T(8,128)(2,1)S(1)} fusion(bf16[4864,128]{1,0:T(8,128)(2,1)S(1)} %collective-permute-done.39, bf16[4864,128]{1,0:T(8,128)(2,1)S(1)} %maximum_select_fusion.4, pred[]{:T(512)S(6)} %eq.111), kind=kLoop, calls=%fused_computation.23 | loop fusion | flops 11206656 | bytes 4980737 | tf_op jit(solution)/shard_map/jit(_where)/select_n | solution.py:142
  561.2 14.0 %shard_map.180 = (f32[38400,128]{1,0:T(8,128)}, f32[38400,128]{1,0:T(8,128)}, f32[38400,128]{1,0:T(8,128)}, f32[38400,128]{1,0:T(8,128)}) custom-call(f32[38400,128]{1,0:T(8,128)} %bitcast.450, f32[38400,128]{1,0:T(8,128)} %bitcast.454, f32[38400,128]{1,0:T(8,128)} %bitcast.458, ...), custom_call_target="tpu_custom_call", output_to_operand_aliasing={{0}: (4, {}), {1}: (5, {}), {2}: (6, {}), {3}: (7, {})} | custom-call | flops 24576000 | bytes 36864000 | tf_op jit(solution)/shard_map/pallas_call | solution.py:247
  (478 shorter events, 294.9 us)
Async XLA Ops:
  1.3 83.2 %collective-permute-start = (bf16[2,480]{1,0:T(2,128)(2,1)S(1)}, bf16[2,480]{1,0:T(2,128)(2,1)S(1)}, u32[]{:S(2)}, u32[]{:S(2)}) collective-permute-start(bf16[2,480]{1,0:T(2,128)(2,1)S(1)} %convert_element_type.426), channel_id=1, source_target_pairs={{0,1},{1,0},{2,3},{3,2},{4,5},{5,4},{6,7},{7,6},{8,9},{9,8},{10,11... | collective-permute-start | bytes 5768 | tf_op jit(solution)/shard_map/ppermute | solution.py:132
  8.3 81.1 %collective-permute-start.1 = (bf16[1,120,1600]{2,1,0:T(8,128)(2,1)}, bf16[1,120,1600]{2,1,0:T(8,128)(2,1)}, u32[]{:S(2)}, u32[]{:S(2)}) collective-permute-start(bf16[1,120,1600]{2,1,0:T(8,128)(2,1)} %concatenate.206), channel_id=1, source_target_pairs={{0,1},{1,0},{2,3},{3,2},{4,5},{5,4},{6,7},{7,6},{8,9},{9,8},{10,11... | collective-permute-start | bytes 1152008 | tf_op jit(solution)/shard_map/ppermute | solution.py:132
  8.3 122.1 %collective-permute-start.7 = (bf16[256,960]{0,1:T(8,128)(2,1)}, bf16[256,960]{0,1:T(8,128)(2,1)}, u32[]{:S(2)}, u32[]{:S(2)}) collective-permute-start(bf16[256,960]{0,1:T(8,128)(2,1)} %param.11), channel_id=1, source_target_pairs={{0,1},{1,0},{2,3},{3,2},{4,5},{5,4},{6,7},{7,6},{8,9},{9,8},{10,11... | collective-permute-start | bytes 1474568 | tf_op jit(solution)/shard_map/ppermute | solution.py:132
  11.2 74.4 %collective-permute-start.8 = (bf16[1,120,960]{2,1,0:T(8,128)(2,1)}, bf16[1,120,960]{2,1,0:T(8,128)(2,1)}, u32[]{:S(2)}, u32[]{:S(2)}) collective-permute-start(bf16[1,120,960]{2,1,0:T(8,128)(2,1)} %reshape.515), channel_id=1, source_target_pairs={{0,1},{1,0},{2,3},{3,2},{4,5},{5,4},{6,7},{7,6},{8,9},{9,8},{10,11... | collective-permute-start | bytes 691208 | tf_op jit(solution)/shard_map/ppermute | solution.py:132
  16.8 93.0 %collective-permute-start.12 = (bf16[1,120,5120]{2,1,0:T(8,128)(2,1)}, bf16[1,120,5120]{2,1,0:T(8,128)(2,1)}, u32[]{:S(2)}, u32[]{:S(2)}) collective-permute-start(bf16[1,120,5120]{2,1,0:T(8,128)(2,1)} %pad_maximum_fusion.4), channel_id=1, source_target_pairs={{0,1},{1,0},{2,3},{3,2},{4,5},{5,4},{6,7},{7,6},{8,9},{9,8},{10,11... | collective-permute-start | bytes 3686408 | tf_op jit(solution)/shard_map/ppermute | solution.py:132
  100.5 29.8 %collective-permute-start.6 = (bf16[256,480]{0,1:T(8,128)(2,1)S(1)}, bf16[256,480]{0,1:T(8,128)(2,1)S(1)}, u32[]{:S(2)}, u32[]{:S(2)}) collective-permute-start(bf16[256,480]{0,1:T(8,128)(2,1)S(1)} %get-tuple-element.113), channel_id=1, source_target_pairs={{0,1},{1,0},{2,3},{3,2},{4,5},{5,4},{6,7},{7,6},{8,9},{9,8},{10,11... | collective-permute-start | bytes 737288 | tf_op jit(solution)/shard_map/ppermute | solution.py:132
  121.0 28.9 %collective-permute-start.13 = (bf16[1,120,5120]{2,1,0:T(8,128)(2,1)}, bf16[1,120,5120]{2,1,0:T(8,128)(2,1)S(1)}, u32[]{:S(2)}, u32[]{:S(2)}) collective-permute-start(bf16[1,120,5120]{2,1,0:T(8,128)(2,1)} %collective-permute-done.12), channel_id=1, source_target_pairs={{0,4},{2,6},{4,0},{6,2},{8,12},{10,14},{12,8},{14,10},{16,20},{18,... | collective-permute-start | bytes 3686408 | tf_op jit(solution)/shard_map/ppermute | solution.py:136
  122.1 28.7 %collective-permute-start.14 = (bf16[1,120,5120]{2,1,0:T(8,128)(2,1)}, bf16[1,120,5120]{2,1,0:T(8,128)(2,1)S(1)}, u32[]{:S(2)}, u32[]{:S(2)}) collective-permute-start(bf16[1,120,5120]{2,1,0:T(8,128)(2,1)} %collective-permute-done.12), channel_id=1, source_target_pairs={{0,2},{2,0},{4,6},{6,4},{8,10},{10,8},{12,14},{14,12},{16,18},{18,... | collective-permute-start | bytes 3686408 | tf_op jit(solution)/shard_map/ppermute | solution.py:136
  123.0 26.8 %collective-permute-start.19 = (bf16[1,320,960]{2,1,0:T(8,128)(2,1)S(1)}, bf16[1,320,960]{2,1,0:T(8,128)(2,1)S(1)}, u32[]{:S(2)}, u32[]{:S(2)}) collective-permute-start(bf16[1,320,960]{2,1,0:T(8,128)(2,1)S(1)} %collective-permute-done.17), channel_id=1, source_target_pairs={{0,2},{2,0},{4,6},{6,4},{8,10},{10,8},{12,14},{14,12},{16,18},{18,... | collective-permute-start | bytes 1843208 | tf_op jit(solution)/shard_map/ppermute | solution.py:136
  132.8 34.7 %collective-permute-start.20 = (bf16[256,480]{0,1:T(8,128)(2,1)}, bf16[256,480]{0,1:T(8,128)(2,1)}, u32[]{:S(2)}, u32[]{:S(2)}) collective-permute-start(bf16[256,480]{0,1:T(8,128)(2,1)} %get-tuple-element.111), channel_id=1, source_target_pairs={{0,1},{1,0},{2,3},{3,2},{4,5},{5,4},{6,7},{7,6},{8,9},{9,8},{10,11... | collective-permute-start | bytes 737288 | tf_op jit(solution)/shard_map/ppermute | solution.py:132
  135.6 31.9 %collective-permute-start.21 = (bf16[256,480]{0,1:T(8,128)(2,1)}, bf16[256,480]{0,1:T(8,128)(2,1)}, u32[]{:S(2)}, u32[]{:S(2)}) collective-permute-start(bf16[256,480]{0,1:T(8,128)(2,1)} %get-tuple-element.115), channel_id=1, source_target_pairs={{0,1},{1,0},{2,3},{3,2},{4,5},{5,4},{6,7},{7,6},{8,9},{9,8},{10,11... | collective-permute-start | bytes 737288 | tf_op jit(solution)/shard_map/ppermute | solution.py:132
  163.3 144.7 %collective-permute-start.24 = (bf16[256,2560]{1,0:T(8,128)(2,1)}, bf16[256,2560]{1,0:T(8,128)(2,1)}, u32[]{:S(2)}, u32[]{:S(2)}) collective-permute-start(bf16[256,2560]{1,0:T(8,128)(2,1)} %get-tuple-element.97), channel_id=1, source_target_pairs={{0,1},{1,0},{2,3},{3,2},{4,5},{5,4},{6,7},{7,6},{8,9},{9,8},{10,11... | collective-permute-start | bytes 3932168 | tf_op jit(solution)/shard_map/ppermute | solution.py:132
  166.9 188.6 %collective-permute-start.27 = (bf16[256,2560]{1,0:T(8,128)(2,1)}, bf16[256,2560]{1,0:T(8,128)(2,1)}, u32[]{:S(2)}, u32[]{:S(2)}) collective-permute-start(bf16[256,2560]{1,0:T(8,128)(2,1)} %get-tuple-element.98), channel_id=1, source_target_pairs={{0,1},{1,0},{2,3},{3,2},{4,5},{5,4},{6,7},{7,6},{8,9},{9,8},{10,11... | collective-permute-start | bytes 3932168 | tf_op jit(solution)/shard_map/ppermute | solution.py:132
  171.1 65.3 %collective-permute-start.22 = (bf16[256,1280]{1,0:T(8,128)(2,1)S(1)}, bf16[256,1280]{1,0:T(8,128)(2,1)S(1)}, u32[]{:S(2)}, u32[]{:S(2)}) collective-permute-start(bf16[256,1280]{1,0:T(8,128)(2,1)S(1)} %get-tuple-element.103), channel_id=1, source_target_pairs={{0,1},{1,0},{2,3},{3,2},{4,5},{5,4},{6,7},{7,6},{8,9},{9,8},{10,11... | collective-permute-start | bytes 1966088 | tf_op jit(solution)/shard_map/ppermute | solution.py:132
  240.9 35.3 %collective-permute-start.30 = (bf16[256,960]{0,1:T(8,128)(2,1)}, bf16[256,960]{0,1:T(8,128)(2,1)}, u32[]{:S(2)}, u32[]{:S(2)}) collective-permute-start(bf16[256,960]{0,1:T(8,128)(2,1)} %fusion.127), channel_id=1, source_target_pairs={{0,1},{1,0},{2,3},{3,2},{4,5},{5,4},{6,7},{7,6},{8,9},{9,8},{10,11... | collective-permute-start | bytes 1474568 | tf_op jit(solution)/shard_map/ppermute | solution.py:132
  319.7 34.4 %collective-permute-start.28 = (bf16[4800,128]{1,0:T(8,128)(2,1)S(1)}, bf16[4800,128]{1,0:T(8,128)(2,1)S(1)}, u32[]{:S(2)}, u32[]{:S(2)}) collective-permute-start(bf16[4800,128]{1,0:T(8,128)(2,1)S(1)} %dynamic-slice_bitcast_fusion.2), channel_id=1, source_target_pairs={{0,2},{2,0},{4,6},{6,4},{8,10},{10,8},{12,14},{14,12},{16,18},{18,... | collective-permute-start | bytes 3686408 | tf_op jit(solution)/shard_map/ppermute | solution.py:136
  353.9 60.8 %collective-permute-start.59 = (bf16[2400,128]{1,0:T(8,128)(2,1)}, bf16[2400,128]{1,0:T(8,128)(2,1)}, u32[]{:S(2)}, u32[]{:S(2)}) collective-permute-start(bf16[2400,128]{1,0:T(8,128)(2,1)} %maximum_select_fusion.11), channel_id=1, source_target_pairs={{0,4},{2,6},{4,0},{6,2},{8,12},{10,14},{12,8},{14,10},{16,20},{18,... | collective-permute-start | bytes 1843208 | tf_op jit(solution)/shard_map/ppermute | solution.py:136
  359.6 30.6 %collective-permute-start.29 = (bf16[256,1600]{0,1:T(8,128)(2,1)}, bf16[256,1600]{0,1:T(8,128)(2,1)}, u32[]{:S(2)}, u32[]{:S(2)}) collective-permute-start(bf16[256,1600]{0,1:T(8,128)(2,1)} %pad_maximum_fusion.5), channel_id=1, source_target_pairs={{0,1},{1,0},{2,3},{3,2},{4,5},{5,4},{6,7},{7,6},{8,9},{9,8},{10,11... | collective-permute-start | bytes 2457608 | tf_op jit(solution)/shard_map/ppermute | solution.py:132
  375.2 37.0 %collective-permute-start.40 = (bf16[4800,128]{1,0:T(8,128)(2,1)}, bf16[4800,128]{1,0:T(8,128)(2,1)}, u32[]{:S(2)}, u32[]{:S(2)}) collective-permute-start(bf16[4800,128]{1,0:T(8,128)(2,1)} %dynamic-slice_bitcast_fusion.1), channel_id=1, source_target_pairs={{0,2},{2,0},{4,6},{6,4},{8,10},{10,8},{12,14},{14,12},{16,18},{18,... | collective-permute-start | bytes 3686408 | tf_op jit(solution)/shard_map/ppermute | solution.py:136
  416.8 65.2 %collective-permute-start.60 = (bf16[4800,128]{1,0:T(8,128)(2,1)S(1)}, bf16[4800,128]{1,0:T(8,128)(2,1)S(1)}, u32[]{:S(2)}, u32[]{:S(2)}) collective-permute-start(bf16[4800,128]{1,0:T(8,128)(2,1)S(1)} %maximum_select_fusion.7), channel_id=1, source_target_pairs={{0,2},{2,0},{4,6},{6,4},{8,10},{10,8},{12,14},{14,12},{16,18},{18,... | collective-permute-start | bytes 3686408 | tf_op jit(solution)/shard_map/ppermute | solution.py:136
  467.0 39.2 %collective-permute-start.54 = (bf16[4800,128]{1,0:T(8,128)(2,1)S(1)}, bf16[4800,128]{1,0:T(8,128)(2,1)S(1)}, u32[]{:S(2)}, u32[]{:S(2)}) collective-permute-start(bf16[4800,128]{1,0:T(8,128)(2,1)S(1)} %maximum_select_fusion.6), channel_id=1, source_target_pairs={{0,2},{2,0},{4,6},{6,4},{8,10},{10,8},{12,14},{14,12},{16,18},{18,... | collective-permute-start | bytes 3686408 | tf_op jit(solution)/shard_map/ppermute | solution.py:136
  474.7 30.2 %collective-permute-start.46 = (bf16[2400,128]{1,0:T(8,128)(2,1)S(1)}, bf16[2400,128]{1,0:T(8,128)(2,1)S(1)}, u32[]{:S(2)}, u32[]{:S(2)}) collective-permute-start(bf16[2400,128]{1,0:T(8,128)(2,1)S(1)} %maximum_select_fusion.9), channel_id=1, source_target_pairs={{0,4},{2,6},{4,0},{6,2},{8,12},{10,14},{12,8},{14,10},{16,20},{18,... | collective-permute-start | bytes 1843208 | tf_op jit(solution)/shard_map/ppermute | solution.py:136
  481.6 23.7 %collective-permute-start.38 = (bf16[2432,128]{1,0:T(8,128)(2,1)S(1)}, bf16[2432,128]{1,0:T(8,128)(2,1)S(1)}, u32[]{:S(2)}, u32[]{:S(2)}) collective-permute-start(bf16[2432,128]{1,0:T(8,128)(2,1)S(1)} %maximum_select_fusion.8), channel_id=1, source_target_pairs={{0,4},{2,6},{4,0},{6,2},{8,12},{10,14},{12,8},{14,10},{16,20},{18,... | collective-permute-start | bytes 1867784 | tf_op jit(solution)/shard_map/ppermute | solution.py:136
  505.7 46.0 %collective-permute-start.39 = (bf16[4864,128]{1,0:T(8,128)(2,1)S(1)}, bf16[4864,128]{1,0:T(8,128)(2,1)S(1)}, u32[]{:S(2)}, u32[]{:S(2)}) collective-permute-start(bf16[4864,128]{1,0:T(8,128)(2,1)S(1)} %maximum_select_fusion.4), channel_id=1, source_target_pairs={{0,2},{2,0},{4,6},{6,4},{8,10},{10,8},{12,14},{14,12},{16,18},{18,... | collective-permute-start | bytes 3735560 | tf_op jit(solution)/shard_map/ppermute | solution.py:136
  (112 other events, 1715.8 us)

commit v3 on v2

--- a/solution.py
+++ b/solution.py
@@ -152,32 +152,32 @@
     return (jnp.where(my_shard == 0, lower, upper), jnp.where(my_shard == 0, upper, lower))
 
 
-def gather_rows(params, columns):
+def fetch_quarter(params, columns):
+    quarter = lax.axis_index("dp") % 4
+    pieces = [
+        lax.dynamic_slice_in_dim(
+            params, offset + quarter * (rows // 4 * width), rows // 4 * width
+        )
+        .astype(jnp.bfloat16)
+        .reshape(1, rows // 4, width)
+        for offset, rows, width in columns
+    ]
+    return swap_shards(jnp.concatenate(pieces, axis=2))
+
+
+def gather_rows(params, columns, fetched):
     my_shard = lax.axis_index("cp")
     quarter = lax.axis_index("dp") % 4
-    low_type = jnp.bfloat16
-
-    def piece_of(start, size):
-        return lax.dynamic_slice_in_dim(params, start, size).astype(low_type)
-
-    fetched = jnp.concatenate(
+    across = swap_replicas(fetched, 2)
+    mine = jnp.concatenate(
         [
-            piece_of(offset + quarter * (rows // 4 * width), rows // 4 * width).reshape(
-                1, rows // 4, width
-            )
+            params[offset : offset + rows * width]
+            .astype(jnp.bfloat16)
+            .reshape(4, rows // 4, width)
             for offset, rows, width in columns
         ],
         axis=2,
     )
-    fetched = swap_shards(fetched)
-    mine = jnp.concatenate(
-        [
-            params[offset : offset + rows * width].astype(low_type).reshape(4, rows // 4, width)
-            for offset, rows, width in columns
-        ],
-        axis=2,
-    )
-    across = swap_replicas(fetched, 2)
     whole = jnp.concatenate([mine, mine], axis=0)
     other = (1 - my_shard) * 4
     for piece, place in (
@@ -214,21 +214,24 @@
 
 def gather_steps(piece):
     distance = lax.axis_size("dp") // 2
-    while distance >= 1:
+    while distance >= 2:
         bit = (lax.axis_index("dp") // distance) % 2
         piece = in_order(piece, swap_replicas(piece, distance), bit, 0)
         distance //= 2
-    return piece
+    return (piece, swap_replicas(piece, 1))
 
 
 BLOCK = 1200
 CHUNK_BLOCKS = 8
 
 
-def update_kernel(first_rate, last_rate, split, *refs):
-    params_ref, first_ref, second_ref, grad_ref = refs[:4]
+def update_kernel(first_rate, last_rate, split, bit_ref, *refs):
+    params_ref, first_ref, second_ref, mine_ref, received_ref = refs[:5]
     grad_out, first_out, second_out, params_out = refs[-4:]
-    gradient = grad_ref[...].astype(jnp.float32)
+    own_half = pl.program_id(0) // (CHUNK_BLOCKS // 2) == bit_ref[0]
+    gradient = jnp.where(
+        own_half, mine_ref[...].astype(jnp.float32), received_ref[...].astype(jnp.float32)
+    )
     rate = jnp.where(pl.program_id(0) < split, first_rate, last_rate)
     grad_out[...] = gradient
     first_out[...], second_out[...], params_out[...] = adamw_step(
@@ -236,28 +239,31 @@
     )
 
 
-def update_chunk(state, gradient, chunk, rates, split, earlier):
+def update_chunk(state, halves, bit, chunk, rates, split, earlier):
     rows = state[0].shape[0]
 
     def state_block(i):
         return (chunk * CHUNK_BLOCKS + i, 0)
 
     spec = pl.BlockSpec((BLOCK, 128), state_block)
-    grad_spec = pl.BlockSpec((BLOCK, 128), lambda i: (i, 0))
+    half_spec = pl.BlockSpec((BLOCK, 128), lambda i: (i % (CHUNK_BLOCKS // 2), 0))
     return pl.pallas_call(
         lambda *refs: update_kernel(rates[0], rates[1], split, *refs),
         grid=(CHUNK_BLOCKS,),
-        in_specs=[spec] * 3 + [grad_spec] + [pl.BlockSpec(memory_space=pl.ANY)] * len(earlier),
+        in_specs=[pl.BlockSpec(memory_space=pltpu.SMEM)]
+        + [spec] * 3
+        + [half_spec] * 2
+        + [pl.BlockSpec(memory_space=pl.ANY)] * len(earlier),
         out_specs=[spec] * 4,
         out_shape=[jax.ShapeDtypeStruct((rows, 128), jnp.float32)] * 4,
-        input_output_aliases={4 + index: index for index in range(len(earlier))},
+        input_output_aliases={6 + index: index for index in range(len(earlier))},
         compiler_params=pltpu.CompilerParams(vmem_limit_bytes=40 * 1024 * 1024),
         cost_estimate=pl.CostEstimate(
             flops=20 * BLOCK * CHUNK_BLOCKS * 128,
-            bytes_accessed=30 * BLOCK * CHUNK_BLOCKS * 128,
+            bytes_accessed=32 * BLOCK * CHUNK_BLOCKS * 128,
             transcendentals=0,
         ),
-    )(*state, gradient, *earlier)
+    )(bit, *state, *halves, *earlier)
 
 
 def body(
@@ -287,10 +293,17 @@
         offset += row_count // shard_count * col_count
     gains_low = norm_gains.astype(low_type)
     gain_pair = in_order(gains_low, swap_shards(gains_low), my_shard, 1)
-    w_qkv = gather_rows(params, blocks[:3])
-    w_out = gather_rows(params, blocks[3:4])
-    w_pair = gather_rows(params, blocks[4:6])
-    w_down = gather_rows(params, blocks[6:])
+    fetched = [
+        fetch_quarter(params, columns)
+        for columns in (blocks[:3], blocks[3:4], blocks[4:6], blocks[6:])
+    ]
+    w_qkv = gather_rows(params, blocks[:3], fetched[0])
+    held, fetched[0] = lax.optimization_barrier((params, fetched[0]))
+    w_out = gather_rows(held, blocks[3:4], fetched[1])
+    held, fetched[1] = lax.optimization_barrier((held, fetched[1]))
+    w_pair = gather_rows(held, blocks[4:6], fetched[2])
+    held, fetched[2] = lax.optimization_barrier((held, fetched[2]))
+    w_down = gather_rows(held, blocks[6:], fetched[3])
 
     out_peer = swap_shards(out_grad)
     segment_all, position_all = window_layout(lengths[0], slot_positions[0])
@@ -354,15 +367,16 @@
     grad_gate_act, grad_up_act = pull_act(grad_hidden)
     gate_back = grad_gate_act.astype(low_type)
     up_back = grad_up_act.astype(low_type)
-    gate_peer = swap_shards(gate_back)
-    up_peer = swap_shards(up_back)
     pair_back = jnp.concatenate([gate_back, up_back], axis=1)
     pair_back, attn_peer, two_peer = lax.optimization_barrier((pair_back, attn_peer, two_peer))
     grad_xn_two = jnp.dot(pair_back, w_pair.T, preferred_element_type=jnp.float32)
+    gate_sent, hidden_peer, grad_xn_two = lax.optimization_barrier(
+        (gate_back, hidden_peer, grad_xn_two)
+    )
+    gate_peer = swap_shards(gate_sent)
     back_two, gain_grad_two = pull_two(grad_xn_two)
     grad_resid = out_grad.astype(jnp.float32) + back_two
     resid_low = grad_resid.astype(low_type)
-    resid_low, hidden_peer = lax.optimization_barrier((resid_low, hidden_peer))
     resid_peer = swap_shards(resid_low)
     grad_down = owned_product(hidden_mine, hidden_peer, out_grad, out_peer).reshape(-1, 128)
     down_part = scatter_replicas(grad_down, 1)
@@ -372,8 +386,16 @@
     for group in range(KVH):
         grad_group = grad_groups[group]
         if group == 3:
-            grad_group, down_part = lax.optimization_barrier((grad_group, down_part))
+            earlier_group = backward_groups[2]
+            grad_group, down_part, earlier_group = lax.optimization_barrier(
+                (grad_group, down_part, earlier_group)
+            )
+            backward_groups[2] = earlier_group
             down_part = scatter_replicas(down_part, 2)
+            up_sent, gate_peer, grad_group = lax.optimization_barrier(
+                (up_back, gate_peer, grad_group)
+            )
+            up_peer = swap_shards(up_sent)
         backward_groups.append(
             group_backward(
                 (
@@ -421,13 +443,16 @@
     gain_mine, gain_theirs = split_columns(gain_local, my_shard)
     gain_rows = (gain_mine + swap_shards(gain_theirs)).astype(low_type).reshape(-1)
     gain_rows = jnp.pad(gain_rows, (0, 128 * 128 - gain_rows.shape[0])).reshape(128, 128)
+    half_rows = BLOCK * CHUNK_BLOCKS // 2
+    key_rows = grad_qkv[:, QD : QD + KD].reshape(-1, 128)
     grad_attn_owned = jnp.concatenate(
         [
             grad_qkv[:, :QD].reshape(-1, 128),
-            grad_qkv[:, QD : QD + KD].reshape(-1, 128),
+            key_rows,
+            gain_rows[:64],
             grad_qkv[:, QD + KD :].reshape(-1, 128),
             grad_out.reshape(-1, 128),
-            gain_rows,
+            gain_rows[64:],
         ],
         axis=0,
     )
@@ -435,14 +460,17 @@
     gate_sum = gather_steps(scatter_steps(gate_part, 2, replica_count))
     up_sum = gather_steps(scatter_steps(grad_up, 1, replica_count))
     attn_sum = gather_steps(scatter_steps(grad_attn_owned, 1, replica_count))
-    gain_owned = attn_sum[9600:9608].reshape(-1)[: 2 * (D // shard_count)]
+    core = lax.axis_index("dp") % 2
+    gain_sum = jnp.where(core == 0, attn_sum[0][half_rows:], attn_sum[1][half_rows:])
+    gain_owned = gain_sum[:8].reshape(-1)[: 2 * (D // shard_count)]
     gain_owned = gain_owned.reshape(2, -1).astype(jnp.float32)
     rates = matrix_rates(longest)
+    bit = core.reshape(1).astype(jnp.int32)
     state = [values.reshape(-1, 128) for values in (params, first_moment, second_moment)]
-    updated = update_chunk(state, down_sum, 3, (rates[6], rates[6]), 0, ())
-    updated = update_chunk(state, gate_sum, 1, (rates[4], rates[4]), 0, updated)
-    updated = update_chunk(state, up_sum, 2, (rates[5], rates[5]), 0, updated)
-    updated = update_chunk(state, attn_sum, 0, (rates[0], rates[3]), 5, updated)
+    updated = update_chunk(state, down_sum, bit, 3, (rates[6], rates[6]), 0, ())
+    updated = update_chunk(state, gate_sum, bit, 1, (rates[4], rates[4]), 0, updated)
+    updated = update_chunk(state, up_sum, bit, 2, (rates[5], rates[5]), 0, updated)
+    updated = update_chunk(state, attn_sum, bit, 0, (rates[0], rates[3]), 5, updated)
     owned_grad, new_first, new_second, new_params = [values.reshape(-1) for values in updated]
     new_gain_first, new_gain_second, new_gains = adamw_step(
         norm_gains, gain_owned, gain_first, gain_second, gain_rate, 0.0

time: 586 us -> 545 us (0.930)
  other arithmetic: 97.8 us -> 65.8 us
  starting transfers between devices: 43.5 us -> 57.9 us
  local copies, waits for them, and re-layouts: 112 us -> 99 us
  waiting for transfers between devices: 193 us -> 182 us
    select_n x17 -> x13, other arithmetic: 40 us -> 6.92 us  [in_order(): jnp.where(my_shard == 0, jnp.concatenate([mine, theirs], axis=axis), jnp....]
    ppermute x44, starting transfers between devices: 24.5 us -> 40.3 us  [swap_replicas(): lax.ppermute(values, 'dp', [(index, index ^ distance) for index in range(...]
    ppermute x17, waiting for transfers between devices: 62.9 us -> 51.9 us  [swap_shards(): return lax.ppermute(values, 'cp', [(0, 1), (1, 0)])]
    concatenate x4, other arithmetic: 19.8 us -> 9.88 us  [gather_rows(): whole = jnp.concatenate([mine, mine], axis=0)]
    another operation x6 -> x7, other arithmetic: 7.98 us -> 15.7 us
    unnamed x158 -> x178, local copies, waits for them, and re-layouts: 13.9 us -> 7.05 us
  transfers between devices with their start and end apart: 61 -> 61, of which waited for: 24 -> 24; matrix products, arithmetic and copies ran while one was open for 46% -> 40% of each run, Pallas kernels for 7% -> 9%
where the time goes in v3:
time: 545 us; the launch traced here: 539 us
  waiting for transfers between devices  182 us (33%)
  local copies, waits for them, and re-layouts  99 us (18%)
  matrix products  70.1 us (13%)
  other arithmetic  65.8 us (12%)
  Pallas kernels  61.4 us (11%)
  starting transfers between devices  57.9 us (11%)
    ppermute x44, waiting for transfers between devices, swap_replicas(): lax.ppermute(values, 'dp', [(index, index ^ distance) for index in range(...  130 us
    pallas_call x4, Pallas kernels, update_chunk(): pl.pallas_call(lambda *refs: update_kernel(rates[0], rates[1], split, *re...  61.4 us
    ppermute x17, waiting for transfers between devices, swap_shards(): return lax.ppermute(values, 'cp', [(0, 1), (1, 0)])  51.9 us
    ppermute x44, starting transfers between devices, swap_replicas(): lax.ppermute(values, 'dp', [(index, index ^ distance) for index in range(...  40.3 us
    dot_general x5, matrix products, owned_product(): jnp.dot(left.T, right, preferred_element_type=jnp.float32)  18.5 us
    convert_element_type x7, local copies, waits for them, and re-layouts, gather_rows(): mine = jnp.concatenate([params[offset:offset + rows * width].astype(jnp.b...  18.4 us
    ppermute x17, starting transfers between devices, swap_shards(): return lax.ppermute(values, 'cp', [(0, 1), (1, 0)])  17.6 us
    another operation x3, local copies, waits for them, and re-layouts, scatter_replicas(): halves = flat.reshape(2, flat.shape[0] // 2, flat.shape[1])  16.1 us
  transfers between devices with their start and end apart: 61, of which 24 were waited for; matrix products, arithmetic and copies ran while one was open for 40% of the time, Pallas kernels for 9%

profile of v3, /device:TPU:0, one launch (start us, length us, event | category | flops | bytes accessed | tf_op | source)
XLA Modules:
  0.0 539.3 jit_solution(771955996420522004)
XLA Ops:
  17.8 7.7 %convert.69 = bf16[4915200]{0:T(1024)(128)(2,1)S(1)} convert(f32[4915200]{0:T(1024)} %param.14) | non-fusion elementwise | flops 4915200 | bytes 29491200 | tf_op jit(solution)/shard_map/convert.38
  42.5 7.4 %convert.76 = bf16[4915200]{0:T(1024)(128)(2,1)S(1)} convert(f32[4915200]{0:T(1024)} %param.14) | non-fusion elementwise | flops 4915200 | bytes 29491200 | tf_op jit(solution)/shard_map/convert.27
  62.9 7.2 %maximum_maximum_fusion = bf16[8,120,5120]{2,1,0:T(8,128)(2,1)} fusion(bf16[4,120,2560]{2,1,0:T(8,128)(2,1)S(1)} %convert_element_type.461, bf16[4,120,2560]{2,1,0:T(8,128)(2,1)} %convert_element_type.460), kind=kLoop, calls=%fused_computation | loop fusion | flops 39321600 | bytes 14745600 | tf_op jit(solution)/shard_map/concatenate | solution.py:181
  88.2 17.3 %collective-permute-done.12 = bf16[1,120,5120]{2,1,0:T(8,128)(2,1)S(1)} collective-permute-done((bf16[1,120,5120]{2,1,0:T(8,128)(2,1)S(1)}, bf16[1,120,5120]{2,1,0:T(8,128)(2,1)S(1)}, u32[]{:S(2)}, u32[]{:S(2)}) %collective-permute-start.12) | collective-permute-done | bytes 1228832 | tf_op jit(solution)/shard_map/ppermute | solution.py:132
  135.6 9.2 %collective-permute-done.13 = bf16[1,120,5120]{2,1,0:T(8,128)(2,1)S(1)} collective-permute-done((bf16[1,120,5120]{2,1,0:T(8,128)(2,1)S(1)}, bf16[1,120,5120]{2,1,0:T(8,128)(2,1)S(1)}, u32[]{:S(2)}, u32[]{:S(2)}) %collective-permute-start.13) | collective-permute-done | bytes 1228832 | tf_op jit(solution)/shard_map/ppermute | solution.py:136
  168.0 8.5 %collective-permute-done.20 = bf16[256,1280]{1,0:T(8,128)(2,1)S(1)} collective-permute-done((bf16[256,1280]{1,0:T(8,128)(2,1)S(1)}, bf16[256,1280]{1,0:T(8,128)(2,1)S(1)}, u32[]{:S(2)}, u32[]{:S(2)}) %collective-permute-start.20) | collective-permute-done | bytes 655392 | tf_op jit(solution)/shard_map/ppermute | solution.py:132
  227.1 11.8 %collective-permute-done.24 = bf16[256,2560]{1,0:T(8,128)(2,1)} collective-permute-done((bf16[256,2560]{1,0:T(8,128)(2,1)}, bf16[256,2560]{1,0:T(8,128)(2,1)}, u32[]{:S(2)}, u32[]{:S(2)}) %collective-permute-start.24) | collective-permute-done | bytes 1310752 | tf_op jit(solution)/shard_map/ppermute | solution.py:132
  259.9 6.9 %collective-permute-done.55 = bf16[1200,128]{1,0:T(8,128)(2,1)S(1)} collective-permute-done((bf16[1200,128]{1,0:T(8,128)(2,1)S(1)}, bf16[1200,128]{1,0:T(8,128)(2,1)S(1)}, u32[]{:S(2)}, u32[]{:S(2)}) %collective-permute-start.55) | collective-permute-done | bytes 307232 | tf_op jit(solution)/shard_map/ppermute | solution.py:136
  269.5 13.0 %collective-permute-done.26 = bf16[256,640]{0,1:T(8,128)(2,1)} collective-permute-done((bf16[256,640]{0,1:T(8,128)(2,1)S(1)}, bf16[256,640]{0,1:T(8,128)(2,1)}, u32[]{:S(2)}, u32[]{:S(2)}) %collective-permute-start.26) | collective-permute-done | bytes 327712 | tf_op jit(solution)/shard_map/ppermute | solution.py:132
  286.4 6.2 %collective-permute-done.57 = bf16[600,128]{1,0:T(8,128)(2,1)S(1)} collective-permute-done((bf16[600,128]{1,0:T(8,128)(2,1)S(1)}, bf16[600,128]{1,0:T(8,128)(2,1)S(1)}, u32[]{:S(2)}, u32[]{:S(2)}) %collective-permute-start.57) | collective-permute-done | bytes 153632 | tf_op jit(solution)/shard_map/ppermute | solution.py:136
  293.6 7.3 %collective-permute-done.58 = bf16[1200,128]{1,0:T(8,128)(2,1)S(1)} collective-permute-done((bf16[1200,128]{1,0:T(8,128)(2,1)S(1)}, bf16[1200,128]{1,0:T(8,128)(2,1)S(1)}, u32[]{:S(2)}, u32[]{:S(2)}) %collective-permute-start.58) | collective-permute-done | bytes 307232 | tf_op jit(solution)/shard_map/ppermute | solution.py:136
  325.1 9.5 %collective-permute-done.48 = bf16[2400,128]{1,0:T(8,128)(2,1)} collective-permute-done((bf16[2400,128]{1,0:T(8,128)(2,1)}, bf16[2400,128]{1,0:T(8,128)(2,1)}, u32[]{:S(2)}, u32[]{:S(2)}) %collective-permute-start.48) | collective-permute-done | bytes 614432 | tf_op jit(solution)/shard_map/ppermute | solution.py:136
  373.0 8.0 %collective-permute-done.33 = bf16[2432,128]{1,0:T(8,128)(2,1)S(1)} collective-permute-done((bf16[2432,128]{1,0:T(8,128)(2,1)S(1)}, bf16[2432,128]{1,0:T(8,128)(2,1)S(1)}, u32[]{:S(2)}, u32[]{:S(2)}) %collective-permute-start.33) | collective-permute-done | bytes 622624 | tf_op jit(solution)/shard_map/ppermute | solution.py:136
  384.6 8.6 %collective-permute-done.41 = bf16[2400,128]{1,0:T(8,128)(2,1)S(1)} collective-permute-done((bf16[2400,128]{1,0:T(8,128)(2,1)S(1)}, bf16[2400,128]{1,0:T(8,128)(2,1)S(1)}, u32[]{:S(2)}, u32[]{:S(2)}) %collective-permute-start.41) | collective-permute-done | bytes 614432 | tf_op jit(solution)/shard_map/ppermute | solution.py:136
  396.3 8.8 %collective-permute-done.42 = bf16[1200,128]{1,0:T(8,128)(2,1)S(1)} collective-permute-done((bf16[1200,128]{1,0:T(8,128)(2,1)S(1)}, bf16[1200,128]{1,0:T(8,128)(2,1)S(1)}, u32[]{:S(2)}, u32[]{:S(2)}) %collective-permute-start.42) | collective-permute-done | bytes 307232 | tf_op jit(solution)/shard_map/ppermute | solution.py:136
  408.3 8.7 %collective-permute-done.43 = bf16[600,128]{1,0:T(8,128)(2,1)S(1)} collective-permute-done((bf16[600,128]{1,0:T(8,128)(2,1)S(1)}, bf16[600,128]{1,0:T(8,128)(2,1)S(1)}, u32[]{:S(2)}, u32[]{:S(2)}) %collective-permute-start.43) | collective-permute-done | bytes 153632 | tf_op jit(solution)/shard_map/ppermute | solution.py:136
  417.2 6.5 %collective-permute-done.36 = bf16[608,128]{1,0:T(8,128)(2,1)S(1)} collective-permute-done((bf16[608,128]{1,0:T(8,128)(2,1)S(1)}, bf16[608,128]{1,0:T(8,128)(2,1)S(1)}, u32[]{:S(2)}, u32[]{:S(2)}) %collective-permute-start.36) | collective-permute-done | bytes 155680 | tf_op jit(solution)/shard_map/ppermute | solution.py:136
  427.7 6.5 %collective-permute-done.37 = bf16[1216,128]{1,0:T(8,128)(2,1)S(1)} collective-permute-done((bf16[1216,128]{1,0:T(8,128)(2,1)S(1)}, bf16[1216,128]{1,0:T(8,128)(2,1)S(1)}, u32[]{:S(2)}, u32[]{:S(2)}) %collective-permute-start.37) | collective-permute-done | bytes 311328 | tf_op jit(solution)/shard_map/ppermute | solution.py:136
  442.9 11.3 %collective-permute-done.38 = bf16[2432,128]{1,0:T(8,128)(2,1)S(1)} collective-permute-done((bf16[2432,128]{1,0:T(8,128)(2,1)S(1)}, bf16[2432,128]{1,0:T(8,128)(2,1)S(1)}, u32[]{:S(2)}, u32[]{:S(2)}) %collective-permute-start.38) | collective-permute-done | bytes 622624 | tf_op jit(solution)/shard_map/ppermute | solution.py:136
  454.7 11.2 %collective-permute-done.46 = bf16[2400,128]{1,0:T(8,128)(2,1)S(1)} collective-permute-done((bf16[2400,128]{1,0:T(8,128)(2,1)S(1)}, bf16[2400,128]{1,0:T(8,128)(2,1)S(1)}, u32[]{:S(2)}, u32[]{:S(2)}) %collective-permute-start.46) | collective-permute-done | bytes 614432 | tf_op jit(solution)/shard_map/ppermute | solution.py:136
  476.1 15.1 %shard_map.177 = (f32[38400,128]{1,0:T(8,128)}, f32[38400,128]{1,0:T(8,128)}, f32[38400,128]{1,0:T(8,128)}, f32[38400,128]{1,0:T(8,128)}) custom-call(s32[1]{0:T(128)} %bitcast.108.refs_0_, f32[38400,128]{1,0:T(8,128)} %bitcast.444, f32[38400,128]{1,0:T(8,128)} %bitcast.448, f32[38400,128]{1,0:T(8,128)} %bitcast.452, ...), custom_call_target="tpu_custom_call" | custom-call | flops 24576000 | bytes 39321600 | tf_op jit(solution)/shard_map/pallas_call | solution.py:250
  491.3 15.5 %shard_map.178 = (f32[38400,128]{1,0:T(8,128)}, f32[38400,128]{1,0:T(8,128)}, f32[38400,128]{1,0:T(8,128)}, f32[38400,128]{1,0:T(8,128)}) custom-call(s32[1]{0:T(128)} %bitcast.108.refs_0_, f32[38400,128]{1,0:T(8,128)} %bitcast.445, f32[38400,128]{1,0:T(8,128)} %bitcast.449, ...), custom_call_target="tpu_custom_call", output_to_operand_aliasing={{0}: (6, {}), {1}: (7, {}), {2}: (8, {}), {3}: (9, {})} | custom-call | flops 24576000 | bytes 39321600 | tf_op jit(solution)/shard_map/pallas_call | solution.py:250
  506.9 15.5 %shard_map.179 = (f32[38400,128]{1,0:T(8,128)}, f32[38400,128]{1,0:T(8,128)}, f32[38400,128]{1,0:T(8,128)}, f32[38400,128]{1,0:T(8,128)}) custom-call(s32[1]{0:T(128)} %bitcast.108.refs_0_, f32[38400,128]{1,0:T(8,128)} %bitcast.446, f32[38400,128]{1,0:T(8,128)} %bitcast.450, ...), custom_call_target="tpu_custom_call", output_to_operand_aliasing={{0}: (6, {}), {1}: (7, {}), {2}: (8, {}), {3}: (9, {})} | custom-call | flops 24576000 | bytes 39321600 | tf_op jit(solution)/shard_map/pallas_call | solution.py:250
  523.9 15.2 %shard_map.180 = (f32[38400,128]{1,0:T(8,128)}, f32[38400,128]{1,0:T(8,128)}, f32[38400,128]{1,0:T(8,128)}, f32[38400,128]{1,0:T(8,128)}) custom-call(s32[1]{0:T(128)} %bitcast.108.refs_0_, f32[38400,128]{1,0:T(8,128)} %bitcast.447, f32[38400,128]{1,0:T(8,128)} %bitcast.451, ...), custom_call_target="tpu_custom_call", output_to_operand_aliasing={{0}: (6, {}), {1}: (7, {}), {2}: (8, {}), {3}: (9, {})} | custom-call | flops 24576000 | bytes 39321600 | tf_op jit(solution)/shard_map/pallas_call | solution.py:250
  (500 shorter events, 293.4 us)
Async XLA Ops:
  1.3 36.0 %collective-permute-start = (bf16[2,480]{1,0:T(2,128)(2,1)S(1)}, bf16[2,480]{1,0:T(2,128)(2,1)S(1)}, u32[]{:S(2)}, u32[]{:S(2)}) collective-permute-start(bf16[2,480]{1,0:T(2,128)(2,1)S(1)} %convert_element_type.426), channel_id=1, source_target_pairs={{0,1},{1,0},{2,3},{3,2},{4,5},{5,4},{6,7},{7,6},{8,9},{9,8},{10,11... | collective-permute-start | bytes 5768 | tf_op jit(solution)/shard_map/ppermute | solution.py:132
  8.2 31.9 %collective-permute-start.1 = (bf16[1,120,1600]{2,1,0:T(8,128)(2,1)}, bf16[1,120,1600]{2,1,0:T(8,128)(2,1)}, u32[]{:S(2)}, u32[]{:S(2)}) collective-permute-start(bf16[1,120,1600]{2,1,0:T(8,128)(2,1)} %concatenate.182), channel_id=1, source_target_pairs={{0,1},{1,0},{2,3},{3,2},{4,5},{5,4},{6,7},{7,6},{8,9},{9,8},{10,11... | collective-permute-start | bytes 1152008 | tf_op jit(solution)/shard_map/ppermute | solution.py:132
  8.2 121.4 %collective-permute-start.7 = (bf16[256,960]{0,1:T(8,128)(2,1)}, bf16[256,960]{0,1:T(8,128)(2,1)}, u32[]{:S(2)}, u32[]{:S(2)}) collective-permute-start(bf16[256,960]{0,1:T(8,128)(2,1)} %param.11), channel_id=1, source_target_pairs={{0,1},{1,0},{2,3},{3,2},{4,5},{5,4},{6,7},{7,6},{8,9},{9,8},{10,11... | collective-permute-start | bytes 1474568 | tf_op jit(solution)/shard_map/ppermute | solution.py:132
  15.8 66.2 %collective-permute-start.16 = (bf16[1,320,960]{2,1,0:T(8,128)(2,1)}, bf16[1,320,960]{2,1,0:T(8,128)(2,1)}, u32[]{:S(2)}, u32[]{:S(2)}) collective-permute-start(bf16[1,320,960]{2,1,0:T(8,128)(2,1)} %reshape.533), channel_id=1, source_target_pairs={{0,1},{1,0},{2,3},{3,2},{4,5},{5,4},{6,7},{7,6},{8,9},{9,8},{10,11... | collective-permute-start | bytes 1843208 | tf_op jit(solution)/shard_map/ppermute | solution.py:132
  38.6 34.4 %collective-permute-start.9 = (bf16[1,120,960]{2,1,0:T(8,128)(2,1)}, bf16[1,120,960]{2,1,0:T(8,128)(2,1)}, u32[]{:S(2)}, u32[]{:S(2)}) collective-permute-start(bf16[1,120,960]{2,1,0:T(8,128)(2,1)} %collective-permute-done.8), channel_id=1, source_target_pairs={{0,4},{2,6},{4,0},{6,2},{8,12},{10,14},{12,8},{14,10},{16,20},{18,... | collective-permute-start | bytes 691208 | tf_op jit(solution)/shard_map/ppermute | solution.py:136
  40.1 34.1 %collective-permute-start.10 = (bf16[1,120,960]{2,1,0:T(8,128)(2,1)}, bf16[1,120,960]{2,1,0:T(8,128)(2,1)}, u32[]{:S(2)}, u32[]{:S(2)}) collective-permute-start(bf16[1,120,960]{2,1,0:T(8,128)(2,1)} %collective-permute-done.8), channel_id=1, source_target_pairs={{0,2},{2,0},{4,6},{6,4},{8,10},{10,8},{12,14},{14,12},{16,18},{18,... | collective-permute-start | bytes 691208 | tf_op jit(solution)/shard_map/ppermute | solution.py:136
  75.6 29.9 %collective-permute-start.12 = (bf16[1,120,5120]{2,1,0:T(8,128)(2,1)S(1)}, bf16[1,120,5120]{2,1,0:T(8,128)(2,1)S(1)}, u32[]{:S(2)}, u32[]{:S(2)}) collective-permute-start(bf16[1,120,5120]{2,1,0:T(8,128)(2,1)S(1)} %copy-done.45), channel_id=1, source_target_pairs={{0,1},{1,0},{2,3},{3,2},{4,5},{5,4},{6,7},{7,6},{8,9},{9,8},{10,11... | collective-permute-start | bytes 3686408 | tf_op jit(solution)/shard_map/ppermute | solution.py:132
  82.0 47.6 %collective-permute-start.6 = (bf16[256,480]{0,1:T(8,128)(2,1)}, bf16[256,480]{0,1:T(8,128)(2,1)}, u32[]{:S(2)}, u32[]{:S(2)}) collective-permute-start(bf16[256,480]{0,1:T(8,128)(2,1)} %get-tuple-element.130), channel_id=1, source_target_pairs={{0,1},{1,0},{2,3},{3,2},{4,5},{5,4},{6,7},{7,6},{8,9},{9,8},{10,11... | collective-permute-start | bytes 737288 | tf_op jit(solution)/shard_map/ppermute | solution.py:132
  82.6 34.5 %collective-permute-start.17 = (bf16[1,320,960]{2,1,0:T(8,128)(2,1)}, bf16[1,320,960]{2,1,0:T(8,128)(2,1)}, u32[]{:S(2)}, u32[]{:S(2)}) collective-permute-start(bf16[1,320,960]{2,1,0:T(8,128)(2,1)} %collective-permute-done.16), channel_id=1, source_target_pairs={{0,4},{2,6},{4,0},{6,2},{8,12},{10,14},{12,8},{14,10},{16,20},{18,... | collective-permute-start | bytes 1843208 | tf_op jit(solution)/shard_map/ppermute | solution.py:136
  83.7 36.4 %collective-permute-start.18 = (bf16[1,320,960]{2,1,0:T(8,128)(2,1)}, bf16[1,320,960]{2,1,0:T(8,128)(2,1)}, u32[]{:S(2)}, u32[]{:S(2)}) collective-permute-start(bf16[1,320,960]{2,1,0:T(8,128)(2,1)} %collective-permute-done.16), channel_id=1, source_target_pairs={{0,2},{2,0},{4,6},{6,4},{8,10},{10,8},{12,14},{14,12},{16,18},{18,... | collective-permute-start | bytes 1843208 | tf_op jit(solution)/shard_map/ppermute | solution.py:136
  131.9 30.6 %collective-permute-start.21 = (bf16[256,480]{0,1:T(8,128)(2,1)S(1)}, bf16[256,480]{0,1:T(8,128)(2,1)}, u32[]{:S(2)}, u32[]{:S(2)}) collective-permute-start(bf16[256,480]{0,1:T(8,128)(2,1)S(1)} %get-tuple-element.128), channel_id=1, source_target_pairs={{0,1},{1,0},{2,3},{3,2},{4,5},{5,4},{6,7},{7,6},{8,9},{9,8},{10,11... | collective-permute-start | bytes 737288 | tf_op jit(solution)/shard_map/ppermute | solution.py:132
  186.8 30.1 %collective-permute-start.31 = (bf16[256,960]{0,1:T(8,128)(2,1)}, bf16[256,960]{0,1:T(8,128)(2,1)}, u32[]{:S(2)}, u32[]{:S(2)}) collective-permute-start(bf16[256,960]{0,1:T(8,128)(2,1)} %fusion.126), channel_id=1, source_target_pairs={{0,1},{1,0},{2,3},{3,2},{4,5},{5,4},{6,7},{7,6},{8,9},{9,8},{10,11... | collective-permute-start | bytes 1474568 | tf_op jit(solution)/shard_map/ppermute | solution.py:132
  207.5 31.5 %collective-permute-start.24 = (bf16[256,2560]{1,0:T(8,128)(2,1)}, bf16[256,2560]{1,0:T(8,128)(2,1)}, u32[]{:S(2)}, u32[]{:S(2)}) collective-permute-start(bf16[256,2560]{1,0:T(8,128)(2,1)} %copy-done.41), channel_id=1, source_target_pairs={{0,1},{1,0},{2,3},{3,2},{4,5},{5,4},{6,7},{7,6},{8,9},{9,8},{10,11... | collective-permute-start | bytes 3932168 | tf_op jit(solution)/shard_map/ppermute | solution.py:132
  244.7 60.1 %collective-permute-start.27 = (bf16[256,2560]{1,0:T(8,128)(2,1)}, bf16[256,2560]{1,0:T(8,128)(2,1)}, u32[]{:S(2)}, u32[]{:S(2)}) collective-permute-start(bf16[256,2560]{1,0:T(8,128)(2,1)} %get-tuple-element.69), channel_id=1, source_target_pairs={{0,1},{1,0},{2,3},{3,2},{4,5},{5,4},{6,7},{7,6},{8,9},{9,8},{10,11... | collective-permute-start | bytes 3932168 | tf_op jit(solution)/shard_map/ppermute | solution.py:132
  247.3 35.2 %collective-permute-start.26 = (bf16[256,640]{0,1:T(8,128)(2,1)S(1)}, bf16[256,640]{0,1:T(8,128)(2,1)}, u32[]{:S(2)}, u32[]{:S(2)}) collective-permute-start(bf16[256,640]{0,1:T(8,128)(2,1)S(1)} %slice.543), channel_id=1, source_target_pairs={{0,1},{1,0},{2,3},{3,2},{4,5},{5,4},{6,7},{7,6},{8,9},{9,8},{10,11... | collective-permute-start | bytes 983048 | tf_op jit(solution)/shard_map/ppermute | solution.py:132
  259.8 43.6 %collective-permute-start.28 = (bf16[4800,128]{1,0:T(8,128)(2,1)S(1)}, bf16[4800,128]{1,0:T(8,128)(2,1)S(1)}, u32[]{:S(2)}, u32[]{:S(2)}) collective-permute-start(bf16[4800,128]{1,0:T(8,128)(2,1)S(1)} %dynamic-slice_bitcast_fusion.2), channel_id=1, source_target_pairs={{0,2},{2,0},{4,6},{6,4},{8,10},{10,8},{12,14},{14,12},{16,18},{18,... | collective-permute-start | bytes 3686408 | tf_op jit(solution)/shard_map/ppermute | solution.py:136
  301.9 54.9 %collective-permute-start.59 = (bf16[2400,128]{1,0:T(8,128)(2,1)}, bf16[2400,128]{1,0:T(8,128)(2,1)}, u32[]{:S(2)}, u32[]{:S(2)}) collective-permute-start(bf16[2400,128]{1,0:T(8,128)(2,1)} %maximum_select_fusion.7), channel_id=1, source_target_pairs={{0,4},{2,6},{4,0},{6,2},{8,12},{10,14},{12,8},{14,10},{16,20},{18,... | collective-permute-start | bytes 1843208 | tf_op jit(solution)/shard_map/ppermute | solution.py:136
  306.9 32.7 %collective-permute-start.29 = (bf16[256,1600]{0,1:T(8,128)(2,1)S(1)}, bf16[256,1600]{0,1:T(8,128)(2,1)}, u32[]{:S(2)}, u32[]{:S(2)}) collective-permute-start(bf16[256,1600]{0,1:T(8,128)(2,1)S(1)} %pad_maximum_fusion.5), channel_id=1, source_target_pairs={{0,1},{1,0},{2,3},{3,2},{4,5},{5,4},{6,7},{7,6},{8,9},{9,8},{10,11... | collective-permute-start | bytes 2457608 | tf_op jit(solution)/shard_map/ppermute | solution.py:132
  323.6 41.9 %collective-permute-start.40 = (bf16[4800,128]{1,0:T(8,128)(2,1)}, bf16[4800,128]{1,0:T(8,128)(2,1)}, u32[]{:S(2)}, u32[]{:S(2)}) collective-permute-start(bf16[4800,128]{1,0:T(8,128)(2,1)} %dynamic-slice_bitcast_fusion.1), channel_id=1, source_target_pairs={{0,2},{2,0},{4,6},{6,4},{8,10},{10,8},{12,14},{14,12},{16,18},{18,... | collective-permute-start | bytes 3686408 | tf_op jit(solution)/shard_map/ppermute | solution.py:136
  358.8 117.4 %collective-permute-start.60 = (bf16[4800,128]{1,0:T(8,128)(2,1)S(1)}, bf16[4800,128]{1,0:T(8,128)(2,1)}, u32[]{:S(2)}, u32[]{:S(2)}) collective-permute-start(bf16[4800,128]{1,0:T(8,128)(2,1)S(1)} %maximum_select_fusion.3.refs_4_), channel_id=1, source_target_pairs={{0,2},{2,0},{4,6},{6,4},{8,10},{10,8},{12,14},{14,12},{16,18},{18,... | collective-permute-start | bytes 3686408 | tf_op jit(solution)/shard_map/ppermute | solution.py:136
  372.9 50.9 %collective-permute-start.52 = (bf16[1200,128]{1,0:T(8,128)(2,1)S(1)}, bf16[1200,128]{1,0:T(8,128)(2,1)S(1)}, u32[]{:S(2)}, u32[]{:S(2)}) collective-permute-start(bf16[1200,128]{1,0:T(8,128)(2,1)S(1)} %maximum_select_fusion.10), channel_id=1, source_target_pairs={{0,8},{2,10},{4,12},{6,14},{8,0},{10,2},{12,4},{14,6},{16,24},{18,... | collective-permute-start | bytes 921608 | tf_op jit(solution)/shard_map/ppermute | solution.py:136
  442.9 48.4 %collective-permute-start.54 = (bf16[4800,128]{1,0:T(8,128)(2,1)}, bf16[4800,128]{1,0:T(8,128)(2,1)}, u32[]{:S(2)}, u32[]{:S(2)}) collective-permute-start(bf16[4800,128]{1,0:T(8,128)(2,1)} %maximum_select_fusion.2.refs_4_), channel_id=1, source_target_pairs={{0,2},{2,0},{4,6},{6,4},{8,10},{10,8},{12,14},{14,12},{16,18},{18,... | collective-permute-start | bytes 3686408 | tf_op jit(solution)/shard_map/ppermute | solution.py:136
  454.6 67.8 %collective-permute-start.39 = (bf16[4864,128]{1,0:T(8,128)(2,1)S(1)}, bf16[4864,128]{1,0:T(8,128)(2,1)}, u32[]{:S(2)}, u32[]{:S(2)}) collective-permute-start(bf16[4864,128]{1,0:T(8,128)(2,1)S(1)} %maximum_select_fusion.refs_4_), channel_id=1, source_target_pairs={{0,2},{2,0},{4,6},{6,4},{8,10},{10,8},{12,14},{14,12},{16,18},{18,... | collective-permute-start | bytes 3735560 | tf_op jit(solution)/shard_map/ppermute | solution.py:136
  467.2 39.6 %collective-permute-start.47 = (bf16[4800,128]{1,0:T(8,128)(2,1)}, bf16[4800,128]{1,0:T(8,128)(2,1)}, u32[]{:S(2)}, u32[]{:S(2)}) collective-permute-start(bf16[4800,128]{1,0:T(8,128)(2,1)} %maximum_select_fusion.1.refs_4_), channel_id=1, source_target_pairs={{0,2},{2,0},{4,6},{6,4},{8,10},{10,8},{12,14},{14,12},{16,18},{18,... | collective-permute-start | bytes 3686408 | tf_op jit(solution)/shard_map/ppermute | solution.py:136
  (121 other events, 1375.5 us)

commit v4 on v3

--- a/solution.py
+++ b/solution.py
@@ -165,21 +165,18 @@
     return swap_shards(jnp.concatenate(pieces, axis=2))
 
 
-def gather_rows(params, columns, fetched):
-    my_shard = lax.axis_index("cp")
+def own_rows(params, columns):
+    offset, rows, width = columns
+    return (
+        params[offset : offset + rows * width].astype(jnp.bfloat16).reshape(4, rows // 4, width)
+    )
+
+
+def gather_rows(mine, fetched, across):
     quarter = lax.axis_index("dp") % 4
-    across = swap_replicas(fetched, 2)
-    mine = jnp.concatenate(
-        [
-            params[offset : offset + rows * width]
-            .astype(jnp.bfloat16)
-            .reshape(4, rows // 4, width)
-            for offset, rows, width in columns
-        ],
-        axis=2,
-    )
+    mine = jnp.concatenate(mine, axis=2)
     whole = jnp.concatenate([mine, mine], axis=0)
-    other = (1 - my_shard) * 4
+    other = (1 - lax.axis_index("cp")) * 4
     for piece, place in (
         (fetched, quarter),
         (across, quarter ^ 2),
@@ -212,12 +209,16 @@
     return flat
 
 
-def gather_steps(piece):
-    distance = lax.axis_size("dp") // 2
-    while distance >= 2:
+def gather_steps(piece, distance, last):
+    while distance >= last:
         bit = (lax.axis_index("dp") // distance) % 2
         piece = in_order(piece, swap_replicas(piece, distance), bit, 0)
         distance //= 2
+    return piece
+
+
+def gather_halves(part):
+    piece = gather_steps(part, lax.axis_size("dp") // 2, 2)
     return (piece, swap_replicas(piece, 1))
 
 
@@ -227,7 +228,8 @@
 
 def update_kernel(first_rate, last_rate, split, bit_ref, *refs):
     params_ref, first_ref, second_ref, mine_ref, received_ref = refs[:5]
-    grad_out, first_out, second_out, params_out = refs[-4:]
+    grad_out, first_out, second_out, params_out, mark_out = refs[-5:]
+    mark_out[...] = jnp.zeros_like(mark_out)
     own_half = pl.program_id(0) // (CHUNK_BLOCKS // 2) == bit_ref[0]
     gradient = jnp.where(
         own_half, mine_ref[...].astype(jnp.float32), received_ref[...].astype(jnp.float32)
@@ -254,8 +256,9 @@
         + [spec] * 3
         + [half_spec] * 2
         + [pl.BlockSpec(memory_space=pl.ANY)] * len(earlier),
-        out_specs=[spec] * 4,
-        out_shape=[jax.ShapeDtypeStruct((rows, 128), jnp.float32)] * 4,
+        out_specs=[spec] * 4 + [pl.BlockSpec((8, 128), lambda i: (0, 0))],
+        out_shape=[jax.ShapeDtypeStruct((rows, 128), jnp.float32)] * 4
+        + [jax.ShapeDtypeStruct((8, 128), jnp.float32)],
         input_output_aliases={6 + index: index for index in range(len(earlier))},
         compiler_params=pltpu.CompilerParams(vmem_limit_bytes=40 * 1024 * 1024),
         cost_estimate=pl.CostEstimate(
@@ -297,13 +300,22 @@
         fetch_quarter(params, columns)
         for columns in (blocks[:3], blocks[3:4], blocks[4:6], blocks[6:])
     ]
-    w_qkv = gather_rows(params, blocks[:3], fetched[0])
-    held, fetched[0] = lax.optimization_barrier((params, fetched[0]))
-    w_out = gather_rows(held, blocks[3:4], fetched[1])
-    held, fetched[1] = lax.optimization_barrier((held, fetched[1]))
-    w_pair = gather_rows(held, blocks[4:6], fetched[2])
-    held, fetched[2] = lax.optimization_barrier((held, fetched[2]))
-    w_down = gather_rows(held, blocks[6:], fetched[3])
+    own_qkv = [own_rows(params, columns) for columns in blocks[:3]]
+    own_out = own_rows(params, blocks[3])
+    held, fetched[0], fetched[1], fetched[2] = lax.optimization_barrier(
+        (params, fetched[0], fetched[1], fetched[2])
+    )
+    across = [swap_replicas(piece, 2) for piece in fetched]
+    own_gate = own_rows(held, blocks[4])
+    held, across[0], across[1], across[2] = lax.optimization_barrier(
+        (held, across[0], across[1], across[2])
+    )
+    own_up = own_rows(held, blocks[5])
+    own_down = own_rows(held, blocks[6])
+    w_qkv = gather_rows(own_qkv, fetched[0], across[0])
+    w_out = gather_rows([own_out], fetched[1], across[1])
+    w_pair = gather_rows([own_gate, own_up], fetched[2], across[2])
+    w_down = gather_rows([own_down], fetched[3], across[3])
 
     out_peer = swap_shards(out_grad)
     segment_all, position_all = window_layout(lengths[0], slot_positions[0])
@@ -367,35 +379,20 @@
     grad_gate_act, grad_up_act = pull_act(grad_hidden)
     gate_back = grad_gate_act.astype(low_type)
     up_back = grad_up_act.astype(low_type)
+    gate_peer = swap_shards(gate_back)
+    up_peer = swap_shards(up_back)
     pair_back = jnp.concatenate([gate_back, up_back], axis=1)
     pair_back, attn_peer, two_peer = lax.optimization_barrier((pair_back, attn_peer, two_peer))
     grad_xn_two = jnp.dot(pair_back, w_pair.T, preferred_element_type=jnp.float32)
-    gate_sent, hidden_peer, grad_xn_two = lax.optimization_barrier(
-        (gate_back, hidden_peer, grad_xn_two)
-    )
-    gate_peer = swap_shards(gate_sent)
     back_two, gain_grad_two = pull_two(grad_xn_two)
     grad_resid = out_grad.astype(jnp.float32) + back_two
     resid_low = grad_resid.astype(low_type)
     resid_peer = swap_shards(resid_low)
-    grad_down = owned_product(hidden_mine, hidden_peer, out_grad, out_peer).reshape(-1, 128)
-    down_part = scatter_replicas(grad_down, 1)
     grad_attn = jnp.dot(resid_low, w_out.T, preferred_element_type=jnp.float32).astype(low_type)
     grad_groups = grad_attn.reshape(local_rows, KVH, group_size, HD).transpose(1, 0, 2, 3)
     backward_groups = []
     for group in range(KVH):
         grad_group = grad_groups[group]
-        if group == 3:
-            earlier_group = backward_groups[2]
-            grad_group, down_part, earlier_group = lax.optimization_barrier(
-                (grad_group, down_part, earlier_group)
-            )
-            backward_groups[2] = earlier_group
-            down_part = scatter_replicas(down_part, 2)
-            up_sent, gate_peer, grad_group = lax.optimization_barrier(
-                (up_back, gate_peer, grad_group)
-            )
-            up_peer = swap_shards(up_sent)
         backward_groups.append(
             group_backward(
                 (
@@ -413,7 +410,7 @@
     key_terms = jnp.concatenate([terms[1] for terms in backward_groups], axis=1)
     value_terms = jnp.concatenate([terms[2] for terms in backward_groups], axis=1)
     terms = jnp.concatenate([key_terms, value_terms], axis=1)
-    terms, gate_peer, down_part = lax.optimization_barrier((terms, gate_peer, down_part))
+    terms, gate_peer = lax.optimization_barrier((terms, gate_peer))
     grad_gate = owned_product(two_mine, two_peer, gate_back, gate_peer).reshape(-1, 128)
     gate_part = scatter_replicas(grad_gate, 1)
     terms_mine = terms[:local_rows] + swap_shards(terms[local_rows:].astype(low_type)).astype(
@@ -431,8 +428,11 @@
         ],
         axis=1,
     )
-    qkv_back, up_peer, gate_part = lax.optimization_barrier((qkv_back, up_peer, gate_part))
+    qkv_back, up_peer, hidden_peer, gate_part = lax.optimization_barrier(
+        (qkv_back, up_peer, hidden_peer, gate_part)
+    )
     grad_up = owned_product(two_mine, two_peer, up_back, up_peer).reshape(-1, 128)
+    grad_down = owned_product(hidden_mine, hidden_peer, out_grad, out_peer).reshape(-1, 128)
     qkv_peer = swap_shards(qkv_back)
     grad_xn_one = jnp.dot(qkv_back, w_qkv.T, preferred_element_type=jnp.float32)
     back_one, gain_grad_one = pull_one(grad_xn_one)
@@ -456,21 +456,26 @@
         ],
         axis=0,
     )
-    down_sum = gather_steps(scatter_steps(down_part, 4, replica_count))
-    gate_sum = gather_steps(scatter_steps(gate_part, 2, replica_count))
-    up_sum = gather_steps(scatter_steps(grad_up, 1, replica_count))
-    attn_sum = gather_steps(scatter_steps(grad_attn_owned, 1, replica_count))
+    gate_sum = gather_halves(scatter_steps(gate_part, 2, replica_count))
+    up_sum = gather_halves(scatter_steps(grad_up, 1, replica_count))
+    down_sum = gather_halves(scatter_steps(grad_down, 1, replica_count))
+    attn_part = scatter_steps(grad_attn_owned, 1, replica_count)
     core = lax.axis_index("dp") % 2
+    bit = core.reshape(1).astype(jnp.int32)
+    rates = matrix_rates(longest)
+    state = [values.reshape(-1, 128) for values in (params, first_moment, second_moment)]
+    *updated, mark = update_chunk(state, gate_sum, bit, 1, (rates[4], rates[4]), 0, ())
+    attn_part, mark = lax.optimization_barrier((attn_part, mark))
+    attn_piece = gather_steps(attn_part, replica_count // 2, 4)
+    *updated, mark = update_chunk(state, up_sum, bit, 2, (rates[5], rates[5]), 0, updated)
+    attn_piece, mark = lax.optimization_barrier((attn_piece, mark))
+    attn_piece = gather_steps(attn_piece, 2, 2)
+    attn_sum = (attn_piece, swap_replicas(attn_piece, 1))
+    *updated, mark = update_chunk(state, down_sum, bit, 3, (rates[6], rates[6]), 0, updated)
+    *updated, mark = update_chunk(state, attn_sum, bit, 0, (rates[0], rates[3]), 5, updated)
     gain_sum = jnp.where(core == 0, attn_sum[0][half_rows:], attn_sum[1][half_rows:])
     gain_owned = gain_sum[:8].reshape(-1)[: 2 * (D // shard_count)]
     gain_owned = gain_owned.reshape(2, -1).astype(jnp.float32)
-    rates = matrix_rates(longest)
-    bit = core.reshape(1).astype(jnp.int32)
-    state = [values.reshape(-1, 128) for values in (params, first_moment, second_moment)]
-    updated = update_chunk(state, down_sum, bit, 3, (rates[6], rates[6]), 0, ())
-    updated = update_chunk(state, gate_sum, bit, 1, (rates[4], rates[4]), 0, updated)
-    updated = update_chunk(state, up_sum, bit, 2, (rates[5], rates[5]), 0, updated)
-    updated = update_chunk(state, attn_sum, bit, 0, (rates[0], rates[3]), 5, updated)
     owned_grad, new_first, new_second, new_params = [values.reshape(-1) for values in updated]
     new_gain_first, new_gain_second, new_gains = adamw_step(
         norm_gains, gain_owned, gain_first, gain_second, gain_rate, 0.0

time: 545 us -> 548 us (level)
  waiting for transfers between devices: 182 us -> 205 us
  matrix products: 70.1 us -> 56.7 us
  other arithmetic: 65.8 us -> 56.5 us
    ppermute x17, waiting for transfers between devices: 51.9 us -> 76.6 us  [swap_shards(): return lax.ppermute(values, 'cp', [(0, 1), (1, 0)])]
    unnamed x178 -> x97, local copies, waits for them, and re-layouts: 7.05 us -> 13.3 us
    ppermute x44, starting transfers between devices: 40.3 us -> 46.1 us  [swap_replicas(): lax.ppermute(values, 'dp', [(index, index ^ distance) for index in range(...]
  transfers between devices with their start and end apart: 61 -> 61, of which waited for: 24 -> 23; matrix products, arithmetic and copies ran while one was open for 40% -> 37% of each run, Pallas kernels for 9% -> 9%
where the time goes in v4:
time: 548 us; the launch traced here: 543 us
  waiting for transfers between devices  205 us (37%)
  local copies, waits for them, and re-layouts  98.3 us (18%)
  starting transfers between devices  62.8 us (11%)
  Pallas kernels  61.4 us (11%)
  matrix products  56.7 us (10%)
  other arithmetic  56.5 us (10%)
    ppermute x44, waiting for transfers between devices, swap_replicas(): lax.ppermute(values, 'dp', [(index, index ^ distance) for index in range(...  128 us
    ppermute x17, waiting for transfers between devices, swap_shards(): return lax.ppermute(values, 'cp', [(0, 1), (1, 0)])  76.6 us
    pallas_call x4, Pallas kernels, update_chunk(): pl.pallas_call(lambda *refs: update_kernel(rates[0], rates[1], split, *re...  61.4 us
    ppermute x44, starting transfers between devices, swap_replicas(): lax.ppermute(values, 'dp', [(index, index ^ distance) for index in range(...  46.1 us
    dot_general x5, matrix products, owned_product(): jnp.dot(left.T, right, preferred_element_type=jnp.float32)  18.4 us
    ppermute x17, starting transfers between devices, swap_shards(): return lax.ppermute(values, 'cp', [(0, 1), (1, 0)])  16.7 us
    another operation x7, other arithmetic  15.7 us
    convert_element_type x7, local copies, waits for them, and re-layouts, own_rows(): params[offset:offset + rows * width].astype(jnp.bfloat16)  14.8 us
  transfers between devices with their start and end apart: 61, of which 23 were waited for; matrix products, arithmetic and copies ran while one was open for 37% of the time, Pallas kernels for 9%

profile of v4, /device:TPU:0, one launch (start us, length us, event | category | flops | bytes accessed | tf_op | source)
XLA Modules:
  0.0 542.7 jit_solution(1191008724566397735)
XLA Ops:
  18.7 7.7 %convert.67 = bf16[4915200]{0:T(1024)(128)(2,1)S(1)} convert(f32[4915200]{0:T(1024)} %param.14) | non-fusion elementwise | flops 4915200 | bytes 29491200 | tf_op jit(solution)/shard_map/convert.38
  38.6 13.6 %collective-permute-done.3 = bf16[1,120,5120]{2,1,0:T(8,128)(2,1)} collective-permute-done((bf16[1,120,5120]{2,1,0:T(8,128)(2,1)}, bf16[1,120,5120]{2,1,0:T(8,128)(2,1)}, u32[]{:S(2)}, u32[]{:S(2)}) %collective-permute-start.3) | collective-permute-done | bytes 1228832 | tf_op jit(solution)/shard_map/ppermute | solution.py:132
  68.3 7.1 %collective-permute-done.16 = bf16[1,320,960]{2,1,0:T(8,128)(2,1)} collective-permute-done((bf16[1,320,960]{2,1,0:T(8,128)(2,1)}, bf16[1,320,960]{2,1,0:T(8,128)(2,1)}, u32[]{:S(2)}, u32[]{:S(2)}) %collective-permute-start.16) | collective-permute-done | bytes 614432 | tf_op jit(solution)/shard_map/ppermute | solution.py:132
  75.7 17.5 %collective-permute-done.5 = bf16[1,120,960]{2,1,0:T(8,128)(2,1)S(1)} collective-permute-done((bf16[1,120,960]{2,1,0:T(8,128)(2,1)}, bf16[1,120,960]{2,1,0:T(8,128)(2,1)S(1)}, u32[]{:S(2)}, u32[]{:S(2)}) %collective-permute-start.5) | collective-permute-done | bytes 230432 | tf_op jit(solution)/shard_map/ppermute | solution.py:136
  95.2 7.4 %convert.74 = bf16[4915200]{0:T(1024)(128)(2,1)S(1)} convert(f32[4915200]{0:T(1024)} %param.14) | non-fusion elementwise | flops 4915200 | bytes 29491200 | tf_op jit(solution)/shard_map/convert.26
  133.4 8.5 %collective-permute-done.9 = bf16[256,640]{0,1:T(8,128)(2,1)S(1)} collective-permute-done((bf16[256,640]{0,1:T(8,128)(2,1)S(1)}, bf16[256,640]{0,1:T(8,128)(2,1)S(1)}, u32[]{:S(2)}, u32[]{:S(2)}) %collective-permute-start.9) | collective-permute-done | bytes 327712 | tf_op jit(solution)/shard_map/ppermute | solution.py:132
  155.5 7.4 %fusion.2 = (bf16[256,2560]{1,0:T(8,128)(2,1)}, bf16[256,2560]{1,0:T(8,128)(2,1)}, bf16[256,2560]{1,0:T(8,128)(2,1)}) fusion(f32[256,5120]{1,0:T(8,128)S(1)} %fusion.147, bf16[2560,960]{1,0:T(8,128)(2,1)} %bitcast.470, bf16[256,960]{0,1:T(8,128)(2,1)} %param.11), kind=kOutput, calls=%fused_computation.12 | convolution fusion | flops 1268776960 | bytes 14581760 | tf_op jit(solution)/shard_map/dot_general | solution.py:378
  187.0 7.8 %collective-permute-done.22 = bf16[256,2560]{1,0:T(8,128)(2,1)S(1)} collective-permute-done((bf16[256,2560]{1,0:T(8,128)(2,1)}, bf16[256,2560]{1,0:T(8,128)(2,1)S(1)}, u32[]{:S(2)}, u32[]{:S(2)}) %collective-permute-start.22) | collective-permute-done | bytes 1310752 | tf_op jit(solution)/shard_map/ppermute | solution.py:132
  206.8 26.7 %collective-permute-done.29 = bf16[256,960]{0,1:T(8,128)(2,1)} collective-permute-done((bf16[256,960]{0,1:T(8,128)(2,1)}, bf16[256,960]{0,1:T(8,128)(2,1)}, u32[]{:S(2)}, u32[]{:S(2)}) %collective-permute-start.29) | collective-permute-done | bytes 491552 | tf_op jit(solution)/shard_map/ppermute | solution.py:132
  239.6 12.8 %collective-permute-done.23 = bf16[256,640]{0,1:T(8,128)(2,1)} collective-permute-done((bf16[256,640]{0,1:T(8,128)(2,1)S(1)}, bf16[256,640]{0,1:T(8,128)(2,1)}, u32[]{:S(2)}, u32[]{:S(2)}) %collective-permute-start.23) | collective-permute-done | bytes 327712 | tf_op jit(solution)/shard_map/ppermute | solution.py:132
  290.4 14.5 %collective-permute-done.54 = bf16[2400,128]{1,0:T(8,128)(2,1)S(1)} collective-permute-done((bf16[2400,128]{1,0:T(8,128)(2,1)}, bf16[2400,128]{1,0:T(8,128)(2,1)S(1)}, u32[]{:S(2)}, u32[]{:S(2)}) %collective-permute-start.54) | collective-permute-done | bytes 614432 | tf_op jit(solution)/shard_map/ppermute | solution.py:136
  340.3 6.7 %collective-permute-done.57 = bf16[600,128]{1,0:T(8,128)(2,1)S(1)} collective-permute-done((bf16[600,128]{1,0:T(8,128)(2,1)S(1)}, bf16[600,128]{1,0:T(8,128)(2,1)S(1)}, u32[]{:S(2)}, u32[]{:S(2)}) %collective-permute-start.57) | collective-permute-done | bytes 153632 | tf_op jit(solution)/shard_map/ppermute | solution.py:136
  349.4 6.9 %collective-permute-done.58 = bf16[1200,128]{1,0:T(8,128)(2,1)S(1)} collective-permute-done((bf16[1200,128]{1,0:T(8,128)(2,1)S(1)}, bf16[1200,128]{1,0:T(8,128)(2,1)S(1)}, u32[]{:S(2)}, u32[]{:S(2)}) %collective-permute-start.58) | collective-permute-done | bytes 307232 | tf_op jit(solution)/shard_map/ppermute | solution.py:136
  360.0 9.7 %collective-permute-done.47 = bf16[2400,128]{1,0:T(8,128)(2,1)S(1)} collective-permute-done((bf16[2400,128]{1,0:T(8,128)(2,1)S(1)}, bf16[2400,128]{1,0:T(8,128)(2,1)S(1)}, u32[]{:S(2)}, u32[]{:S(2)}) %collective-permute-start.47) | collective-permute-done | bytes 614432 | tf_op jit(solution)/shard_map/ppermute | solution.py:136
  383.3 12.0 %collective-permute-done.31 = bf16[2432,128]{1,0:T(8,128)(2,1)S(1)} collective-permute-done((bf16[2432,128]{1,0:T(8,128)(2,1)S(1)}, bf16[2432,128]{1,0:T(8,128)(2,1)S(1)}, u32[]{:S(2)}, u32[]{:S(2)}) %collective-permute-start.31) | collective-permute-done | bytes 622624 | tf_op jit(solution)/shard_map/ppermute | solution.py:136
  400.5 10.1 %collective-permute-done.32 = bf16[1216,128]{1,0:T(8,128)(2,1)S(1)} collective-permute-done((bf16[1216,128]{1,0:T(8,128)(2,1)S(1)}, bf16[1216,128]{1,0:T(8,128)(2,1)S(1)}, u32[]{:S(2)}, u32[]{:S(2)}) %collective-permute-start.32) | collective-permute-done | bytes 311328 | tf_op jit(solution)/shard_map/ppermute | solution.py:136
  410.9 6.4 %collective-permute-start.51 = (bf16[1200,128]{1,0:T(8,128)(2,1)S(1)}, bf16[1200,128]{1,0:T(8,128)(2,1)S(1)}, u32[]{:S(2)}, u32[]{:S(2)}) collective-permute-start(bf16[1200,128]{1,0:T(8,128)(2,1)S(1)} %maximum_select_fusion.10), channel_id=1, source_target_pairs={{0,8},{2,10},{4,12},{6,14},{8,0},{10,2},{12,4},{14,6},{16,24},{18,... | collective-permute-start | bytes 921608 | tf_op jit(solution)/shard_map/ppermute | solution.py:136
  446.6 12.0 %collective-permute-done.36 = bf16[2432,128]{1,0:T(8,128)(2,1)S(1)} collective-permute-done((bf16[2432,128]{1,0:T(8,128)(2,1)S(1)}, bf16[2432,128]{1,0:T(8,128)(2,1)S(1)}, u32[]{:S(2)}, u32[]{:S(2)}) %collective-permute-start.36) | collective-permute-done | bytes 622624 | tf_op jit(solution)/shard_map/ppermute | solution.py:136
  459.0 10.3 %collective-permute-done.44 = bf16[2400,128]{1,0:T(8,128)(2,1)S(1)} collective-permute-done((bf16[2400,128]{1,0:T(8,128)(2,1)S(1)}, bf16[2400,128]{1,0:T(8,128)(2,1)S(1)}, u32[]{:S(2)}, u32[]{:S(2)}) %collective-permute-start.44) | collective-permute-done | bytes 614432 | tf_op jit(solution)/shard_map/ppermute | solution.py:136
  470.6 6.3 %convolution_add_fusion = f32[256,960]{0,1:T(8,128)} fusion(f32[256,960]{0,1:T(8,128)S(1)} %copy-done.4, bf16[256,2560]{1,0:T(8,128)(2,1)} %get-tuple-element.106, bf16[2560,960]{1,0:T(8,128)(2,1)} %bitcast.471), kind=kOutput, calls=%fused_computation.97 | convolution fusion | flops 1258536960 | bytes 8192000 | tf_op jit(solution)/shard_map/dot_general | solution.py:377
  479.5 15.2 %shard_map.177 = (f32[38400,128]{1,0:T(8,128)}, f32[38400,128]{1,0:T(8,128)}, f32[38400,128]{1,0:T(8,128)}, f32[38400,128]{1,0:T(8,128)}, f32[8,128]{1,0:T(8,128)}) custom-call(s32[1]{0:T(128)} %bitcast.103.refs_0_, f32[38400,128]{1,0:T(8,128)} %bitcast.452, f32[38400,128]{1,0:T(8,128)} %bitcast.456, f32[38400,128]{1,0:T(8,128)} %bitcast.460, ...), custom_call_target="tpu_custom_call" | custom-call | flops 24576000 | bytes 39321600 | tf_op jit(solution)/shard_map/pallas_call | solution.py:252
  494.7 15.5 %shard_map.178 = (f32[38400,128]{1,0:T(8,128)}, f32[38400,128]{1,0:T(8,128)}, f32[38400,128]{1,0:T(8,128)}, f32[38400,128]{1,0:T(8,128)}, f32[8,128]{1,0:T(8,128)}) custom-call(s32[1]{0:T(128)} %bitcast.103.refs_0_, f32[38400,128]{1,0:T(8,128)} %bitcast.453, ...), custom_call_target="tpu_custom_call", output_to_operand_aliasing={{0}: (6, {}), {1}: (7, {}), {2}: (8, {}), {3}: (9, {})} | custom-call | flops 24576000 | bytes 39321600 | tf_op jit(solution)/shard_map/pallas_call | solution.py:252
  510.3 15.5 %shard_map.179 = (f32[38400,128]{1,0:T(8,128)}, f32[38400,128]{1,0:T(8,128)}, f32[38400,128]{1,0:T(8,128)}, f32[38400,128]{1,0:T(8,128)}, f32[8,128]{1,0:T(8,128)}) custom-call(s32[1]{0:T(128)} %bitcast.103.refs_0_, f32[38400,128]{1,0:T(8,128)} %bitcast.454, ...), custom_call_target="tpu_custom_call", output_to_operand_aliasing={{0}: (6, {}), {1}: (7, {}), {2}: (8, {}), {3}: (9, {})} | custom-call | flops 24576000 | bytes 39321600 | tf_op jit(solution)/shard_map/pallas_call | solution.py:252
  527.3 15.1 %shard_map.180 = (f32[38400,128]{1,0:T(8,128)}, f32[38400,128]{1,0:T(8,128)}, f32[38400,128]{1,0:T(8,128)}, f32[38400,128]{1,0:T(8,128)}, f32[8,128]{1,0:T(8,128)}) custom-call(s32[1]{0:T(128)} %bitcast.103.refs_0_, f32[38400,128]{1,0:T(8,128)} %bitcast.455, ...), custom_call_target="tpu_custom_call", output_to_operand_aliasing={{0}: (6, {}), {1}: (7, {}), {2}: (8, {}), {3}: (9, {})} | custom-call | flops 24576000 | bytes 39321600 | tf_op jit(solution)/shard_map/pallas_call | solution.py:252
  (416 shorter events, 267.6 us)
Async XLA Ops:
  1.3 53.9 %collective-permute-start = (bf16[2,480]{1,0:T(2,128)(2,1)S(1)}, bf16[2,480]{1,0:T(2,128)(2,1)S(1)}, u32[]{:S(2)}, u32[]{:S(2)}) collective-permute-start(bf16[2,480]{1,0:T(2,128)(2,1)S(1)} %convert_element_type.426), channel_id=1, source_target_pairs={{0,1},{1,0},{2,3},{3,2},{4,5},{5,4},{6,7},{7,6},{8,9},{9,8},{10,11... | collective-permute-start | bytes 5768 | tf_op jit(solution)/shard_map/ppermute | solution.py:132
  8.2 30.5 %collective-permute-start.1 = (bf16[1,120,1600]{2,1,0:T(8,128)(2,1)}, bf16[1,120,1600]{2,1,0:T(8,128)(2,1)}, u32[]{:S(2)}, u32[]{:S(2)}) collective-permute-start(bf16[1,120,1600]{2,1,0:T(8,128)(2,1)} %concatenate.182), channel_id=1, source_target_pairs={{0,1},{1,0},{2,3},{3,2},{4,5},{5,4},{6,7},{7,6},{8,9},{9,8},{10,11... | collective-permute-start | bytes 1152008 | tf_op jit(solution)/shard_map/ppermute | solution.py:132
  9.1 29.5 %collective-permute-start.2 = (bf16[1,120,960]{2,1,0:T(8,128)(2,1)}, bf16[1,120,960]{2,1,0:T(8,128)(2,1)}, u32[]{:S(2)}, u32[]{:S(2)}) collective-permute-start(bf16[1,120,960]{2,1,0:T(8,128)(2,1)} %reshape.521), channel_id=1, source_target_pairs={{0,1},{1,0},{2,3},{3,2},{4,5},{5,4},{6,7},{7,6},{8,9},{9,8},{10,11... | collective-permute-start | bytes 691208 | tf_op jit(solution)/shard_map/ppermute | solution.py:132
  16.7 35.6 %collective-permute-start.3 = (bf16[1,120,5120]{2,1,0:T(8,128)(2,1)}, bf16[1,120,5120]{2,1,0:T(8,128)(2,1)}, u32[]{:S(2)}, u32[]{:S(2)}) collective-permute-start(bf16[1,120,5120]{2,1,0:T(8,128)(2,1)} %pad_maximum_fusion.4), channel_id=1, source_target_pairs={{0,1},{1,0},{2,3},{3,2},{4,5},{5,4},{6,7},{7,6},{8,9},{9,8},{10,11... | collective-permute-start | bytes 3686408 | tf_op jit(solution)/shard_map/ppermute | solution.py:132
  16.7 130.7 %collective-permute-start.11 = (bf16[256,960]{0,1:T(8,128)(2,1)}, bf16[256,960]{0,1:T(8,128)(2,1)}, u32[]{:S(2)}, u32[]{:S(2)}) collective-permute-start(bf16[256,960]{0,1:T(8,128)(2,1)} %param.11), channel_id=1, source_target_pairs={{0,1},{1,0},{2,3},{3,2},{4,5},{5,4},{6,7},{7,6},{8,9},{9,8},{10,11... | collective-permute-start | bytes 1474568 | tf_op jit(solution)/shard_map/ppermute | solution.py:132
  38.6 36.8 %collective-permute-start.16 = (bf16[1,320,960]{2,1,0:T(8,128)(2,1)}, bf16[1,320,960]{2,1,0:T(8,128)(2,1)}, u32[]{:S(2)}, u32[]{:S(2)}) collective-permute-start(bf16[1,320,960]{2,1,0:T(8,128)(2,1)} %reshape.533), channel_id=1, source_target_pairs={{0,1},{1,0},{2,3},{3,2},{4,5},{5,4},{6,7},{7,6},{8,9},{9,8},{10,11... | collective-permute-start | bytes 1843208 | tf_op jit(solution)/shard_map/ppermute | solution.py:132
  52.3 42.4 %collective-permute-start.6 = (bf16[1,120,5120]{2,1,0:T(8,128)(2,1)}, bf16[1,120,5120]{2,1,0:T(8,128)(2,1)}, u32[]{:S(2)}, u32[]{:S(2)}) collective-permute-start(bf16[1,120,5120]{2,1,0:T(8,128)(2,1)} %collective-permute-done.3), channel_id=1, source_target_pairs={{0,4},{2,6},{4,0},{6,2},{8,12},{10,14},{12,8},{14,10},{16,20},{18,... | collective-permute-start | bytes 3686408 | tf_op jit(solution)/shard_map/ppermute | solution.py:136
  55.6 39.1 %collective-permute-start.4 = (bf16[1,120,1600]{2,1,0:T(8,128)(2,1)}, bf16[1,120,1600]{2,1,0:T(8,128)(2,1)}, u32[]{:S(2)}, u32[]{:S(2)}) collective-permute-start(bf16[1,120,1600]{2,1,0:T(8,128)(2,1)} %collective-permute-done.1), channel_id=1, source_target_pairs={{0,4},{2,6},{4,0},{6,2},{8,12},{10,14},{12,8},{14,10},{16,20},{18,... | collective-permute-start | bytes 1152008 | tf_op jit(solution)/shard_map/ppermute | solution.py:136
  57.0 36.2 %collective-permute-start.5 = (bf16[1,120,960]{2,1,0:T(8,128)(2,1)}, bf16[1,120,960]{2,1,0:T(8,128)(2,1)S(1)}, u32[]{:S(2)}, u32[]{:S(2)}) collective-permute-start(bf16[1,120,960]{2,1,0:T(8,128)(2,1)} %collective-permute-done.2), channel_id=1, source_target_pairs={{0,4},{2,6},{4,0},{6,2},{8,12},{10,14},{12,8},{14,10},{16,20},{18,... | collective-permute-start | bytes 691208 | tf_op jit(solution)/shard_map/ppermute | solution.py:136
  75.4 72.0 %collective-permute-start.10 = (bf16[256,480]{0,1:T(8,128)(2,1)}, bf16[256,480]{0,1:T(8,128)(2,1)}, u32[]{:S(2)}, u32[]{:S(2)}) collective-permute-start(bf16[256,480]{0,1:T(8,128)(2,1)} %get-tuple-element.120), channel_id=1, source_target_pairs={{0,1},{1,0},{2,3},{3,2},{4,5},{5,4},{6,7},{7,6},{8,9},{9,8},{10,11... | collective-permute-start | bytes 737288 | tf_op jit(solution)/shard_map/ppermute | solution.py:132
  162.9 31.9 %collective-permute-start.22 = (bf16[256,2560]{1,0:T(8,128)(2,1)}, bf16[256,2560]{1,0:T(8,128)(2,1)S(1)}, u32[]{:S(2)}, u32[]{:S(2)}) collective-permute-start(bf16[256,2560]{1,0:T(8,128)(2,1)} %get-tuple-element.104), channel_id=1, source_target_pairs={{0,1},{1,0},{2,3},{3,2},{4,5},{5,4},{6,7},{7,6},{8,9},{9,8},{10,11... | collective-permute-start | bytes 3932168 | tf_op jit(solution)/shard_map/ppermute | solution.py:132
  173.9 83.6 %collective-permute-start.24 = (bf16[256,2560]{1,0:T(8,128)(2,1)}, bf16[256,2560]{1,0:T(8,128)(2,1)}, u32[]{:S(2)}, u32[]{:S(2)}) collective-permute-start(bf16[256,2560]{1,0:T(8,128)(2,1)} %get-tuple-element.105), channel_id=1, source_target_pairs={{0,1},{1,0},{2,3},{3,2},{4,5},{5,4},{6,7},{7,6},{8,9},{9,8},{10,11... | collective-permute-start | bytes 3932168 | tf_op jit(solution)/shard_map/ppermute | solution.py:132
  175.4 58.1 %collective-permute-start.29 = (bf16[256,960]{0,1:T(8,128)(2,1)}, bf16[256,960]{0,1:T(8,128)(2,1)}, u32[]{:S(2)}, u32[]{:S(2)}) collective-permute-start(bf16[256,960]{0,1:T(8,128)(2,1)} %fusion.129), channel_id=1, source_target_pairs={{0,1},{1,0},{2,3},{3,2},{4,5},{5,4},{6,7},{7,6},{8,9},{9,8},{10,11... | collective-permute-start | bytes 1474568 | tf_op jit(solution)/shard_map/ppermute | solution.py:132
  183.3 74.2 %collective-permute-start.25 = (bf16[256,1280]{1,0:T(8,128)(2,1)}, bf16[256,1280]{1,0:T(8,128)(2,1)}, u32[]{:S(2)}, u32[]{:S(2)}) collective-permute-start(bf16[256,1280]{1,0:T(8,128)(2,1)} %get-tuple-element.110), channel_id=1, source_target_pairs={{0,1},{1,0},{2,3},{3,2},{4,5},{5,4},{6,7},{7,6},{8,9},{9,8},{10,11... | collective-permute-start | bytes 1966088 | tf_op jit(solution)/shard_map/ppermute | solution.py:132
  194.9 57.5 %collective-permute-start.23 = (bf16[256,640]{0,1:T(8,128)(2,1)S(1)}, bf16[256,640]{0,1:T(8,128)(2,1)}, u32[]{:S(2)}, u32[]{:S(2)}) collective-permute-start(bf16[256,640]{0,1:T(8,128)(2,1)S(1)} %slice.543), channel_id=1, source_target_pairs={{0,1},{1,0},{2,3},{3,2},{4,5},{5,4},{6,7},{7,6},{8,9},{9,8},{10,11... | collective-permute-start | bytes 983048 | tf_op jit(solution)/shard_map/ppermute | solution.py:132
  205.3 49.4 %collective-permute-start.26 = (bf16[4800,128]{1,0:T(8,128)(2,1)}, bf16[4800,128]{1,0:T(8,128)(2,1)}, u32[]{:S(2)}, u32[]{:S(2)}) collective-permute-start(bf16[4800,128]{1,0:T(8,128)(2,1)} %dynamic-slice_bitcast_fusion.3), channel_id=1, source_target_pairs={{0,2},{2,0},{4,6},{6,4},{8,10},{10,8},{12,14},{14,12},{16,18},{18,... | collective-permute-start | bytes 3686408 | tf_op jit(solution)/shard_map/ppermute | solution.py:136
  260.8 48.5 %collective-permute-start.27 = (bf16[256,1600]{0,1:T(8,128)(2,1)}, bf16[256,1600]{0,1:T(8,128)(2,1)}, u32[]{:S(2)}, u32[]{:S(2)}) collective-permute-start(bf16[256,1600]{0,1:T(8,128)(2,1)} %pad_maximum_fusion.5), channel_id=1, source_target_pairs={{0,1},{1,0},{2,3},{3,2},{4,5},{5,4},{6,7},{7,6},{8,9},{9,8},{10,11... | collective-permute-start | bytes 2457608 | tf_op jit(solution)/shard_map/ppermute | solution.py:132
  276.5 61.6 %collective-permute-start.38 = (bf16[4800,128]{1,0:T(8,128)(2,1)}, bf16[4800,128]{1,0:T(8,128)(2,1)}, u32[]{:S(2)}, u32[]{:S(2)}) collective-permute-start(bf16[4800,128]{1,0:T(8,128)(2,1)} %dynamic-slice_bitcast_fusion.2), channel_id=1, source_target_pairs={{0,2},{2,0},{4,6},{6,4},{8,10},{10,8},{12,14},{14,12},{16,18},{18,... | collective-permute-start | bytes 3686408 | tf_op jit(solution)/shard_map/ppermute | solution.py:136
  290.0 57.2 %collective-permute-start.46 = (bf16[4800,128]{1,0:T(8,128)(2,1)}, bf16[4800,128]{1,0:T(8,128)(2,1)}, u32[]{:S(2)}, u32[]{:S(2)}) collective-permute-start(bf16[4800,128]{1,0:T(8,128)(2,1)} %dynamic-slice_bitcast_fusion.1), channel_id=1, source_target_pairs={{0,2},{2,0},{4,6},{6,4},{8,10},{10,8},{12,14},{14,12},{16,18},{18,... | collective-permute-start | bytes 3686408 | tf_op jit(solution)/shard_map/ppermute | solution.py:136
  332.5 40.7 %collective-permute-start.30 = (bf16[4864,128]{1,0:T(8,128)(2,1)S(1)}, bf16[4864,128]{1,0:T(8,128)(2,1)S(1)}, u32[]{:S(2)}, u32[]{:S(2)}) collective-permute-start(bf16[4864,128]{1,0:T(8,128)(2,1)S(1)} %dynamic-slice_bitcast_fusion), channel_id=1, source_target_pairs={{0,2},{2,0},{4,6},{6,4},{8,10},{10,8},{12,14},{14,12},{16,18},{18,... | collective-permute-start | bytes 3735560 | tf_op jit(solution)/shard_map/ppermute | solution.py:136
  383.2 96.3 %collective-permute-start.60 = (bf16[4800,128]{1,0:T(8,128)(2,1)S(1)}, bf16[4800,128]{1,0:T(8,128)(2,1)}, u32[]{:S(2)}, u32[]{:S(2)}) collective-permute-start(bf16[4800,128]{1,0:T(8,128)(2,1)S(1)} %maximum_select_fusion.3.refs_4_), channel_id=1, source_target_pairs={{0,2},{2,0},{4,6},{6,4},{8,10},{10,8},{12,14},{14,12},{16,18},{18,... | collective-permute-start | bytes 3686408 | tf_op jit(solution)/shard_map/ppermute | solution.py:136
  446.6 48.1 %collective-permute-start.53 = (bf16[4800,128]{1,0:T(8,128)(2,1)}, bf16[4800,128]{1,0:T(8,128)(2,1)}, u32[]{:S(2)}, u32[]{:S(2)}) collective-permute-start(bf16[4800,128]{1,0:T(8,128)(2,1)} %maximum_select_fusion.2.refs_4_), channel_id=1, source_target_pairs={{0,2},{2,0},{4,6},{6,4},{8,10},{10,8},{12,14},{14,12},{16,18},{18,... | collective-permute-start | bytes 3686408 | tf_op jit(solution)/shard_map/ppermute | solution.py:136
  458.9 66.9 %collective-permute-start.37 = (bf16[4864,128]{1,0:T(8,128)(2,1)S(1)}, bf16[4864,128]{1,0:T(8,128)(2,1)}, u32[]{:S(2)}, u32[]{:S(2)}) collective-permute-start(bf16[4864,128]{1,0:T(8,128)(2,1)S(1)} %maximum_select_fusion.refs_4_), channel_id=1, source_target_pairs={{0,2},{2,0},{4,6},{6,4},{8,10},{10,8},{12,14},{14,12},{16,18},{18,... | collective-permute-start | bytes 3735560 | tf_op jit(solution)/shard_map/ppermute | solution.py:136
  470.6 39.6 %collective-permute-start.45 = (bf16[4800,128]{1,0:T(8,128)(2,1)}, bf16[4800,128]{1,0:T(8,128)(2,1)}, u32[]{:S(2)}, u32[]{:S(2)}) collective-permute-start(bf16[4800,128]{1,0:T(8,128)(2,1)} %maximum_select_fusion.1.refs_4_), channel_id=1, source_target_pairs={{0,2},{2,0},{4,6},{6,4},{8,10},{10,8},{12,14},{14,12},{16,18},{18,... | collective-permute-start | bytes 3686408 | tf_op jit(solution)/shard_map/ppermute | solution.py:136
  (82 other events, 903.6 us)

commit v5 on v4

--- a/solution.py
+++ b/solution.py
@@ -465,10 +465,10 @@
     rates = matrix_rates(longest)
     state = [values.reshape(-1, 128) for values in (params, first_moment, second_moment)]
     *updated, mark = update_chunk(state, gate_sum, bit, 1, (rates[4], rates[4]), 0, ())
-    attn_part, mark = lax.optimization_barrier((attn_part, mark))
+    attn_part = attn_part + mark[:1].astype(low_type)
     attn_piece = gather_steps(attn_part, replica_count // 2, 4)
     *updated, mark = update_chunk(state, up_sum, bit, 2, (rates[5], rates[5]), 0, updated)
-    attn_piece, mark = lax.optimization_barrier((attn_piece, mark))
+    attn_piece = attn_piece + mark[:1].astype(low_type)
     attn_piece = gather_steps(attn_piece, 2, 2)
     attn_sum = (attn_piece, swap_replicas(attn_piece, 1))
     *updated, mark = update_chunk(state, down_sum, bit, 3, (rates[6], rates[6]), 0, updated)

time: 548 us -> 521 us (0.951)
  starting transfers between devices: 62.8 us -> 54.2 us
  local copies, waits for them, and re-layouts: 98.3 us -> 90.4 us
    ppermute x44, starting transfers between devices: 46.1 us -> 37.5 us  [swap_replicas(): lax.ppermute(values, 'dp', [(index, index ^ distance) for index in range(...]
    unnamed x97 -> x105, local copies, waits for them, and re-layouts: 13.3 us -> 9.43 us
    another operation x7 -> x9, other arithmetic: 15.7 us -> 15.7 us
  transfers between devices with their start and end apart: 61 -> 61, of which waited for: 23 -> 22; matrix products, arithmetic and copies ran while one was open for 37% -> 36% of each run, Pallas kernels for 9% -> 8%
where the time goes in v5:
time: 521 us; the launch traced here: 516 us
  waiting for transfers between devices  201 us (39%)
  local copies, waits for them, and re-layouts  90.4 us (17%)
  Pallas kernels  58.5 us (11%)
  matrix products  56.5 us (11%)
  starting transfers between devices  54.2 us (10%)
  other arithmetic  52.5 us (10%)
    ppermute x44, waiting for transfers between devices, swap_replicas(): lax.ppermute(values, 'dp', [(index, index ^ distance) for index in range(...  125 us
    ppermute x17, waiting for transfers between devices, swap_shards(): return lax.ppermute(values, 'cp', [(0, 1), (1, 0)])  76.7 us
    pallas_call x4, Pallas kernels, update_chunk(): pl.pallas_call(lambda *refs: update_kernel(rates[0], rates[1], split, *re...  58.5 us
    ppermute x44, starting transfers between devices, swap_replicas(): lax.ppermute(values, 'dp', [(index, index ^ distance) for index in range(...  37.5 us
    dot_general x5, matrix products, owned_product(): jnp.dot(left.T, right, preferred_element_type=jnp.float32)  18.4 us
    ppermute x17, starting transfers between devices, swap_shards(): return lax.ppermute(values, 'cp', [(0, 1), (1, 0)])  16.7 us
    another operation x9, other arithmetic  15.7 us
    convert_element_type x7, local copies, waits for them, and re-layouts, own_rows(): params[offset:offset + rows * width].astype(jnp.bfloat16)  14.8 us
  transfers between devices with their start and end apart: 61, of which 22 were waited for; matrix products, arithmetic and copies ran while one was open for 36% of the time, Pallas kernels for 8%

profile of v5, /device:TPU:0, one launch (start us, length us, event | category | flops | bytes accessed | tf_op | source)
XLA Modules:
  0.0 516.0 jit_solution(34278273028696415)
XLA Ops:
  18.7 7.7 %convert.73 = bf16[4915200]{0:T(1024)(128)(2,1)S(1)} convert(f32[4915200]{0:T(1024)} %param.14) | non-fusion elementwise | flops 4915200 | bytes 29491200 | tf_op jit(solution)/shard_map/convert.40
  38.7 13.6 %collective-permute-done.3 = bf16[1,120,5120]{2,1,0:T(8,128)(2,1)} collective-permute-done((bf16[1,120,5120]{2,1,0:T(8,128)(2,1)}, bf16[1,120,5120]{2,1,0:T(8,128)(2,1)}, u32[]{:S(2)}, u32[]{:S(2)}) %collective-permute-start.3) | collective-permute-done | bytes 1228832 | tf_op jit(solution)/shard_map/ppermute | solution.py:132
  68.2 7.2 %collective-permute-done.16 = bf16[1,320,960]{2,1,0:T(8,128)(2,1)} collective-permute-done((bf16[1,320,960]{2,1,0:T(8,128)(2,1)}, bf16[1,320,960]{2,1,0:T(8,128)(2,1)}, u32[]{:S(2)}, u32[]{:S(2)}) %collective-permute-start.16) | collective-permute-done | bytes 614432 | tf_op jit(solution)/shard_map/ppermute | solution.py:132
  75.7 17.5 %collective-permute-done.5 = bf16[1,120,960]{2,1,0:T(8,128)(2,1)S(1)} collective-permute-done((bf16[1,120,960]{2,1,0:T(8,128)(2,1)}, bf16[1,120,960]{2,1,0:T(8,128)(2,1)S(1)}, u32[]{:S(2)}, u32[]{:S(2)}) %collective-permute-start.5) | collective-permute-done | bytes 230432 | tf_op jit(solution)/shard_map/ppermute | solution.py:136
  95.2 7.4 %convert.80 = bf16[4915200]{0:T(1024)(128)(2,1)S(1)} convert(f32[4915200]{0:T(1024)} %param.14) | non-fusion elementwise | flops 4915200 | bytes 29491200 | tf_op jit(solution)/shard_map/convert.28
  133.4 8.5 %collective-permute-done.9 = bf16[256,640]{0,1:T(8,128)(2,1)S(1)} collective-permute-done((bf16[256,640]{0,1:T(8,128)(2,1)S(1)}, bf16[256,640]{0,1:T(8,128)(2,1)S(1)}, u32[]{:S(2)}, u32[]{:S(2)}) %collective-permute-start.9) | collective-permute-done | bytes 327712 | tf_op jit(solution)/shard_map/ppermute | solution.py:132
  155.5 7.4 %fusion.2 = (bf16[256,2560]{1,0:T(8,128)(2,1)}, bf16[256,2560]{1,0:T(8,128)(2,1)}, bf16[256,2560]{1,0:T(8,128)(2,1)}) fusion(f32[256,5120]{1,0:T(8,128)S(1)} %fusion.149, bf16[2560,960]{1,0:T(8,128)(2,1)} %bitcast.474, bf16[256,960]{0,1:T(8,128)(2,1)} %param.11), kind=kOutput, calls=%fused_computation.12 | convolution fusion | flops 1268776960 | bytes 14581760 | tf_op jit(solution)/shard_map/dot_general | solution.py:378
  187.0 7.9 %collective-permute-done.22 = bf16[256,2560]{1,0:T(8,128)(2,1)S(1)} collective-permute-done((bf16[256,2560]{1,0:T(8,128)(2,1)}, bf16[256,2560]{1,0:T(8,128)(2,1)S(1)}, u32[]{:S(2)}, u32[]{:S(2)}) %collective-permute-start.22) | collective-permute-done | bytes 1310752 | tf_op jit(solution)/shard_map/ppermute | solution.py:132
  206.8 26.8 %collective-permute-done.29 = bf16[256,960]{0,1:T(8,128)(2,1)} collective-permute-done((bf16[256,960]{0,1:T(8,128)(2,1)}, bf16[256,960]{0,1:T(8,128)(2,1)}, u32[]{:S(2)}, u32[]{:S(2)}) %collective-permute-start.29) | collective-permute-done | bytes 491552 | tf_op jit(solution)/shard_map/ppermute | solution.py:132
  239.5 12.8 %collective-permute-done.23 = bf16[256,640]{0,1:T(8,128)(2,1)} collective-permute-done((bf16[256,640]{0,1:T(8,128)(2,1)S(1)}, bf16[256,640]{0,1:T(8,128)(2,1)}, u32[]{:S(2)}, u32[]{:S(2)}) %collective-permute-start.23) | collective-permute-done | bytes 327712 | tf_op jit(solution)/shard_map/ppermute | solution.py:132
  307.9 7.5 %collective-permute-done.36 = bf16[600,128]{1,0:T(8,128)(2,1)S(1)} collective-permute-done((bf16[600,128]{1,0:T(8,128)(2,1)S(1)}, bf16[600,128]{1,0:T(8,128)(2,1)S(1)}, u32[]{:S(2)}, u32[]{:S(2)}) %collective-permute-start.36) | collective-permute-done | bytes 153632 | tf_op jit(solution)/shard_map/ppermute | solution.py:136
  315.7 9.2 %collective-permute-done.37 = bf16[600,128]{1,0:T(8,128)(2,1)S(1)} collective-permute-done((bf16[600,128]{1,0:T(8,128)(2,1)S(1)}, bf16[600,128]{1,0:T(8,128)(2,1)S(1)}, u32[]{:S(2)}, u32[]{:S(2)}) %collective-permute-start.37) | collective-permute-done | bytes 153632 | tf_op jit(solution)/shard_map/ppermute | solution.py:136
  336.1 7.7 %collective-permute-done.44 = bf16[2400,128]{1,0:T(8,128)(2,1)S(1)} collective-permute-done((bf16[2400,128]{1,0:T(8,128)(2,1)S(1)}, bf16[2400,128]{1,0:T(8,128)(2,1)S(1)}, u32[]{:S(2)}, u32[]{:S(2)}) %collective-permute-start.44) | collective-permute-done | bytes 614432 | tf_op jit(solution)/shard_map/ppermute | solution.py:136
  345.9 11.0 %collective-permute-done.54 = bf16[2400,128]{1,0:T(8,128)(2,1)S(1)} collective-permute-done((bf16[2400,128]{1,0:T(8,128)(2,1)S(1)}, bf16[2400,128]{1,0:T(8,128)(2,1)S(1)}, u32[]{:S(2)}, u32[]{:S(2)}) %collective-permute-start.54) | collective-permute-done | bytes 614432 | tf_op jit(solution)/shard_map/ppermute | solution.py:136
  376.1 6.4 %collective-permute-done.31 = bf16[2432,128]{1,0:T(8,128)(2,1)S(1)} collective-permute-done((bf16[2432,128]{1,0:T(8,128)(2,1)S(1)}, bf16[2432,128]{1,0:T(8,128)(2,1)S(1)}, u32[]{:S(2)}, u32[]{:S(2)}) %collective-permute-start.31) | collective-permute-done | bytes 622624 | tf_op jit(solution)/shard_map/ppermute | solution.py:136
  387.1 7.4 %collective-permute-done.32 = bf16[1216,128]{1,0:T(8,128)(2,1)S(1)} collective-permute-done((bf16[1216,128]{1,0:T(8,128)(2,1)S(1)}, bf16[1216,128]{1,0:T(8,128)(2,1)S(1)}, u32[]{:S(2)}, u32[]{:S(2)}) %collective-permute-start.32) | collective-permute-done | bytes 311328 | tf_op jit(solution)/shard_map/ppermute | solution.py:136
  400.6 14.0 %shard_map.177 = (f32[38400,128]{1,0:T(8,128)}, f32[38400,128]{1,0:T(8,128)}, f32[38400,128]{1,0:T(8,128)}, f32[38400,128]{1,0:T(8,128)}, f32[8,128]{1,0:T(8,128)S(1)}) custom-call(s32[1]{0:T(128)} %bitcast.103.refs_0_, f32[38400,128]{1,0:T(8,128)} %bitcast.456, f32[38400,128]{1,0:T(8,128)} %bitcast.460, f32[38400,128]{1,0:T(8,128)} %bitcast.464, ...), custom_call_target="tpu_custom_call" | custom-call | flops 24576000 | bytes 39321600 | tf_op jit(solution)/shard_map/pallas_call | solution.py:252
  417.8 11.3 %collective-permute-done.41 = bf16[608,128]{1,0:T(8,128)(2,1)S(1)} collective-permute-done((bf16[608,128]{1,0:T(8,128)(2,1)S(1)}, bf16[608,128]{1,0:T(8,128)(2,1)S(1)}, u32[]{:S(2)}, u32[]{:S(2)}) %collective-permute-start.41) | collective-permute-done | bytes 155680 | tf_op jit(solution)/shard_map/ppermute | solution.py:136
  431.9 14.1 %shard_map.178 = (f32[38400,128]{1,0:T(8,128)}, f32[38400,128]{1,0:T(8,128)}, f32[38400,128]{1,0:T(8,128)}, f32[38400,128]{1,0:T(8,128)}, f32[8,128]{1,0:T(8,128)S(1)}) custom-call(s32[1]{0:T(128)} %bitcast.103.refs_0_, f32[38400,128]{1,0:T(8,128)} %bitcast.457, ...), custom_call_target="tpu_custom_call", output_to_operand_aliasing={{0}: (6, {}), {1}: (7, {}), {2}: (8, {}), {3}: (9, {})} | custom-call | flops 24576000 | bytes 39321600 | tf_op jit(solution)/shard_map/pallas_call | solution.py:252
  448.7 14.7 %collective-permute-done.51 = bf16[2432,128]{1,0:T(8,128)(2,1)S(1)} collective-permute-done((bf16[2432,128]{1,0:T(8,128)(2,1)S(1)}, bf16[2432,128]{1,0:T(8,128)(2,1)S(1)}, u32[]{:S(2)}, u32[]{:S(2)}) %collective-permute-start.51) | collective-permute-done | bytes 622624 | tf_op jit(solution)/shard_map/ppermute | solution.py:136
  463.8 11.0 %collective-permute-done.59 = bf16[2400,128]{1,0:T(8,128)(2,1)S(1)} collective-permute-done((bf16[2400,128]{1,0:T(8,128)(2,1)S(1)}, bf16[2400,128]{1,0:T(8,128)(2,1)S(1)}, u32[]{:S(2)}, u32[]{:S(2)}) %collective-permute-start.59) | collective-permute-done | bytes 614432 | tf_op jit(solution)/shard_map/ppermute | solution.py:136
  475.2 6.1 %convolution_add_fusion = f32[256,960]{0,1:T(8,128)} fusion(f32[256,960]{0,1:T(8,128)S(1)} %copy-done.6, bf16[256,2560]{1,0:T(8,128)(2,1)} %get-tuple-element.110, bf16[2560,960]{1,0:T(8,128)(2,1)} %bitcast.475), kind=kOutput, calls=%fused_computation.97 | convolution fusion | flops 1258536960 | bytes 8192000 | tf_op jit(solution)/shard_map/dot_general | solution.py:377
  483.9 15.2 %shard_map.179 = (f32[38400,128]{1,0:T(8,128)}, f32[38400,128]{1,0:T(8,128)}, f32[38400,128]{1,0:T(8,128)}, f32[38400,128]{1,0:T(8,128)}, f32[8,128]{1,0:T(8,128)}) custom-call(s32[1]{0:T(128)} %bitcast.103.refs_0_, f32[38400,128]{1,0:T(8,128)} %bitcast.458, ...), custom_call_target="tpu_custom_call", output_to_operand_aliasing={{0}: (6, {}), {1}: (7, {}), {2}: (8, {}), {3}: (9, {})} | custom-call | flops 24576000 | bytes 39321600 | tf_op jit(solution)/shard_map/pallas_call | solution.py:252
  500.6 15.1 %shard_map.180 = (f32[38400,128]{1,0:T(8,128)}, f32[38400,128]{1,0:T(8,128)}, f32[38400,128]{1,0:T(8,128)}, f32[38400,128]{1,0:T(8,128)}, f32[8,128]{1,0:T(8,128)}) custom-call(s32[1]{0:T(128)} %bitcast.103.refs_0_, f32[38400,128]{1,0:T(8,128)} %bitcast.459, ...), custom_call_target="tpu_custom_call", output_to_operand_aliasing={{0}: (6, {}), {1}: (7, {}), {2}: (8, {}), {3}: (9, {})} | custom-call | flops 24576000 | bytes 39321600 | tf_op jit(solution)/shard_map/pallas_call | solution.py:252
  (428 shorter events, 246.1 us)
Async XLA Ops:
  1.3 53.9 %collective-permute-start = (bf16[2,480]{1,0:T(2,128)(2,1)S(1)}, bf16[2,480]{1,0:T(2,128)(2,1)S(1)}, u32[]{:S(2)}, u32[]{:S(2)}) collective-permute-start(bf16[2,480]{1,0:T(2,128)(2,1)S(1)} %convert_element_type.428), channel_id=1, source_target_pairs={{0,1},{1,0},{2,3},{3,2},{4,5},{5,4},{6,7},{7,6},{8,9},{9,8},{10,11... | collective-permute-start | bytes 5768 | tf_op jit(solution)/shard_map/ppermute | solution.py:132
  8.2 30.5 %collective-permute-start.1 = (bf16[1,120,1600]{2,1,0:T(8,128)(2,1)}, bf16[1,120,1600]{2,1,0:T(8,128)(2,1)}, u32[]{:S(2)}, u32[]{:S(2)}) collective-permute-start(bf16[1,120,1600]{2,1,0:T(8,128)(2,1)} %concatenate.182), channel_id=1, source_target_pairs={{0,1},{1,0},{2,3},{3,2},{4,5},{5,4},{6,7},{7,6},{8,9},{9,8},{10,11... | collective-permute-start | bytes 1152008 | tf_op jit(solution)/shard_map/ppermute | solution.py:132
  16.7 35.6 %collective-permute-start.3 = (bf16[1,120,5120]{2,1,0:T(8,128)(2,1)}, bf16[1,120,5120]{2,1,0:T(8,128)(2,1)}, u32[]{:S(2)}, u32[]{:S(2)}) collective-permute-start(bf16[1,120,5120]{2,1,0:T(8,128)(2,1)} %pad_maximum_fusion.4), channel_id=1, source_target_pairs={{0,1},{1,0},{2,3},{3,2},{4,5},{5,4},{6,7},{7,6},{8,9},{9,8},{10,11... | collective-permute-start | bytes 3686408 | tf_op jit(solution)/shard_map/ppermute | solution.py:132
  16.7 130.7 %collective-permute-start.11 = (bf16[256,960]{0,1:T(8,128)(2,1)}, bf16[256,960]{0,1:T(8,128)(2,1)}, u32[]{:S(2)}, u32[]{:S(2)}) collective-permute-start(bf16[256,960]{0,1:T(8,128)(2,1)} %param.11), channel_id=1, source_target_pairs={{0,1},{1,0},{2,3},{3,2},{4,5},{5,4},{6,7},{7,6},{8,9},{9,8},{10,11... | collective-permute-start | bytes 1474568 | tf_op jit(solution)/shard_map/ppermute | solution.py:132
  38.6 36.8 %collective-permute-start.16 = (bf16[1,320,960]{2,1,0:T(8,128)(2,1)}, bf16[1,320,960]{2,1,0:T(8,128)(2,1)}, u32[]{:S(2)}, u32[]{:S(2)}) collective-permute-start(bf16[1,320,960]{2,1,0:T(8,128)(2,1)} %reshape.533), channel_id=1, source_target_pairs={{0,1},{1,0},{2,3},{3,2},{4,5},{5,4},{6,7},{7,6},{8,9},{9,8},{10,11... | collective-permute-start | bytes 1843208 | tf_op jit(solution)/shard_map/ppermute | solution.py:132
  52.3 42.4 %collective-permute-start.6 = (bf16[1,120,5120]{2,1,0:T(8,128)(2,1)}, bf16[1,120,5120]{2,1,0:T(8,128)(2,1)}, u32[]{:S(2)}, u32[]{:S(2)}) collective-permute-start(bf16[1,120,5120]{2,1,0:T(8,128)(2,1)} %collective-permute-done.3), channel_id=1, source_target_pairs={{0,4},{2,6},{4,0},{6,2},{8,12},{10,14},{12,8},{14,10},{16,20},{18,... | collective-permute-start | bytes 3686408 | tf_op jit(solution)/shard_map/ppermute | solution.py:136
  55.6 39.1 %collective-permute-start.4 = (bf16[1,120,1600]{2,1,0:T(8,128)(2,1)}, bf16[1,120,1600]{2,1,0:T(8,128)(2,1)}, u32[]{:S(2)}, u32[]{:S(2)}) collective-permute-start(bf16[1,120,1600]{2,1,0:T(8,128)(2,1)} %collective-permute-done.1), channel_id=1, source_target_pairs={{0,4},{2,6},{4,0},{6,2},{8,12},{10,14},{12,8},{14,10},{16,20},{18,... | collective-permute-start | bytes 1152008 | tf_op jit(solution)/shard_map/ppermute | solution.py:136
  57.0 36.2 %collective-permute-start.5 = (bf16[1,120,960]{2,1,0:T(8,128)(2,1)}, bf16[1,120,960]{2,1,0:T(8,128)(2,1)S(1)}, u32[]{:S(2)}, u32[]{:S(2)}) collective-permute-start(bf16[1,120,960]{2,1,0:T(8,128)(2,1)} %collective-permute-done.2), channel_id=1, source_target_pairs={{0,4},{2,6},{4,0},{6,2},{8,12},{10,14},{12,8},{14,10},{16,20},{18,... | collective-permute-start | bytes 691208 | tf_op jit(solution)/shard_map/ppermute | solution.py:136
  75.4 72.0 %collective-permute-start.10 = (bf16[256,480]{0,1:T(8,128)(2,1)}, bf16[256,480]{0,1:T(8,128)(2,1)}, u32[]{:S(2)}, u32[]{:S(2)}) collective-permute-start(bf16[256,480]{0,1:T(8,128)(2,1)} %get-tuple-element.124), channel_id=1, source_target_pairs={{0,1},{1,0},{2,3},{3,2},{4,5},{5,4},{6,7},{7,6},{8,9},{9,8},{10,11... | collective-permute-start | bytes 737288 | tf_op jit(solution)/shard_map/ppermute | solution.py:132
  162.9 31.9 %collective-permute-start.22 = (bf16[256,2560]{1,0:T(8,128)(2,1)}, bf16[256,2560]{1,0:T(8,128)(2,1)S(1)}, u32[]{:S(2)}, u32[]{:S(2)}) collective-permute-start(bf16[256,2560]{1,0:T(8,128)(2,1)} %get-tuple-element.108), channel_id=1, source_target_pairs={{0,1},{1,0},{2,3},{3,2},{4,5},{5,4},{6,7},{7,6},{8,9},{9,8},{10,11... | collective-permute-start | bytes 3932168 | tf_op jit(solution)/shard_map/ppermute | solution.py:132
  173.9 82.5 %collective-permute-start.24 = (bf16[256,2560]{1,0:T(8,128)(2,1)}, bf16[256,2560]{1,0:T(8,128)(2,1)}, u32[]{:S(2)}, u32[]{:S(2)}) collective-permute-start(bf16[256,2560]{1,0:T(8,128)(2,1)} %get-tuple-element.109), channel_id=1, source_target_pairs={{0,1},{1,0},{2,3},{3,2},{4,5},{5,4},{6,7},{7,6},{8,9},{9,8},{10,11... | collective-permute-start | bytes 3932168 | tf_op jit(solution)/shard_map/ppermute | solution.py:132
  175.5 58.1 %collective-permute-start.29 = (bf16[256,960]{0,1:T(8,128)(2,1)}, bf16[256,960]{0,1:T(8,128)(2,1)}, u32[]{:S(2)}, u32[]{:S(2)}) collective-permute-start(bf16[256,960]{0,1:T(8,128)(2,1)} %fusion.131), channel_id=1, source_target_pairs={{0,1},{1,0},{2,3},{3,2},{4,5},{5,4},{6,7},{7,6},{8,9},{9,8},{10,11... | collective-permute-start | bytes 1474568 | tf_op jit(solution)/shard_map/ppermute | solution.py:132
  183.3 73.2 %collective-permute-start.25 = (bf16[256,1280]{1,0:T(8,128)(2,1)}, bf16[256,1280]{1,0:T(8,128)(2,1)}, u32[]{:S(2)}, u32[]{:S(2)}) collective-permute-start(bf16[256,1280]{1,0:T(8,128)(2,1)} %get-tuple-element.114), channel_id=1, source_target_pairs={{0,1},{1,0},{2,3},{3,2},{4,5},{5,4},{6,7},{7,6},{8,9},{9,8},{10,11... | collective-permute-start | bytes 1966088 | tf_op jit(solution)/shard_map/ppermute | solution.py:132
  194.9 57.5 %collective-permute-start.23 = (bf16[256,640]{0,1:T(8,128)(2,1)S(1)}, bf16[256,640]{0,1:T(8,128)(2,1)}, u32[]{:S(2)}, u32[]{:S(2)}) collective-permute-start(bf16[256,640]{0,1:T(8,128)(2,1)S(1)} %slice.555), channel_id=1, source_target_pairs={{0,1},{1,0},{2,3},{3,2},{4,5},{5,4},{6,7},{7,6},{8,9},{9,8},{10,11... | collective-permute-start | bytes 983048 | tf_op jit(solution)/shard_map/ppermute | solution.py:132
  205.3 49.4 %collective-permute-start.26 = (bf16[4800,128]{1,0:T(8,128)(2,1)}, bf16[4800,128]{1,0:T(8,128)(2,1)}, u32[]{:S(2)}, u32[]{:S(2)}) collective-permute-start(bf16[4800,128]{1,0:T(8,128)(2,1)} %dynamic-slice_bitcast_fusion.3), channel_id=1, source_target_pairs={{0,2},{2,0},{4,6},{6,4},{8,10},{10,8},{12,14},{14,12},{16,18},{18,... | collective-permute-start | bytes 3686408 | tf_op jit(solution)/shard_map/ppermute | solution.py:136
  260.2 32.4 %collective-permute-start.27 = (bf16[256,1600]{0,1:T(8,128)(2,1)}, bf16[256,1600]{0,1:T(8,128)(2,1)}, u32[]{:S(2)}, u32[]{:S(2)}) collective-permute-start(bf16[256,1600]{0,1:T(8,128)(2,1)} %pad_maximum_fusion.5), channel_id=1, source_target_pairs={{0,1},{1,0},{2,3},{3,2},{4,5},{5,4},{6,7},{7,6},{8,9},{9,8},{10,11... | collective-permute-start | bytes 2457608 | tf_op jit(solution)/shard_map/ppermute | solution.py:132
  274.4 50.8 %collective-permute-start.43 = (bf16[4800,128]{1,0:T(8,128)(2,1)}, bf16[4800,128]{1,0:T(8,128)(2,1)}, u32[]{:S(2)}, u32[]{:S(2)}) collective-permute-start(bf16[4800,128]{1,0:T(8,128)(2,1)} %dynamic-slice_bitcast_fusion.2), channel_id=1, source_target_pairs={{0,2},{2,0},{4,6},{6,4},{8,10},{10,8},{12,14},{14,12},{16,18},{18,... | collective-permute-start | bytes 3686408 | tf_op jit(solution)/shard_map/ppermute | solution.py:136
  289.1 39.5 %collective-permute-start.53 = (bf16[4800,128]{1,0:T(8,128)(2,1)}, bf16[4800,128]{1,0:T(8,128)(2,1)}, u32[]{:S(2)}, u32[]{:S(2)}) collective-permute-start(bf16[4800,128]{1,0:T(8,128)(2,1)} %dynamic-slice_bitcast_fusion.1), channel_id=1, source_target_pairs={{0,2},{2,0},{4,6},{6,4},{8,10},{10,8},{12,14},{14,12},{16,18},{18,... | collective-permute-start | bytes 3686408 | tf_op jit(solution)/shard_map/ppermute | solution.py:136
  315.6 43.4 %collective-permute-start.30 = (bf16[4864,128]{1,0:T(8,128)(2,1)S(1)}, bf16[4864,128]{1,0:T(8,128)(2,1)S(1)}, u32[]{:S(2)}, u32[]{:S(2)}) collective-permute-start(bf16[4864,128]{1,0:T(8,128)(2,1)S(1)} %dynamic-slice_bitcast_fusion), channel_id=1, source_target_pairs={{0,2},{2,0},{4,6},{6,4},{8,10},{10,8},{12,14},{14,12},{16,18},{18,... | collective-permute-start | bytes 3735560 | tf_op jit(solution)/shard_map/ppermute | solution.py:136
  334.5 35.8 %collective-permute-start.39 = (bf16[2400,128]{1,0:T(8,128)(2,1)S(1)}, bf16[2400,128]{1,0:T(8,128)(2,1)S(1)}, u32[]{:S(2)}, u32[]{:S(2)}) collective-permute-start(bf16[2400,128]{1,0:T(8,128)(2,1)S(1)} %maximum_select_fusion.5), channel_id=1, source_target_pairs={{0,4},{2,6},{4,0},{6,2},{8,12},{10,14},{12,8},{14,10},{16,20},{18,... | collective-permute-start | bytes 1843208 | tf_op jit(solution)/shard_map/ppermute | solution.py:136
  370.6 30.0 %collective-permute-start.40 = (bf16[4800,128]{1,0:T(8,128)(2,1)S(1)}, bf16[4800,128]{1,0:T(8,128)(2,1)S(1)}, u32[]{:S(2)}, u32[]{:S(2)}) collective-permute-start(bf16[4800,128]{1,0:T(8,128)(2,1)S(1)} %maximum_select_fusion.1.refs_4_), channel_id=1, source_target_pairs={{0,2},{2,0},{4,6},{6,4},{8,10},{10,8},{12,14},{14,12},{16,18},{18,... | collective-permute-start | bytes 3686408 | tf_op jit(solution)/shard_map/ppermute | solution.py:136
  386.2 30.3 %collective-permute-start.56 = (bf16[600,128]{1,0:T(8,128)(2,1)S(1)}, bf16[600,128]{1,0:T(8,128)(2,1)S(1)}, u32[]{:S(2)}, u32[]{:S(2)}) collective-permute-start(bf16[600,128]{1,0:T(8,128)(2,1)S(1)} %dynamic-slice_bitcast_fusion.13), channel_id=1, source_target_pairs={{0,16},{2,18},{4,20},{6,22},{8,24},{10,26},{12,28},{14,30},{16,0},... | collective-permute-start | bytes 460808 | tf_op jit(solution)/shard_map/ppermute | solution.py:136
  399.2 32.7 %collective-permute-start.50 = (bf16[4800,128]{1,0:T(8,128)(2,1)S(1)}, bf16[4800,128]{1,0:T(8,128)(2,1)S(1)}, u32[]{:S(2)}, u32[]{:S(2)}) collective-permute-start(bf16[4800,128]{1,0:T(8,128)(2,1)S(1)} %maximum_select_fusion.2.refs_4_), channel_id=1, source_target_pairs={{0,2},{2,0},{4,6},{6,4},{8,10},{10,8},{12,14},{14,12},{16,18},{18,... | collective-permute-start | bytes 3686408 | tf_op jit(solution)/shard_map/ppermute | solution.py:136
  463.7 35.5 %collective-permute-start.52 = (bf16[4864,128]{1,0:T(8,128)(2,1)S(1)}, bf16[4864,128]{1,0:T(8,128)(2,1)}, u32[]{:S(2)}, u32[]{:S(2)}) collective-permute-start(bf16[4864,128]{1,0:T(8,128)(2,1)S(1)} %maximum_select_fusion.refs_4_), channel_id=1, source_target_pairs={{0,2},{2,0},{4,6},{6,4},{8,10},{10,8},{12,14},{14,12},{16,18},{18,... | collective-permute-start | bytes 3735560 | tf_op jit(solution)/shard_map/ppermute | solution.py:136
  (86 other events, 879.8 us)
